TPU v7x, 32 devices: a whole 2x2x4 slice. The times are simulated.
32 devices in a mesh: region: 8 (over z, x), eig: 4 (over y, core).
Axes of the slice: x: 2, y: 2, z: 4, core: 2. Of those that a mesh axis runs over, the one named last changes fastest.
Arguments:
- residual: float32 [2, 192, 32, 3072], P(None, 'region', None, 'eig'), may hold values from -6 to 6
- basis: float32 [2, 192, 64, 3072], P(None, 'region', None, 'eig'), may hold values from -0.078125 to 0.078125
- eigvecs: bfloat16 [2, 192, 64, 1024], P(None, 'region', None, 'eig'), may hold values from -0.0390625 to 0.0390625
- weights: float32 [1024], P('eig'), may hold values from 6 to 24
Outputs:
- correction: float32 [2, 192, 32, 3072], P(None, 'region', None, 'eig')
All inputs are finite; a program needn't handle non-finite values.
Results may differ from a plain program's by a relative error of at most 0.013.
Values may be sent and summed in bfloat16 or wider, within the bound.
No kernel may reach another device: no remote copies, remote signals or barrier semaphores. Data moves between devices by JAX's collectives and lax.ppermute only.
A program may use at most 64 MiB of HBM per device.

v0:
```python
import jax
import jax.numpy as jnp
from jax import lax
from jax.sharding import PartitionSpec as P


def mix(form, left, right):
    return jnp.einsum(form, left, right, precision=lax.Precision.HIGHEST)


def mix_low(form, left, right):
    return jnp.einsum(form, left, right, preferred_element_type=jnp.float32)


def project(basis, residual):
    coarse_re = mix("bkc,bnc->bnk", basis[0], residual[0]) + mix(
        "bkc,bnc->bnk", basis[1], residual[1]
    )
    coarse_im = mix("bkc,bnc->bnk", basis[0], residual[1]) - mix(
        "bkc,bnc->bnk", basis[1], residual[0]
    )
    return jnp.stack([coarse_re, coarse_im], axis=1)


def contract(coarse, eig_re, eig_im):
    spec_re = mix_low("bnk,bkj->nj", coarse[:, 0], eig_re) + mix_low(
        "bnk,bkj->nj", coarse[:, 1], eig_im
    )
    spec_im = mix_low("bnk,bkj->nj", coarse[:, 1], eig_re) - mix_low(
        "bnk,bkj->nj", coarse[:, 0], eig_im
    )
    return jnp.stack([spec_re, spec_im])


def expand(weighted, eig_re, eig_im):
    lift_re = mix_low("nj,bkj->bnk", weighted[0], eig_re) - mix_low(
        "nj,bkj->bnk", weighted[1], eig_im
    )
    lift_im = mix_low("nj,bkj->bnk", weighted[0], eig_im) + mix_low(
        "nj,bkj->bnk", weighted[1], eig_re
    )
    return jnp.stack([lift_re, lift_im], axis=1)


def prolong(bas_part, lifted):
    out_re = mix("bkc,bnk->bnc", bas_part[0], lifted[:, 0]) - mix(
        "bkc,bnk->bnc", bas_part[1], lifted[:, 1]
    )
    out_im = mix("bkc,bnk->bnc", bas_part[0], lifted[:, 1]) + mix(
        "bkc,bnk->bnc", bas_part[1], lifted[:, 0]
    )
    return jnp.stack([out_re, out_im])


def shards(residual, basis, eigvecs, weights):
    partial_coarse = project(basis, residual)
    eig_re, eig_im = (eigvecs[0], eigvecs[1])
    coarse = lax.psum(partial_coarse, "eig").astype(jnp.bfloat16)
    spectral = contract(coarse, eig_re, eig_im)
    summed = lax.psum(spectral, "region")
    weighted = (summed * weights[None, None, :]).astype(jnp.bfloat16)
    lifted = lax.psum(expand(weighted, eig_re, eig_im).astype(jnp.bfloat16), "eig").astype(
        jnp.float32
    )
    return prolong(basis, lifted)


def solution(mesh):
    in_specs = (
        P(None, "region", None, "eig"),
        P(None, "region", None, "eig"),
        P(None, "region", None, "eig"),
        P("eig"),
    )
    out_specs = P(None, "region", None, "eig")
    return jax.shard_map(shards, mesh=mesh, in_specs=in_specs, out_specs=out_specs, check_vma=False)
```

profile of v0, /device:TPU:0, one launch (start us, length us, event | category | flops | bytes accessed | tf_op | source)
XLA Modules:
  0.0 182.6 jit_solution(13521938585177216193)
XLA Ops:
  6.5 0.0 all-reduce.4.cloned.1.call-start
  6.5 0.0 copy-start
  6.5 7.2 %fusion.4 = f32[24,32,64]{2,1,0:T(8,128)S(1)} fusion(f32[2,24,64,768]{3,2,1,0:T(8,128)} %param.5, f32[2,24,32,768]{3,2,1,0:T(8,128)} %param.4), kind=kOutput, calls=%fused_computation.5 | convolution fusion | flops 452984832 | bytes 7274496 | tf_op jit(solution)/shard_map/bkc,bnc->bnk/dot_general | solution.py:8
  13.7 0.0 copy-start.1
  13.7 7.2 %fusion.6 = f32[24,32,64]{2,1,0:T(8,128)S(1)} fusion(f32[2,24,64,768]{3,2,1,0:T(8,128)} %param.5, f32[2,24,32,768]{3,2,1,0:T(8,128)} %param.4), kind=kOutput, calls=%fused_computation.7 | convolution fusion | flops 452984832 | bytes 7274496 | tf_op jit(solution)/shard_map/bkc,bnc->bnk/dot_general | solution.py:8
  20.9 0.0 copy-done
  20.9 0.0 copy-done.1
  20.9 4.0 %fusion.51 = f32[24,1,32,64]{3,2,0,1:T(8,128)S(1)} fusion(f32[24,32,64]{2,1,0:T(8,128)S(1)} %fusion.4, f32[2,24,64,768]{3,2,1,0:T(8,128)S(1)} %copy-done, f32[2,24,32,768]{3,2,1,0:T(8,128)S(1)} %copy-done.1), kind=kOutput, calls=%fused_computation.38 | convolution fusion | flops 453033984 | bytes 7667712 | tf_op jit(solution)/shard_map/bkc,bnc->bnk/dot_general | solution.py:8
  24.9 0.0 copy-start.2
  24.9 4.2 %fusion.41 = f32[24,1,32,64]{3,2,0,1:T(8,128)S(1)} fusion(f32[24,32,64]{2,1,0:T(8,128)S(1)} %fusion.6, f32[2,24,64,768]{3,2,1,0:T(8,128)S(1)} %copy-done, f32[2,24,32,768]{3,2,1,0:T(8,128)S(1)} %copy-done.1), kind=kOutput, calls=%fused_computation.36 | convolution fusion | flops 453033984 | bytes 7667712 | tf_op jit(solution)/shard_map/bkc,bnc->bnk/dot_general | solution.py:8
  29.1 0.0 copy-start.4
  29.1 0.1 pad_maximum_fusion.1
  29.2 21.3 %all-reduce.7 = bf16[24,2,32,64]{3,2,0,1:T(8,128)(2,1)S(1)} all-reduce(f32[24,2,32,64]{3,2,0,1:T(8,128)S(1)} %pad_maximum_fusion.1), channel_id=1, replica_groups=mesh['region'=8,'eig'=4] {'eig'}, use_global_device_ids=true, to_apply=%region_0.0 | all-reduce | flops 98304 | bytes 589824 | tf_op jit(solution)/shard_map/psum | solution.py:58
  50.5 0.0 copy-done.2
  50.5 0.3 convolution_bitcast_fusion.3
  50.7 0.3 convolution_bitcast_fusion.1
  51.0 0.3 fusion.63
  51.3 0.3 fusion.61
  51.6 0.6 pad_maximum_fusion.3
  52.2 0.0 all-reduce.4.cloned.1.call-update
  52.3 0.0 all-reduce.6.cloned.1.call-start
  52.3 69.3 %all-reduce.4.cloned.1.call-done = f32[2,32,256]{2,1,0:T(8,128)} async-done(((f32[2,32,256]{2,1,0:T(8,128)}), f32[2,32,256]{2,1,0:T(8,128)}) %all-reduce.4.cloned.1.call-update) | async-done | bytes 65552 | tf_op jit(solution)/shard_map/psum | solution.py:60
  121.6 0.0 copy-done.4
  121.6 0.8 multiply_convert_fusion
  122.4 0.5 fusion.64
  122.9 0.5 fusion.70
  123.4 0.5 fusion.58
  123.8 0.5 fusion.59
  124.3 0.8 pad_maximum_fusion.2
  125.2 0.0 all-reduce.6.cloned.1.call-update
  125.2 32.7 %all-reduce.6.cloned.1.call-done = bf16[24,2,32,64]{3,2,0,1:T(8,128)(2,1)} async-done(((bf16[24,2,32,64]{3,2,0,1:T(8,128)(2,1)}), bf16[24,2,32,64]{3,2,0,1:T(8,128)(2,1)}) %all-reduce.6.cloned.1.call-update) | async-done | bytes 196624 | tf_op jit(solution)/shard_map/psum | solution.py:62
  157.9 0.0 copy-start.3
  157.9 0.0 slice-start
  157.9 4.4 %fusion = f32[24,32,768]{2,1,0:T(8,128)S(1)} fusion(f32[2,24,64,768]{3,2,1,0:T(8,128)} %param.5, bf16[24,2,32,64]{3,2,0,1:T(8,128)(2,1)} %all-reduce.6.cloned.1.call-done), kind=kOutput, calls=%fused_computation.1 | convolution fusion | flops 452984832 | bytes 7274496 | tf_op jit(solution)/shard_map/bkc,bnk->bnc/dot_general | solution.py:8
  162.3 0.0 copy-done.3
  162.3 0.0 slice-start.1
  162.4 4.3 %fusion.2 = f32[24,32,768]{2,1,0:T(8,128)S(1)} fusion(f32[2,24,64,768]{3,2,1,0:T(8,128)} %param.5, bf16[24,2,32,64]{3,2,0,1:T(8,128)(2,1)S(1)} %copy-done.3), kind=kOutput, calls=%fused_computation.3 | convolution fusion | flops 452984832 | bytes 7274496 | tf_op jit(solution)/shard_map/bkc,bnk->bnc/dot_general | solution.py:8
  166.7 0.0 slice-start.2
  166.7 4.5 %add_bitcast_fusion = f32[1,24,32,768]{3,2,1,0:T(8,128)S(1)} fusion(f32[24,32,768]{2,1,0:T(8,128)S(1)} %fusion, f32[2,24,64,768]{3,2,1,0:T(8,128)} %param.5, bf16[24,2,32,64]{3,2,0,1:T(8,128)(2,1)S(1)} %copy-done.3), kind=kOutput, calls=%fused_computation.29 | convolution fusion | flops 453574656 | bytes 9633792 | tf_op jit(solution)/shard_map/bkc,bnk->bnc/dot_general | solution.py:8
  171.2 0.0 slice-done
  171.2 0.0 slice-done.1
  171.2 0.0 slice-done.2
  171.2 2.1 %subtract_bitcast_fusion = f32[1,24,32,768]{3,2,1,0:T(8,128)S(1)} fusion(f32[24,32,768]{2,1,0:T(8,128)S(1)} %fusion.2, f32[2,24,64,768]{3,2,1,0:T(8,128)S(1)} %bitcast.129, bf16[24,2,32,64]{3,2,0,1:T(8,128)(2,1)S(1)} %copy-done.3), kind=kOutput, calls=%fused_computation.30 | convolution fusion | flops 453574656 | bytes 9633792 | tf_op jit(solution)/shard_map/bkc,bnk->bnc/dot_general | solution.py:8
  173.3 2.5 %pad_maximum_fusion = f32[2,24,32,768]{3,2,1,0:T(8,128)} fusion(f32[1,24,32,768]{3,2,1,0:T(8,128)S(1)} %add_bitcast_fusion, f32[1,24,32,768]{3,2,1,0:T(8,128)S(1)} %subtract_bitcast_fusion), kind=kLoop, calls=%fused_computation | loop fusion | flops 1179648 | bytes 9437184 | tf_op jit(solution)/shard_map/stack | solution.py:52
  (1 shorter events, 0.0 us)
Async XLA Ops:
  6.5 115.0 %all-reduce.4.cloned.1.call-start = ((), (), s32[]{:S(2)}) async-start(), calls=%async_computation | async-start | bytes 131072 | tf_op jit(solution)/shard_map/psum | solution.py:60
  6.5 14.4 %copy-start = (f32[2,24,64,768]{3,2,1,0:T(8,128)S(1)}, f32[2,24,64,768]{3,2,1,0:T(8,128)}, u32[]{:S(2)}) copy-start(f32[2,24,64,768]{3,2,1,0:T(8,128)} %param.5) | copy-start | bytes 28311556
  13.7 7.2 %copy-start.1 = (f32[2,24,32,768]{3,2,1,0:T(8,128)S(1)}, f32[2,24,32,768]{3,2,1,0:T(8,128)}, u32[]{:S(2)}) copy-start(f32[2,24,32,768]{3,2,1,0:T(8,128)} %param.4) | copy-start | bytes 14155780
  24.9 25.5 %copy-start.2 = (bf16[2,24,64,256]{3,2,1,0:T(8,128)(2,1)S(1)}, bf16[2,24,64,256]{3,2,1,0:T(8,128)(2,1)}, u32[]{:S(2)}) copy-start(bf16[2,24,64,256]{3,2,1,0:T(8,128)(2,1)} %param.6) | copy-start | bytes 4718596
  29.1 92.5 %copy-start.4 = (f32[256]{0:T(256)S(1)}, f32[256]{0:T(256)}, u32[]{:S(2)}) copy-start(f32[256]{0:T(256)} %param.7) | copy-start | bytes 3076
  52.3 105.6 %all-reduce.6.cloned.1.call-start = ((), (), s32[]{:S(2)}) async-start(), calls=%async_computation.1 | async-start | bytes 786432 | tf_op jit(solution)/shard_map/psum | solution.py:62
  157.9 4.4 %copy-start.3 = (bf16[24,2,32,64]{3,2,0,1:T(8,128)(2,1)S(1)}, bf16[24,2,32,64]{3,2,0,1:T(8,128)(2,1)}, u32[]{:S(2)}) copy-start(bf16[24,2,32,64]{3,2,0,1:T(8,128)(2,1)} %all-reduce.6.cloned.1.call-done) | copy-start | bytes 589828
  157.9 13.3 %slice-start = ((s8[9437184]{0:T(1024)(128)(4,1)}), s8[4194304]{0:T(1024)(128)(4,1)S(1)}, s32[]{:S(2)}) async-start(s8[9437184]{0:T(1024)(128)(4,1)} %bitcast.128), calls=%async_computation.2 | async-start | bytes 8388608
  162.3 8.8 %slice-start.1 = ((s8[9437184]{0:T(1024)(128)(4,1)}), s8[4194304]{0:T(1024)(128)(4,1)S(1)}, s32[]{:S(2)}) async-start(s8[9437184]{0:T(1024)(128)(4,1)} %bitcast.128), calls=%async_computation.3 | async-start | bytes 8388608
  166.7 4.5 %slice-start.2 = ((s8[9437184]{0:T(1024)(128)(4,1)}), s8[1048576]{0:T(1024)(128)(4,1)S(1)}, s32[]{:S(2)}) async-start(s8[9437184]{0:T(1024)(128)(4,1)} %bitcast.128), calls=%async_computation.4 | async-start | bytes 2097152
Sparse Core Ops, SparseCore 0:
  52.4 69.1 all-reduce.3
  125.3 32.5 all-reduce.5
where the time goes:
time: 183 us
  waiting for transfers between devices  102 us (56%)
  matrix products  40.8 us (22%)
  blocking collectives  21.3 us (12%)
  between operations  13.6 us (7%)
  other arithmetic  4.88 us (3%)
    psum x1, waiting for transfers between devices, shards(): summed = lax.psum(spectral, 'region')  69.3 us
    dot_general x8, matrix products, mix(): return jnp.einsum(form, left, right, precision=lax.Precision.HIGHEST)  37.8 us
    psum x1, waiting for transfers between devices, shards(): lax.psum(expand(weighted, eig_re, eig_im).astype(jnp.bfloat16), 'eig')  32.7 us
    psum x1, blocking collectives, shards(): coarse = lax.psum(partial_coarse, 'eig').astype(jnp.bfloat16)  21.3 us
  transfers between devices with their start and end apart: 2, of which 2 were waited for; matrix products, arithmetic and copies ran while one was open for 0% of the time, Pallas kernels for 0%

commit v1 on v0

v1 whole, which is shorter than its diff:
```python
import functools

import jax
import jax.numpy as jnp
from jax import lax
from jax.experimental import pallas as pl
from jax.experimental.pallas import tpu as pltpu
from jax.sharding import PartitionSpec as P

BF = jnp.bfloat16
F32 = jnp.float32
NT = (((1,), (1,)), ((), ()))
NN = (((1,), (0,)), ((), ()))
MIB = 1 << 20


def dot(left, right, dims):
    return lax.dot_general(left, right, dims, preferred_element_type=F32)


def project_kernel(half, res_ref, bas_ref, out_ref, copy_ref):
    step = pl.program_id(0)
    cols, comp = res_ref.shape[2:]
    pair = 2 * bas_ref.shape[2]
    res = res_ref[...].reshape(4 * cols, comp).astype(BF)
    bas = bas_ref[...].reshape(2 * pair, comp).astype(BF)
    copy_ref[step] = bas
    prod = dot(res, bas, NT)
    first = lax.broadcasted_iota(jnp.int32, (cols, pair), 1) < pair // 2

    def part(row, lane):
        lanes = slice(lane * pair, (lane + 1) * pair)
        top = prod[(2 * row) * cols : (2 * row + 1) * cols, lanes]
        low = prod[(2 * row + 1) * cols : (2 * row + 2) * cols, lanes]
        return jnp.where(first, top, low)

    out_ref[0] = (part(0, 0) + part(1, 1)).astype(out_ref.dtype)
    out_ref[1] = (part(1, 0) - part(0, 1)).astype(out_ref.dtype)


def project(half, residual, basis, dtype):
    _, blocks, cols, comp = residual.shape
    vecs = basis.shape[2]
    pairs = blocks // 4
    where = lambda i, half: (0, half[0] * pairs + i, 0, 0)
    return pl.pallas_call(
        project_kernel,
        grid_spec=pltpu.PrefetchScalarGridSpec(
            num_scalar_prefetch=1,
            grid=(pairs,),
            in_specs=[
                pl.BlockSpec((2, 2, cols, comp), where),
                pl.BlockSpec((2, 2, vecs, comp), where),
            ],
            out_specs=[
                pl.BlockSpec((2, cols, 2 * vecs), lambda i, half: (0, 0, i)),
                pl.BlockSpec(memory_space=pltpu.VMEM),
            ],
        ),
        out_shape=[
            jax.ShapeDtypeStruct((2, cols, pairs * 2 * vecs), dtype),
            pltpu.VMEM((pairs, 4 * vecs, comp), BF),
        ],
        compiler_params=pltpu.CompilerParams(vmem_limit_bytes=16 * MIB),
        cost_estimate=pl.CostEstimate(
            flops=16 * pairs * cols * vecs * comp * 2, bytes_accessed=(residual.size + basis.size) * 2, transcendentals=0
        ),
        name="project",
    )(half, residual, basis)


def contract_kernel(own, own_ref, other_ref, eig_ref, wgt_ref, out_ref):
    cols = own_ref.shape[1]
    depth = own_ref.shape[2]
    re = im = None
    for coarse_ref, half in ((own_ref, own[0]), (other_ref, 1 - own[0])):
        rows = pl.ds(pl.multiple_of(half * depth, depth), depth)
        coarse = coarse_ref[...].reshape(2 * cols, depth)
        by_re = dot(coarse, eig_ref[0, rows, :], NN)
        by_im = dot(coarse, eig_ref[1, rows, :], NN)
        re = by_re[:cols] + by_im[cols:] + (0 if re is None else re)
        im = by_re[cols:] - by_im[:cols] + (0 if im is None else im)
    out_ref[0] = re * wgt_ref[...]
    out_ref[1] = im * wgt_ref[...]


def whole():
    return pl.BlockSpec(memory_space=pltpu.VMEM)


def contract(own, coarse_own, coarse_other, eig, weights):
    _, cols, depth = coarse_own.shape
    vectors = eig.shape[-1]
    return pl.pallas_call(
        contract_kernel,
        in_specs=[pl.BlockSpec(memory_space=pltpu.SMEM)] + [whole()] * 4,
        out_specs=whole(),
        out_shape=jax.ShapeDtypeStruct((2, cols, vectors), F32),
        compiler_params=pltpu.CompilerParams(vmem_limit_bytes=16 * MIB),
        cost_estimate=pl.CostEstimate(flops=16 * cols * depth * vectors, bytes_accessed=eig.size * 2, transcendentals=0),
        name="contract",
    )(own, coarse_own, coarse_other, eig, weights)


def expand_kernel(half, wgt_ref, eig_ref, out_ref):
    cols, depth = out_ref.shape[1:]
    rows = pl.ds(pl.multiple_of(half[0] * depth, depth), depth)
    weighted = wgt_ref[...].reshape(2 * cols, wgt_ref.shape[2])
    by_re = dot(weighted, eig_ref[0, rows, :], NT)
    by_im = dot(weighted, eig_ref[1, rows, :], NT)
    out_ref[0] = (by_re[:cols] - by_im[cols:]).astype(out_ref.dtype)
    out_ref[1] = (by_re[cols:] + by_im[:cols]).astype(out_ref.dtype)


def expand(half, weighted, eig, dtype):
    _, cols, vectors = weighted.shape
    depth = eig.shape[1] // 2
    return pl.pallas_call(
        expand_kernel,
        in_specs=[pl.BlockSpec(memory_space=pltpu.SMEM)] + [whole()] * 2,
        out_specs=whole(),
        out_shape=jax.ShapeDtypeStruct((2, cols, depth), dtype),
        compiler_params=pltpu.CompilerParams(vmem_limit_bytes=16 * MIB),
        cost_estimate=pl.CostEstimate(flops=8 * cols * depth * vectors, bytes_accessed=eig.size, transcendentals=0),
        name="expand",
    )(half, weighted, eig)


def prolong_kernel(half, lift_ref, bas_ref, *refs):
    out_ref = refs[-1]
    step = pl.program_id(0)
    cols, comp = out_ref.shape[2:]
    pair = bas_ref.shape[1] // 2
    re, im = lift_ref[0], lift_ref[1]
    first = lax.broadcasted_iota(jnp.int32, (cols, pair), 1) < pair // 2
    none = jnp.zeros_like(re)
    re0, re1 = jnp.where(first, re, none), jnp.where(first, none, re)
    im0, im1 = jnp.where(first, im, none), jnp.where(first, none, im)
    left = jnp.concatenate(
        [
            jnp.concatenate([re0, re1, im0, im1], axis=0),
            jnp.concatenate([-im0, -im1, re0, re1], axis=0),
        ],
        axis=1,
    )
    out_ref[...] = dot(left, bas_ref[step], NN).reshape(out_ref.shape)


def prolong(half, lifted, bas, shape, into=None):
    _, cols, depth = lifted.shape
    pairs, rows, comp = bas.shape
    where = lambda i, half: (0, half[0] * pairs + i, 0, 0)
    out = jax.ShapeDtypeStruct(shape, F32)
    return pl.pallas_call(
        prolong_kernel,
        grid_spec=pltpu.PrefetchScalarGridSpec(
            num_scalar_prefetch=1,
            grid=(pairs,),
            in_specs=[
                pl.BlockSpec((2, cols, rows // 2), lambda i, half: (0, 0, i)),
                pl.BlockSpec(memory_space=pltpu.VMEM),
            ]
            + ([] if into is None else [pl.BlockSpec(memory_space=pl.ANY)]),
            out_specs=pl.BlockSpec((2, 2, cols, comp), where),
        ),
        out_shape=out,
        input_output_aliases={} if into is None else {3: 0},
        compiler_params=pltpu.CompilerParams(vmem_limit_bytes=16 * MIB),
        cost_estimate=pl.CostEstimate(flops=4 * cols * 2 * depth * comp * 2, bytes_accessed=2 * cols * depth // 8 * comp, transcendentals=0),
        name="prolong",
    )(half, lifted, bas, *(() if into is None else (into,)))


def swap(value, axis, size, step):
    return lax.ppermute(value, axis, [(i, i ^ step) for i in range(size)])


def sum_chips(value, size):
    step = 2
    while step < size:
        value = (value.astype(F32) + swap(value.astype(BF), "eig", size, step).astype(F32)).astype(BF)
        step *= 2
    return value


def sum_regions(value, size):
    step = 1
    while step < size:
        steps = [step] if step == 1 or 2 * step >= size else [step, 2 * step, 3 * step]
        sent = value.astype(BF)
        for arrived in [swap(sent, "region", size, s) for s in steps]:
            value = value + arrived.astype(F32)
        step *= 2 if len(steps) == 1 else 4
    return value


def shards(regions, shares, residual, basis, eigvecs, weights):
    own = (lax.axis_index("eig") % 2).astype(jnp.int32).reshape(1)
    other = 1 - own
    blocks, vecs = basis.shape[1:3]
    eig = eigvecs.reshape(2, blocks * vecs, eigvecs.shape[3])

    part_other, bas_other = project(other, residual, basis, BF)
    got = swap(part_other, "eig", shares, 1)
    part_own, bas_own = project(own, residual, basis, F32)
    coarse_own = sum_chips((part_own + got.astype(F32)).astype(BF), shares)
    coarse_other = swap(coarse_own, "eig", shares, 1)

    spectral = contract(own, coarse_own, coarse_other, eig, weights.reshape(1, -1))
    weighted = sum_regions(spectral, regions).astype(BF)

    lift_other = expand(other, weighted, eig, BF)
    got = swap(lift_other, "eig", shares, 1)
    lift_own = expand(own, weighted, eig, F32)
    lifted_own = sum_chips((lift_own + got.astype(F32)).astype(BF), shares)
    lifted_other = swap(lifted_own, "eig", shares, 1)

    out = prolong(own, lifted_own, bas_own, residual.shape)
    return prolong(other, lifted_other, bas_other, residual.shape, out)


def solution(mesh):
    split = P(None, "region", None, "eig")
    return jax.shard_map(
        functools.partial(shards, mesh.shape["region"], mesh.shape["eig"]),
        mesh=mesh,
        in_specs=(split, split, split, P("eig")),
        out_specs=split,
        check_vma=False,
    )
```

time: 183 us -> 47.3 us (0.26)
  waiting for transfers between devices: 102 us -> 14.6 us
  matrix products: 40.8 us -> 0 us
  blocking collectives: 21.3 us -> 0 us
  between operations: 13.6 us -> 0.12 us
  Pallas kernels: 0 us -> 12.3 us
  starting transfers between devices: 0.04 us -> 11.8 us
  local copies, waits for them, and re-layouts: 0.05 us -> 8.07 us
  other arithmetic: 4.88 us -> 0.13 us
    psum x2 -> x0, waiting for transfers between devices: 102 us -> none  [the longest x1 69.3 us: shards(): summed = lax.psum(spectral, 'region')]
    dot_general x16 -> x0, matrix products: 40.8 us -> none  [the longest x8 37.8 us: mix(): return jnp.einsum(form, left, right, precision=lax.Precision.HIGHEST)]
    psum x1 -> x0, blocking collectives: 21.3 us -> none  [shards(): coarse = lax.psum(partial_coarse, 'eig').astype(jnp.bfloat16)]
    ppermute x0 -> x10, waiting for transfers between devices: none -> 14.6 us  [swap(): return lax.ppermute(value, axis, [(i, i ^ step) for i in range(size)])]
    pallas_call x0 -> x7, Pallas kernels: none -> 12.3 us  [the longest x2 6.34 us: prolong(): pl.pallas_call(prolong_kernel, grid_spec=pltpu.PrefetchScalarGridSpec(num...]
    ppermute x0 -> x10, starting transfers between devices: none -> 11.8 us  [swap(): return lax.ppermute(value, axis, [(i, i ^ step) for i in range(size)])]
    unnamed x16 -> x12, local copies, waits for them, and re-layouts: 0.05 us -> 8.07 us
    another operation x4 -> x0, other arithmetic: 4.04 us -> none  [the longest x1 2.49 us: prolong(): return jnp.stack([out_re, out_im])]
  transfers between devices with their start and end apart: 2 -> 10, of which waited for: 2 -> 7; matrix products, arithmetic and copies ran while one was open for 0% -> 0% of each run, Pallas kernels for 0% -> 13%
where the time goes in v1:
time: 47.3 us; the launch traced here: 47.1 us
  waiting for transfers between devices  14.6 us (31%)
  Pallas kernels  12.3 us (26%)
  starting transfers between devices  11.8 us (25%)
  local copies, waits for them, and re-layouts  8.07 us (17%)
    ppermute x10, waiting for transfers between devices, swap(): return lax.ppermute(value, axis, [(i, i ^ step) for i in range(size)])  14.6 us
    ppermute x10, starting transfers between devices, swap(): return lax.ppermute(value, axis, [(i, i ^ step) for i in range(size)])  11.8 us
    unnamed x12, local copies, waits for them, and re-layouts  8.07 us
    pallas_call x2, Pallas kernels, prolong(): pl.pallas_call(prolong_kernel, grid_spec=pltpu.PrefetchScalarGridSpec(num...  6.34 us
    pallas_call x2, Pallas kernels, project(): pl.pallas_call(project_kernel, grid_spec=pltpu.PrefetchScalarGridSpec(num...  4.81 us
  transfers between devices with their start and end apart: 10, of which 7 were waited for; matrix products, arithmetic and copies ran while one was open for 0% of the time, Pallas kernels for 13%

profile of v1, /device:TPU:0, one launch (start us, length us, event | category | flops | bytes accessed | tf_op | source)
XLA Modules:
  0.0 47.1 jit_solution(6925137527922350726)
XLA Ops:
  0.0 0.0 copy-start
  0.0 3.7 %copy-done = f32[2,24,64,768]{3,2,1,0:T(8,128)S(1)} copy-done((f32[2,24,64,768]{3,2,1,0:T(8,128)S(1)}, f32[2,24,64,768]{3,2,1,0:T(8,128)}, u32[]{:S(2)}) %copy-start) | copy-done | bytes 9437208
  3.7 0.0 copy-start.2
  3.7 2.3 %copy-done.2 = f32[2,24,32,768]{3,2,1,0:T(8,128)S(1)} copy-done((f32[2,24,32,768]{3,2,1,0:T(8,128)S(1)}, f32[2,24,32,768]{3,2,1,0:T(8,128)}, u32[]{:S(2)}) %copy-start.2) | copy-done | bytes 4718616
  6.0 0.0 copy-start.1
  6.0 0.0 copy-start.3
  6.0 2.4 %project.3 = (bf16[2,32,768]{2,1,0:T(8,128)(2,1)S(1)}, bf16[6,256,768]{2,1,0:T(8,128)(2,1)S(1)}) custom-call(s32[1]{0:T(128)S(6)} %sub.3.half, f32[2,24,32,768]{3,2,1,0:T(8,128)S(1)} %copy-done.2, f32[2,24,64,768]{3,2,1,0:T(8,128)S(1)} %copy-done), custom_call_target="tpu_custom_call" | custom-call | flops 301989888 | bytes 7077888 | tf_op jit(solution)/shard_map/project/pallas_call | solution.py:46
  8.4 0.0 copy-start.4
  8.5 0.0 copy-start.5
  8.5 0.5 %collective-permute-start = (bf16[2,32,768]{2,1,0:T(8,128)(2,1)S(1)}, bf16[2,32,768]{2,1,0:T(8,128)(2,1)S(1)}, u32[]{:S(2)}, u32[]{:S(2)}) collective-permute-start(bf16[2,32,768]{2,1,0:T(8,128)(2,1)S(1)} %get-tuple-element.10), channel_id=1, source_target_pairs={{0,1},{1,0},{2,3},{3,2},{4,5},{5,4},{6,7},{7,6},{8,9},{9,8},{10,11... | collective-permute-start | bytes 294920 | tf_op jit(solution)/shard_map/ppermute | solution.py:175
  9.0 0.7 %copy-done.1 = f32[2,24,64,768]{3,2,1,0:T(8,128)S(1)} copy-done((f32[2,24,64,768]{3,2,1,0:T(8,128)S(1)}, f32[2,24,64,768]{3,2,1,0:T(8,128)}, u32[]{:S(2)}) %copy-start.1) | copy-done | bytes 9437208
  9.7 1.3 %copy-done.3 = f32[2,24,32,768]{3,2,1,0:T(8,128)S(1)} copy-done((f32[2,24,32,768]{3,2,1,0:T(8,128)S(1)}, f32[2,24,32,768]{3,2,1,0:T(8,128)}, u32[]{:S(2)}) %copy-start.3) | copy-done | bytes 4718616
  11.0 2.4 %project.2 = (f32[2,32,768]{2,1,0:T(8,128)S(1)}, bf16[6,256,768]{2,1,0:T(8,128)(2,1)S(1)}) custom-call(s32[1]{0:T(128)} %bitcast.half.own, f32[2,24,32,768]{3,2,1,0:T(8,128)S(1)} %copy-done.3, f32[2,24,64,768]{3,2,1,0:T(8,128)S(1)} %copy-done.1), custom_call_target="tpu_custom_call" | custom-call | flops 301989888 | bytes 7077888 | tf_op jit(solution)/shard_map/project/pallas_call | solution.py:46
  13.4 0.0 collective-permute-done
  13.5 3.0 %collective-permute-start.1 = (bf16[2,32,768]{2,1,0:T(8,128)(2,1)S(1)}, bf16[2,32,768]{2,1,0:T(8,128)(2,1)S(1)}, u32[]{:S(2)}, u32[]{:S(2)}) collective-permute-start(bf16[2,32,768]{2,1,0:T(8,128)(2,1)S(1)} %add_convert_fusion.3), channel_id=1, source_target_pairs={{0,2},{1,3},{2,0},{3,1},{4,6},{5,7},{6,4},{7,5},{8,10},{9,11},{10,... | collective-permute-start | bytes 294920 | tf_op jit(solution)/shard_map/ppermute | solution.py:175
  16.5 2.8 %collective-permute-done.1 = bf16[2,32,768]{2,1,0:T(8,128)(2,1)S(1)} collective-permute-done((bf16[2,32,768]{2,1,0:T(8,128)(2,1)S(1)}, bf16[2,32,768]{2,1,0:T(8,128)(2,1)S(1)}, u32[]{:S(2)}, u32[]{:S(2)}) %collective-permute-start.1) | collective-permute-done | bytes 98336 | tf_op jit(solution)/shard_map/ppermute | solution.py:175
  19.3 0.1 collective-permute-start.2
  19.4 1.3 %collective-permute-done.2.other_ref = bf16[2,32,768]{2,1,0:T(8,128)(2,1)S(1)} collective-permute-done((bf16[2,32,768]{2,1,0:T(8,128)(2,1)S(1)}, bf16[2,32,768]{2,1,0:T(8,128)(2,1)S(1)}, u32[]{:S(2)}, u32[]{:S(2)}) %collective-permute-start.2) | collective-permute-done | bytes 98336 | tf_op jit(solution)/shard_map/ppermute | solution.py:175
  20.7 0.0 copy-done.4
  20.7 0.0 copy-done.5
  20.7 0.4 contract.1
  21.1 1.9 %collective-permute-start.3 = (bf16[2,32,256]{2,1,0:T(8,128)(2,1)S(1)}, bf16[2,32,256]{2,1,0:T(8,128)(2,1)S(1)}, u32[]{:S(2)}, u32[]{:S(2)}) collective-permute-start(bf16[2,32,256]{2,1,0:T(8,128)(2,1)S(1)} %convert_element_type.56), channel_id=1, source_target_pairs={{0,4},{4,0},{8,12},{12,8},{16,20},{20,16},{24,28},{28,24},{1,5},{5... | collective-permute-start | bytes 98312 | tf_op jit(solution)/shard_map/ppermute | solution.py:175
  23.0 2.1 %collective-permute-done.3 = bf16[2,32,256]{2,1,0:T(8,128)(2,1)S(1)} collective-permute-done((bf16[2,32,256]{2,1,0:T(8,128)(2,1)S(1)}, bf16[2,32,256]{2,1,0:T(8,128)(2,1)S(1)}, u32[]{:S(2)}, u32[]{:S(2)}) %collective-permute-start.3) | collective-permute-done | bytes 32800 | tf_op jit(solution)/shard_map/ppermute | solution.py:175
  25.1 4.0 %collective-permute-start.6 = (bf16[2,32,256]{2,1,0:T(8,128)(2,1)S(1)}, bf16[2,32,256]{2,1,0:T(8,128)(2,1)S(1)}, u32[]{:S(2)}, u32[]{:S(2)}) collective-permute-start(bf16[2,32,256]{2,1,0:T(8,128)(2,1)S(1)} %fusion), channel_id=1, source_target_pairs={{0,24},{4,28},{8,16},{12,20},{16,8},{20,12},{24,0},{28,4},{1,25},{... | collective-permute-start | bytes 98312 | tf_op jit(solution)/shard_map/ppermute | solution.py:175
  29.1 0.0 collective-permute-start.5
  29.1 0.6 %collective-permute-start.4 = (bf16[2,32,256]{2,1,0:T(8,128)(2,1)S(1)}, bf16[2,32,256]{2,1,0:T(8,128)(2,1)S(1)}, u32[]{:S(2)}, u32[]{:S(2)}) collective-permute-start(bf16[2,32,256]{2,1,0:T(8,128)(2,1)S(1)} %fusion), channel_id=1, source_target_pairs={{0,8},{4,12},{8,0},{12,4},{16,24},{20,28},{24,16},{28,20},{1,9},{5... | collective-permute-start | bytes 98312 | tf_op jit(solution)/shard_map/ppermute | solution.py:175
  29.7 1.4 %collective-permute-done.6 = bf16[2,32,256]{2,1,0:T(8,128)(2,1)S(1)} collective-permute-done((bf16[2,32,256]{2,1,0:T(8,128)(2,1)S(1)}, bf16[2,32,256]{2,1,0:T(8,128)(2,1)S(1)}, u32[]{:S(2)}, u32[]{:S(2)}) %collective-permute-start.6) | collective-permute-done | bytes 32800 | tf_op jit(solution)/shard_map/ppermute | solution.py:175
  31.1 2.8 %collective-permute-done.5 = bf16[2,32,256]{2,1,0:T(8,128)(2,1)S(1)} collective-permute-done((bf16[2,32,256]{2,1,0:T(8,128)(2,1)S(1)}, bf16[2,32,256]{2,1,0:T(8,128)(2,1)S(1)}, u32[]{:S(2)}, u32[]{:S(2)}) %collective-permute-start.5) | collective-permute-done | bytes 32800 | tf_op jit(solution)/shard_map/ppermute | solution.py:175
  33.9 0.0 collective-permute-done.4
  33.9 0.4 expand.3
  34.3 0.1 collective-permute-start.7
  34.4 0.4 expand.2
  34.8 0.9 %collective-permute-done.7 = bf16[2,32,768]{2,1,0:T(8,128)(2,1)S(1)} collective-permute-done((bf16[2,32,768]{2,1,0:T(8,128)(2,1)S(1)}, bf16[2,32,768]{2,1,0:T(8,128)(2,1)S(1)}, u32[]{:S(2)}, u32[]{:S(2)}) %collective-permute-start.7) | collective-permute-done | bytes 98336 | tf_op jit(solution)/shard_map/ppermute | solution.py:175
  35.7 1.6 %collective-permute-start.8 = (bf16[2,32,768]{2,1,0:T(8,128)(2,1)S(1)}, bf16[2,32,768]{2,1,0:T(8,128)(2,1)S(1)}, u32[]{:S(2)}, u32[]{:S(2)}) collective-permute-start(bf16[2,32,768]{2,1,0:T(8,128)(2,1)S(1)} %add_convert_fusion.1), channel_id=1, source_target_pairs={{0,2},{1,3},{2,0},{3,1},{4,6},{5,7},{6,4},{7,5},{8,10},{9,11},{10,... | collective-permute-start | bytes 294920 | tf_op jit(solution)/shard_map/ppermute | solution.py:175
  37.3 3.3 %collective-permute-done.8 = bf16[2,32,768]{2,1,0:T(8,128)(2,1)S(1)} collective-permute-done((bf16[2,32,768]{2,1,0:T(8,128)(2,1)S(1)}, bf16[2,32,768]{2,1,0:T(8,128)(2,1)S(1)}, u32[]{:S(2)}, u32[]{:S(2)}) %collective-permute-start.8) | collective-permute-done | bytes 98336 | tf_op jit(solution)/shard_map/ppermute | solution.py:175
  40.6 0.1 collective-permute-start.9
  40.7 3.2 %prolong.2.refs_0_ = f32[2,24,32,768]{3,2,1,0:T(8,128)} custom-call(s32[1]{0:T(128)} %bitcast.half.own, bf16[2,32,768]{2,1,0:T(8,128)(2,1)S(1)} %add_convert_fusion.lift_ref, bf16[6,256,768]{2,1,0:T(8,128)(2,1)S(1)} %get-tuple-element.12.bas_ref), custom_call_target="tpu_custom_call" | custom-call | flops 301989888 | bytes 4718592 | tf_op jit(solution)/shard_map/prolong/pallas_call | solution.py:154
  43.9 0.0 collective-permute-done.9.lift_ref
  43.9 3.2 %prolong.3 = f32[2,24,32,768]{3,2,1,0:T(8,128)} custom-call(s32[1]{0:T(128)S(6)} %sub.3.half, bf16[2,32,768]{2,1,0:T(8,128)(2,1)S(1)} %collective-permute-done.9.lift_ref, bf16[6,256,768]{2,1,0:T(8,128)(2,1)S(1)} %get-tuple-element.11.bas_ref, f32[2,24,32,768]{3,2,1,0:T(8,128)} %prolong.2.refs_0_), custom_call_target="tpu_custom_call", output_to_operand_aliasing={{}: (3, {})} | custom-call | flops 301989888 | bytes 4718592 | tf_op jit(solution)/shard_map/prolong/pallas_call | solution.py:154
  (7 shorter events, 0.1 us)
Async XLA Ops:
  0.0 3.7 %copy-start = (f32[2,24,64,768]{3,2,1,0:T(8,128)S(1)}, f32[2,24,64,768]{3,2,1,0:T(8,128)}, u32[]{:S(2)}) copy-start(f32[2,24,64,768]{3,2,1,0:T(8,128)} %bas_ref.3) | copy-start | bytes 28311556
  3.7 2.3 %copy-start.2 = (f32[2,24,32,768]{3,2,1,0:T(8,128)S(1)}, f32[2,24,32,768]{3,2,1,0:T(8,128)}, u32[]{:S(2)}) copy-start(f32[2,24,32,768]{3,2,1,0:T(8,128)} %res_ref.3) | copy-start | bytes 14155780
  6.0 3.7 %copy-start.1 = (f32[2,24,64,768]{3,2,1,0:T(8,128)S(1)}, f32[2,24,64,768]{3,2,1,0:T(8,128)}, u32[]{:S(2)}) copy-start(f32[2,24,64,768]{3,2,1,0:T(8,128)} %bas_ref.3) | copy-start | bytes 28311556
  6.0 5.0 %copy-start.3 = (f32[2,24,32,768]{3,2,1,0:T(8,128)S(1)}, f32[2,24,32,768]{3,2,1,0:T(8,128)}, u32[]{:S(2)}) copy-start(f32[2,24,32,768]{3,2,1,0:T(8,128)} %res_ref.3) | copy-start | bytes 14155780
  8.4 12.3 %copy-start.4 = (bf16[2,24,64,256]{3,2,1,0:T(8,128)(2,1)S(1)}, bf16[2,24,64,256]{3,2,1,0:T(8,128)(2,1)}, u32[]{:S(2)}) copy-start(bf16[2,24,64,256]{3,2,1,0:T(8,128)(2,1)} %param.6) | copy-start | bytes 4718596
  8.5 12.3 %copy-start.5 = (f32[256]{0:T(256)S(1)}, f32[256]{0:T(256)}, u32[]{:S(2)}) copy-start(f32[256]{0:T(256)} %param.7) | copy-start | bytes 3076
  8.5 5.0 %collective-permute-start = (bf16[2,32,768]{2,1,0:T(8,128)(2,1)S(1)}, bf16[2,32,768]{2,1,0:T(8,128)(2,1)S(1)}, u32[]{:S(2)}, u32[]{:S(2)}) collective-permute-start(bf16[2,32,768]{2,1,0:T(8,128)(2,1)S(1)} %get-tuple-element.10), channel_id=1, source_target_pairs={{0,1},{1,0},{2,3},{3,2},{4,5},{5,4},{6,7},{7,6},{8,9},{9,8},{10,11... | collective-permute-start | bytes 294920 | tf_op jit(solution)/shard_map/ppermute | solution.py:175
  13.5 5.8 %collective-permute-start.1 = (bf16[2,32,768]{2,1,0:T(8,128)(2,1)S(1)}, bf16[2,32,768]{2,1,0:T(8,128)(2,1)S(1)}, u32[]{:S(2)}, u32[]{:S(2)}) collective-permute-start(bf16[2,32,768]{2,1,0:T(8,128)(2,1)S(1)} %add_convert_fusion.3), channel_id=1, source_target_pairs={{0,2},{1,3},{2,0},{3,1},{4,6},{5,7},{6,4},{7,5},{8,10},{9,11},{10,... | collective-permute-start | bytes 294920 | tf_op jit(solution)/shard_map/ppermute | solution.py:175
  19.3 1.4 %collective-permute-start.2 = (bf16[2,32,768]{2,1,0:T(8,128)(2,1)S(1)}, bf16[2,32,768]{2,1,0:T(8,128)(2,1)S(1)}, u32[]{:S(2)}, u32[]{:S(2)}) collective-permute-start(bf16[2,32,768]{2,1,0:T(8,128)(2,1)S(1)} %add_convert_fusion.2.own_ref), channel_id=1, source_target_pairs={{0,1},{1,0},{2,3},{3,2},{4,5},{5,4},{6,7},{7,6},{8,9},{9,8},{10,11... | collective-permute-start | bytes 294920 | tf_op jit(solution)/shard_map/ppermute | solution.py:175
  21.1 4.0 %collective-permute-start.3 = (bf16[2,32,256]{2,1,0:T(8,128)(2,1)S(1)}, bf16[2,32,256]{2,1,0:T(8,128)(2,1)S(1)}, u32[]{:S(2)}, u32[]{:S(2)}) collective-permute-start(bf16[2,32,256]{2,1,0:T(8,128)(2,1)S(1)} %convert_element_type.56), channel_id=1, source_target_pairs={{0,4},{4,0},{8,12},{12,8},{16,20},{20,16},{24,28},{28,24},{1,5},{5... | collective-permute-start | bytes 98312 | tf_op jit(solution)/shard_map/ppermute | solution.py:175
  25.1 6.0 %collective-permute-start.6 = (bf16[2,32,256]{2,1,0:T(8,128)(2,1)S(1)}, bf16[2,32,256]{2,1,0:T(8,128)(2,1)S(1)}, u32[]{:S(2)}, u32[]{:S(2)}) collective-permute-start(bf16[2,32,256]{2,1,0:T(8,128)(2,1)S(1)} %fusion), channel_id=1, source_target_pairs={{0,24},{4,28},{8,16},{12,20},{16,8},{20,12},{24,0},{28,4},{1,25},{... | collective-permute-start | bytes 98312 | tf_op jit(solution)/shard_map/ppermute | solution.py:175
  29.1 4.8 %collective-permute-start.5 = (bf16[2,32,256]{2,1,0:T(8,128)(2,1)S(1)}, bf16[2,32,256]{2,1,0:T(8,128)(2,1)S(1)}, u32[]{:S(2)}, u32[]{:S(2)}) collective-permute-start(bf16[2,32,256]{2,1,0:T(8,128)(2,1)S(1)} %fusion), channel_id=1, source_target_pairs={{0,16},{4,20},{8,24},{12,28},{16,0},{20,4},{24,8},{28,12},{1,17},{... | collective-permute-start | bytes 98312 | tf_op jit(solution)/shard_map/ppermute | solution.py:175
  29.1 4.8 %collective-permute-start.4 = (bf16[2,32,256]{2,1,0:T(8,128)(2,1)S(1)}, bf16[2,32,256]{2,1,0:T(8,128)(2,1)S(1)}, u32[]{:S(2)}, u32[]{:S(2)}) collective-permute-start(bf16[2,32,256]{2,1,0:T(8,128)(2,1)S(1)} %fusion), channel_id=1, source_target_pairs={{0,8},{4,12},{8,0},{12,4},{16,24},{20,28},{24,16},{28,20},{1,9},{5... | collective-permute-start | bytes 98312 | tf_op jit(solution)/shard_map/ppermute | solution.py:175
  34.3 1.4 %collective-permute-start.7 = (bf16[2,32,768]{2,1,0:T(8,128)(2,1)S(1)}, bf16[2,32,768]{2,1,0:T(8,128)(2,1)S(1)}, u32[]{:S(2)}, u32[]{:S(2)}) collective-permute-start(bf16[2,32,768]{2,1,0:T(8,128)(2,1)S(1)} %expand.3), channel_id=1, source_target_pairs={{0,1},{1,0},{2,3},{3,2},{4,5},{5,4},{6,7},{7,6},{8,9},{9,8},{10,11... | collective-permute-start | bytes 294920 | tf_op jit(solution)/shard_map/ppermute | solution.py:175
  35.7 4.9 %collective-permute-start.8 = (bf16[2,32,768]{2,1,0:T(8,128)(2,1)S(1)}, bf16[2,32,768]{2,1,0:T(8,128)(2,1)S(1)}, u32[]{:S(2)}, u32[]{:S(2)}) collective-permute-start(bf16[2,32,768]{2,1,0:T(8,128)(2,1)S(1)} %add_convert_fusion.1), channel_id=1, source_target_pairs={{0,2},{1,3},{2,0},{3,1},{4,6},{5,7},{6,4},{7,5},{8,10},{9,11},{10,... | collective-permute-start | bytes 294920 | tf_op jit(solution)/shard_map/ppermute | solution.py:175
  40.6 3.3 %collective-permute-start.9 = (bf16[2,32,768]{2,1,0:T(8,128)(2,1)S(1)}, bf16[2,32,768]{2,1,0:T(8,128)(2,1)S(1)}, u32[]{:S(2)}, u32[]{:S(2)}) collective-permute-start(bf16[2,32,768]{2,1,0:T(8,128)(2,1)S(1)} %add_convert_fusion.lift_ref), channel_id=1, source_target_pairs={{0,1},{1,0},{2,3},{3,2},{4,5},{5,4},{6,7},{7,6},{8,9},{9,8},{10,11... | collective-permute-start | bytes 294920 | tf_op jit(solution)/shard_map/ppermute | solution.py:175

commit v2 on v1

--- a/solution.py
+++ b/solution.py
@@ -18,55 +18,74 @@
     return lax.dot_general(left, right, dims, preferred_element_type=F32)
 
 
-def project_kernel(half, res_ref, bas_ref, out_ref, copy_ref):
-    step = pl.program_id(0)
+def project_kernel(own, res_hbm, bas_hbm, other_ref, own_ref, bas_other_ref, bas_own_ref, res_ref, bas_ref, sem):
     cols, comp = res_ref.shape[2:]
-    pair = 2 * bas_ref.shape[2]
-    res = res_ref[...].reshape(4 * cols, comp).astype(BF)
-    bas = bas_ref[...].reshape(2 * pair, comp).astype(BF)
-    copy_ref[step] = bas
-    prod = dot(res, bas, NT)
-    first = lax.broadcasted_iota(jnp.int32, (cols, pair), 1) < pair // 2
-
-    def part(row, lane):
-        lanes = slice(lane * pair, (lane + 1) * pair)
-        top = prod[(2 * row) * cols : (2 * row + 1) * cols, lanes]
-        low = prod[(2 * row + 1) * cols : (2 * row + 2) * cols, lanes]
-        return jnp.where(first, top, low)
-
-    out_ref[0] = (part(0, 0) + part(1, 1)).astype(out_ref.dtype)
-    out_ref[1] = (part(1, 0) - part(0, 1)).astype(out_ref.dtype)
-
-
-def project(half, residual, basis, dtype):
+    vecs = bas_ref.shape[2]
+    pair = 2 * vecs
+    pairs = bas_own_ref.shape[0]
+
+    def copies(i):
+        half = 1 - own[0] if i < pairs else own[0]
+        source = pl.ds(2 * (half * pairs + i % pairs), 2)
+        slot = pl.ds(2 * i, 2)
+        return (
+            pltpu.make_async_copy(res_hbm.at[:, source], res_ref.at[:, slot], sem.at[0, i]),
+            pltpu.make_async_copy(bas_hbm.at[:, source], bas_ref.at[:, slot], sem.at[1, i]),
+        )
+
+    for i in range(2 * pairs):
+        for copy in copies(i):
+            copy.start()
+    first = lax.broadcasted_iota(jnp.int32, (cols, pair), 1) < vecs
+    for i in range(2 * pairs):
+        out_ref, copy_ref = (other_ref, bas_other_ref) if i < pairs else (own_ref, bas_own_ref)
+        for copy in copies(i):
+            copy.wait()
+        res = res_ref[:, 2 * i : 2 * i + 2].reshape(4 * cols, comp).astype(BF)
+        bas = bas_ref[:, 2 * i : 2 * i + 2].reshape(2 * pair, comp).astype(BF)
+        copy_ref[i % pairs] = bas
+        prod = dot(res, bas, NT)
+
+        def part(row, lane):
+            lanes = slice(lane * pair, (lane + 1) * pair)
+            top = prod[2 * row * cols : (2 * row + 1) * cols, lanes]
+            low = prod[(2 * row + 1) * cols : (2 * row + 2) * cols, lanes]
+            return jnp.where(first, top, low)
+
+        lanes = slice(i % pairs * pair, (i % pairs + 1) * pair)
+        out_ref[0, :, lanes] = (part(0, 0) + part(1, 1)).astype(out_ref.dtype)
+        out_ref[1, :, lanes] = (part(1, 0) - part(0, 1)).astype(out_ref.dtype)
+
+
+def hbm(value):
+    return pltpu.with_memory_space_constraint(value, pltpu.HBM)
+
+
+def project(own, residual, basis):
     _, blocks, cols, comp = residual.shape
     vecs = basis.shape[2]
     pairs = blocks // 4
-    where = lambda i, half: (0, half[0] * pairs + i, 0, 0)
     return pl.pallas_call(
         project_kernel,
-        grid_spec=pltpu.PrefetchScalarGridSpec(
-            num_scalar_prefetch=1,
-            grid=(pairs,),
-            in_specs=[
-                pl.BlockSpec((2, 2, cols, comp), where),
-                pl.BlockSpec((2, 2, vecs, comp), where),
-            ],
-            out_specs=[
-                pl.BlockSpec((2, cols, 2 * vecs), lambda i, half: (0, 0, i)),
-                pl.BlockSpec(memory_space=pltpu.VMEM),
-            ],
-        ),
+        in_specs=[pl.BlockSpec(memory_space=pltpu.SMEM)] + [pl.BlockSpec(memory_space=pltpu.HBM)] * 2,
+        out_specs=[whole()] * 4,
         out_shape=[
-            jax.ShapeDtypeStruct((2, cols, pairs * 2 * vecs), dtype),
+            pltpu.VMEM((2, cols, pairs * 2 * vecs), BF),
+            pltpu.VMEM((2, cols, pairs * 2 * vecs), F32),
+            pltpu.VMEM((pairs, 4 * vecs, comp), BF),
             pltpu.VMEM((pairs, 4 * vecs, comp), BF),
         ],
-        compiler_params=pltpu.CompilerParams(vmem_limit_bytes=16 * MIB),
+        scratch_shapes=[
+            pltpu.VMEM(residual.shape, F32),
+            pltpu.VMEM(basis.shape, F32),
+            pltpu.SemaphoreType.DMA((2, 2 * pairs)),
+        ],
+        compiler_params=pltpu.CompilerParams(vmem_limit_bytes=28 * MIB),
         cost_estimate=pl.CostEstimate(
-            flops=16 * pairs * cols * vecs * comp * 2, bytes_accessed=(residual.size + basis.size) * 2, transcendentals=0
+            flops=16 * blocks * cols * vecs * comp, bytes_accessed=(residual.size + basis.size) * 4, transcendentals=0
         ),
         name="project",
-    )(half, residual, basis)
+    )(own, hbm(residual), hbm(basis))
 
 
 def contract_kernel(own, own_ref, other_ref, eig_ref, wgt_ref, out_ref):
@@ -127,46 +146,47 @@
 
 
 def prolong_kernel(half, lift_ref, bas_ref, *refs):
-    out_ref = refs[-1]
-    step = pl.program_id(0)
+    out_hbm, out_ref, sem = refs[-3:]
     cols, comp = out_ref.shape[2:]
-    pair = bas_ref.shape[1] // 2
-    re, im = lift_ref[0], lift_ref[1]
+    pairs, pair = bas_ref.shape[0], bas_ref.shape[1] // 2
     first = lax.broadcasted_iota(jnp.int32, (cols, pair), 1) < pair // 2
-    none = jnp.zeros_like(re)
-    re0, re1 = jnp.where(first, re, none), jnp.where(first, none, re)
-    im0, im1 = jnp.where(first, im, none), jnp.where(first, none, im)
-    left = jnp.concatenate(
-        [
-            jnp.concatenate([re0, re1, im0, im1], axis=0),
-            jnp.concatenate([-im0, -im1, re0, re1], axis=0),
-        ],
-        axis=1,
-    )
-    out_ref[...] = dot(left, bas_ref[step], NN).reshape(out_ref.shape)
+
+    def copy(i):
+        target = pl.ds(2 * (half[0] * pairs + i), 2)
+        return pltpu.make_async_copy(out_ref.at[:, pl.ds(2 * i, 2)], out_hbm.at[:, target], sem.at[i])
+
+    for i in range(pairs):
+        lanes = slice(i * pair, (i + 1) * pair)
+        re, im = lift_ref[0, :, lanes], lift_ref[1, :, lanes]
+        none = jnp.zeros_like(re)
+        re0, re1 = jnp.where(first, re, none), jnp.where(first, none, re)
+        im0, im1 = jnp.where(first, im, none), jnp.where(first, none, im)
+        left = jnp.concatenate(
+            [
+                jnp.concatenate([re0, re1, im0, im1], axis=0),
+                jnp.concatenate([-im0, -im1, re0, re1], axis=0),
+            ],
+            axis=1,
+        )
+        out_ref[:, 2 * i : 2 * i + 2] = dot(left, bas_ref[i], NN).reshape(2, 2, cols, comp)
+        copy(i).start()
+    for i in range(pairs):
+        copy(i).wait()
 
 
 def prolong(half, lifted, bas, shape, into=None):
     _, cols, depth = lifted.shape
     pairs, rows, comp = bas.shape
-    where = lambda i, half: (0, half[0] * pairs + i, 0, 0)
-    out = jax.ShapeDtypeStruct(shape, F32)
+    anywhere = pl.BlockSpec(memory_space=pltpu.HBM)
     return pl.pallas_call(
         prolong_kernel,
-        grid_spec=pltpu.PrefetchScalarGridSpec(
-            num_scalar_prefetch=1,
-            grid=(pairs,),
-            in_specs=[
-                pl.BlockSpec((2, cols, rows // 2), lambda i, half: (0, 0, i)),
-                pl.BlockSpec(memory_space=pltpu.VMEM),
-            ]
-            + ([] if into is None else [pl.BlockSpec(memory_space=pl.ANY)]),
-            out_specs=pl.BlockSpec((2, 2, cols, comp), where),
-        ),
-        out_shape=out,
+        in_specs=[pl.BlockSpec(memory_space=pltpu.SMEM)] + [whole()] * 2 + ([] if into is None else [anywhere]),
+        out_specs=anywhere,
+        out_shape=jax.ShapeDtypeStruct(shape, F32),
         input_output_aliases={} if into is None else {3: 0},
+        scratch_shapes=[pltpu.VMEM((2, 2 * pairs, cols, comp), F32), pltpu.SemaphoreType.DMA((pairs,))],
         compiler_params=pltpu.CompilerParams(vmem_limit_bytes=16 * MIB),
-        cost_estimate=pl.CostEstimate(flops=4 * cols * 2 * depth * comp * 2, bytes_accessed=2 * cols * depth // 8 * comp, transcendentals=0),
+        cost_estimate=pl.CostEstimate(flops=16 * pairs * cols * rows * comp, bytes_accessed=pairs * cols * comp * 16, transcendentals=0),
         name="prolong",
     )(half, lifted, bas, *(() if into is None else (into,)))
 
@@ -200,9 +220,8 @@
     blocks, vecs = basis.shape[1:3]
     eig = eigvecs.reshape(2, blocks * vecs, eigvecs.shape[3])
 
-    part_other, bas_other = project(other, residual, basis, BF)
+    part_other, part_own, bas_other, bas_own = project(own, residual, basis)
     got = swap(part_other, "eig", shares, 1)
-    part_own, bas_own = project(own, residual, basis, F32)
     coarse_own = sum_chips((part_own + got.astype(F32)).astype(BF), shares)
     coarse_other = swap(coarse_own, "eig", shares, 1)
 

time: 47.3 us -> 38.4 us (0.81)
  local copies, waits for them, and re-layouts: 8.07 us -> 0.01 us
  Pallas kernels: 12.3 us -> 10.4 us
  waiting for transfers between devices: 14.6 us -> 16 us
    unnamed x12 -> x4, local copies, waits for them, and re-layouts: 8.07 us -> 0.01 us
    pallas_call x4 -> x3, Pallas kernels: 11.2 us -> 9.28 us  [the longest x1 5.91 us: project(): pl.pallas_call(project_kernel, in_specs=[pl.BlockSpec(memory_space=pltpu....]
    ppermute x10, waiting for transfers between devices: 14.6 us -> 16 us  [swap(): return lax.ppermute(value, axis, [(i, i ^ step) for i in range(size)])]
  transfers between devices with their start and end apart: 10 -> 10, of which waited for: 7 -> 8; matrix products, arithmetic and copies ran while one was open for 0% -> 0% of each run, Pallas kernels for 13% -> 5%
where the time goes in v2:
time: 38.4 us; the launch traced here: 38.2 us
  waiting for transfers between devices  16 us (42%)
  starting transfers between devices  11.6 us (30%)
  Pallas kernels  10.4 us (27%)
    ppermute x10, waiting for transfers between devices, swap(): return lax.ppermute(value, axis, [(i, i ^ step) for i in range(size)])  16 us
    ppermute x10, starting transfers between devices, swap(): return lax.ppermute(value, axis, [(i, i ^ step) for i in range(size)])  11.6 us
    pallas_call x1, Pallas kernels, project(): pl.pallas_call(project_kernel, in_specs=[pl.BlockSpec(memory_space=pltpu....  5.91 us
    pallas_call x2, Pallas kernels, prolong(): pl.pallas_call(prolong_kernel, in_specs=[pl.BlockSpec(memory_space=pltpu....  3.37 us
  transfers between devices with their start and end apart: 10, of which 8 were waited for; matrix products, arithmetic and copies ran while one was open for 0% of the time, Pallas kernels for 5%

profile of v2, /device:TPU:0, one launch (start us, length us, event | category | flops | bytes accessed | tf_op | source)
XLA Modules:
  0.0 38.2 jit_solution(11797778298909206531)
XLA Ops:
  0.0 0.0 copy-start
  0.0 0.0 copy-start.1
  0.0 5.9 %project.1 = (bf16[2,32,768]{2,1,0:T(8,128)(2,1)S(1)}, f32[2,32,768]{2,1,0:T(8,128)S(1)}, bf16[6,256,768]{2,1,0:T(8,128)(2,1)S(1)}, bf16[6,256,768]{2,1,0:T(8,128)(2,1)S(1)}) custom-call(s32[1]{0:T(128)} %bitcast.own.half, f32[2,24,32,768]{3,2,1,0:T(8,128)} %res_hbm.1, f32[2,24,64,768]{3,2,1,0:T(8,128)} %bas_hbm.1), custom_call_target="tpu_custom_call" | custom-call | flops 603979776 | bytes 14155776 | tf_op jit(solution)/shard_map/project/pallas_call | solution.py:68
  5.9 0.5 %collective-permute-start = (bf16[2,32,768]{2,1,0:T(8,128)(2,1)S(1)}, bf16[2,32,768]{2,1,0:T(8,128)(2,1)S(1)}, u32[]{:S(2)}, u32[]{:S(2)}) collective-permute-start(bf16[2,32,768]{2,1,0:T(8,128)(2,1)S(1)} %get-tuple-element.10), channel_id=1, source_target_pairs={{0,1},{1,0},{2,3},{3,2},{4,5},{5,4},{6,7},{7,6},{8,9},{9,8},{10,11... | collective-permute-start | bytes 294920 | tf_op jit(solution)/shard_map/ppermute | solution.py:195
  6.4 0.9 %collective-permute-done = bf16[2,32,768]{2,1,0:T(8,128)(2,1)S(1)} collective-permute-done((bf16[2,32,768]{2,1,0:T(8,128)(2,1)S(1)}, bf16[2,32,768]{2,1,0:T(8,128)(2,1)S(1)}, u32[]{:S(2)}, u32[]{:S(2)}) %collective-permute-start) | collective-permute-done | bytes 98336 | tf_op jit(solution)/shard_map/ppermute | solution.py:195
  7.4 2.9 %collective-permute-start.1 = (bf16[2,32,768]{2,1,0:T(8,128)(2,1)S(1)}, bf16[2,32,768]{2,1,0:T(8,128)(2,1)S(1)}, u32[]{:S(2)}, u32[]{:S(2)}) collective-permute-start(bf16[2,32,768]{2,1,0:T(8,128)(2,1)S(1)} %add_convert_fusion.3), channel_id=1, source_target_pairs={{0,2},{1,3},{2,0},{3,1},{4,6},{5,7},{6,4},{7,5},{8,10},{9,11},{10,... | collective-permute-start | bytes 294920 | tf_op jit(solution)/shard_map/ppermute | solution.py:195
  10.3 3.1 %collective-permute-done.1 = bf16[2,32,768]{2,1,0:T(8,128)(2,1)S(1)} collective-permute-done((bf16[2,32,768]{2,1,0:T(8,128)(2,1)S(1)}, bf16[2,32,768]{2,1,0:T(8,128)(2,1)S(1)}, u32[]{:S(2)}, u32[]{:S(2)}) %collective-permute-start.1) | collective-permute-done | bytes 98336 | tf_op jit(solution)/shard_map/ppermute | solution.py:195
  13.5 0.1 collective-permute-start.2
  13.6 1.3 %collective-permute-done.2.other_ref = bf16[2,32,768]{2,1,0:T(8,128)(2,1)S(1)} collective-permute-done((bf16[2,32,768]{2,1,0:T(8,128)(2,1)S(1)}, bf16[2,32,768]{2,1,0:T(8,128)(2,1)S(1)}, u32[]{:S(2)}, u32[]{:S(2)}) %collective-permute-start.2) | collective-permute-done | bytes 98336 | tf_op jit(solution)/shard_map/ppermute | solution.py:195
  14.9 0.0 copy-done
  14.9 0.0 copy-done.1
  14.9 0.4 %contract.1 = f32[2,32,256]{2,1,0:T(8,128)S(1)} custom-call(s32[1]{0:T(128)} %bitcast.own.half, bf16[2,32,768]{2,1,0:T(8,128)(2,1)S(1)} %add_convert_fusion.2.own_ref, bf16[2,32,768]{2,1,0:T(8,128)(2,1)S(1)} %collective-permute-done.2.other_ref, bf16[2,1536,256]{2,1,0:T(8,128)(2,1)S(1)} %bitcast.3, f32[1,256]{1,0:T(1,128)S(1)} %bitcast.6), custom_call_target="tpu_custom_call" | custom-call | flops 100663296 | bytes 1572864 | tf_op jit(solution)/shard_map/contract/pallas_call | solution.py:113
  15.3 1.8 %collective-permute-start.3 = (bf16[2,32,256]{2,1,0:T(8,128)(2,1)S(1)}, bf16[2,32,256]{2,1,0:T(8,128)(2,1)S(1)}, u32[]{:S(2)}, u32[]{:S(2)}) collective-permute-start(bf16[2,32,256]{2,1,0:T(8,128)(2,1)S(1)} %convert_element_type.56), channel_id=1, source_target_pairs={{0,4},{4,0},{8,12},{12,8},{16,20},{20,16},{24,28},{28,24},{1,5},{5... | collective-permute-start | bytes 98312 | tf_op jit(solution)/shard_map/ppermute | solution.py:195
  17.0 2.2 %collective-permute-done.3 = bf16[2,32,256]{2,1,0:T(8,128)(2,1)S(1)} collective-permute-done((bf16[2,32,256]{2,1,0:T(8,128)(2,1)S(1)}, bf16[2,32,256]{2,1,0:T(8,128)(2,1)S(1)}, u32[]{:S(2)}, u32[]{:S(2)}) %collective-permute-start.3) | collective-permute-done | bytes 32800 | tf_op jit(solution)/shard_map/ppermute | solution.py:195
  19.3 3.9 %collective-permute-start.6 = (bf16[2,32,256]{2,1,0:T(8,128)(2,1)S(1)}, bf16[2,32,256]{2,1,0:T(8,128)(2,1)S(1)}, u32[]{:S(2)}, u32[]{:S(2)}) collective-permute-start(bf16[2,32,256]{2,1,0:T(8,128)(2,1)S(1)} %fusion), channel_id=1, source_target_pairs={{0,24},{4,28},{8,16},{12,20},{16,8},{20,12},{24,0},{28,4},{1,25},{... | collective-permute-start | bytes 98312 | tf_op jit(solution)/shard_map/ppermute | solution.py:195
  23.2 0.0 collective-permute-start.5
  23.2 0.6 %collective-permute-start.4 = (bf16[2,32,256]{2,1,0:T(8,128)(2,1)S(1)}, bf16[2,32,256]{2,1,0:T(8,128)(2,1)S(1)}, u32[]{:S(2)}, u32[]{:S(2)}) collective-permute-start(bf16[2,32,256]{2,1,0:T(8,128)(2,1)S(1)} %fusion), channel_id=1, source_target_pairs={{0,8},{4,12},{8,0},{12,4},{16,24},{20,28},{24,16},{28,20},{1,9},{5... | collective-permute-start | bytes 98312 | tf_op jit(solution)/shard_map/ppermute | solution.py:195
  23.8 1.4 %collective-permute-done.6 = bf16[2,32,256]{2,1,0:T(8,128)(2,1)S(1)} collective-permute-done((bf16[2,32,256]{2,1,0:T(8,128)(2,1)S(1)}, bf16[2,32,256]{2,1,0:T(8,128)(2,1)S(1)}, u32[]{:S(2)}, u32[]{:S(2)}) %collective-permute-start.6) | collective-permute-done | bytes 32800 | tf_op jit(solution)/shard_map/ppermute | solution.py:195
  25.2 2.8 %collective-permute-done.5 = bf16[2,32,256]{2,1,0:T(8,128)(2,1)S(1)} collective-permute-done((bf16[2,32,256]{2,1,0:T(8,128)(2,1)S(1)}, bf16[2,32,256]{2,1,0:T(8,128)(2,1)S(1)}, u32[]{:S(2)}, u32[]{:S(2)}) %collective-permute-start.5) | collective-permute-done | bytes 32800 | tf_op jit(solution)/shard_map/ppermute | solution.py:195
  28.0 0.0 collective-permute-done.4
  28.0 0.4 expand.3
  28.4 0.1 collective-permute-start.7
  28.4 0.4 expand.2
  28.8 0.9 %collective-permute-done.7 = bf16[2,32,768]{2,1,0:T(8,128)(2,1)S(1)} collective-permute-done((bf16[2,32,768]{2,1,0:T(8,128)(2,1)S(1)}, bf16[2,32,768]{2,1,0:T(8,128)(2,1)S(1)}, u32[]{:S(2)}, u32[]{:S(2)}) %collective-permute-start.7) | collective-permute-done | bytes 98336 | tf_op jit(solution)/shard_map/ppermute | solution.py:195
  29.8 1.6 %collective-permute-start.8 = (bf16[2,32,768]{2,1,0:T(8,128)(2,1)S(1)}, bf16[2,32,768]{2,1,0:T(8,128)(2,1)S(1)}, u32[]{:S(2)}, u32[]{:S(2)}) collective-permute-start(bf16[2,32,768]{2,1,0:T(8,128)(2,1)S(1)} %add_convert_fusion.1), channel_id=1, source_target_pairs={{0,2},{1,3},{2,0},{3,1},{4,6},{5,7},{6,4},{7,5},{8,10},{9,11},{10,... | collective-permute-start | bytes 294920 | tf_op jit(solution)/shard_map/ppermute | solution.py:195
  31.3 3.3 %collective-permute-done.8 = bf16[2,32,768]{2,1,0:T(8,128)(2,1)S(1)} collective-permute-done((bf16[2,32,768]{2,1,0:T(8,128)(2,1)S(1)}, bf16[2,32,768]{2,1,0:T(8,128)(2,1)S(1)}, u32[]{:S(2)}, u32[]{:S(2)}) %collective-permute-start.8) | collective-permute-done | bytes 98336 | tf_op jit(solution)/shard_map/ppermute | solution.py:195
  34.7 0.1 collective-permute-start.9
  34.8 1.7 %prolong.2.refs_0_ = f32[2,24,32,768]{3,2,1,0:T(8,128)} custom-call(s32[1]{0:T(128)} %bitcast.own.half, bf16[2,32,768]{2,1,0:T(8,128)(2,1)S(1)} %add_convert_fusion.lift_ref, bf16[6,256,768]{2,1,0:T(8,128)(2,1)S(1)} %get-tuple-element.12.bas_ref), custom_call_target="tpu_custom_call" | custom-call | flops 603979776 | bytes 2359296 | tf_op jit(solution)/shard_map/prolong/pallas_call | solution.py:181
  36.5 0.0 collective-permute-done.9.lift_ref
  36.5 1.7 %prolong.3 = f32[2,24,32,768]{3,2,1,0:T(8,128)} custom-call(s32[1]{0:T(128)S(6)} %sub.3.half, bf16[2,32,768]{2,1,0:T(8,128)(2,1)S(1)} %collective-permute-done.9.lift_ref, bf16[6,256,768]{2,1,0:T(8,128)(2,1)S(1)} %get-tuple-element.11.bas_ref, f32[2,24,32,768]{3,2,1,0:T(8,128)} %prolong.2.refs_0_), custom_call_target="tpu_custom_call", output_to_operand_aliasing={{}: (3, {})} | custom-call | flops 603979776 | bytes 2359296 | tf_op jit(solution)/shard_map/prolong/pallas_call | solution.py:181
  (7 shorter events, 0.1 us)
Async XLA Ops:
  0.0 14.9 %copy-start = (bf16[2,24,64,256]{3,2,1,0:T(8,128)(2,1)S(1)}, bf16[2,24,64,256]{3,2,1,0:T(8,128)(2,1)}, u32[]{:S(2)}) copy-start(bf16[2,24,64,256]{3,2,1,0:T(8,128)(2,1)} %param.6) | copy-start | bytes 4718596
  0.0 14.9 %copy-start.1 = (f32[256]{0:T(256)S(1)}, f32[256]{0:T(256)}, u32[]{:S(2)}) copy-start(f32[256]{0:T(256)} %param.7) | copy-start | bytes 3076
  5.9 1.5 %collective-permute-start = (bf16[2,32,768]{2,1,0:T(8,128)(2,1)S(1)}, bf16[2,32,768]{2,1,0:T(8,128)(2,1)S(1)}, u32[]{:S(2)}, u32[]{:S(2)}) collective-permute-start(bf16[2,32,768]{2,1,0:T(8,128)(2,1)S(1)} %get-tuple-element.10), channel_id=1, source_target_pairs={{0,1},{1,0},{2,3},{3,2},{4,5},{5,4},{6,7},{7,6},{8,9},{9,8},{10,11... | collective-permute-start | bytes 294920 | tf_op jit(solution)/shard_map/ppermute | solution.py:195
  7.4 6.0 %collective-permute-start.1 = (bf16[2,32,768]{2,1,0:T(8,128)(2,1)S(1)}, bf16[2,32,768]{2,1,0:T(8,128)(2,1)S(1)}, u32[]{:S(2)}, u32[]{:S(2)}) collective-permute-start(bf16[2,32,768]{2,1,0:T(8,128)(2,1)S(1)} %add_convert_fusion.3), channel_id=1, source_target_pairs={{0,2},{1,3},{2,0},{3,1},{4,6},{5,7},{6,4},{7,5},{8,10},{9,11},{10,... | collective-permute-start | bytes 294920 | tf_op jit(solution)/shard_map/ppermute | solution.py:195
  13.5 1.4 %collective-permute-start.2 = (bf16[2,32,768]{2,1,0:T(8,128)(2,1)S(1)}, bf16[2,32,768]{2,1,0:T(8,128)(2,1)S(1)}, u32[]{:S(2)}, u32[]{:S(2)}) collective-permute-start(bf16[2,32,768]{2,1,0:T(8,128)(2,1)S(1)} %add_convert_fusion.2.own_ref), channel_id=1, source_target_pairs={{0,1},{1,0},{2,3},{3,2},{4,5},{5,4},{6,7},{7,6},{8,9},{9,8},{10,11... | collective-permute-start | bytes 294920 | tf_op jit(solution)/shard_map/ppermute | solution.py:195
  15.3 4.0 %collective-permute-start.3 = (bf16[2,32,256]{2,1,0:T(8,128)(2,1)S(1)}, bf16[2,32,256]{2,1,0:T(8,128)(2,1)S(1)}, u32[]{:S(2)}, u32[]{:S(2)}) collective-permute-start(bf16[2,32,256]{2,1,0:T(8,128)(2,1)S(1)} %convert_element_type.56), channel_id=1, source_target_pairs={{0,4},{4,0},{8,12},{12,8},{16,20},{20,16},{24,28},{28,24},{1,5},{5... | collective-permute-start | bytes 98312 | tf_op jit(solution)/shard_map/ppermute | solution.py:195
  19.3 5.9 %collective-permute-start.6 = (bf16[2,32,256]{2,1,0:T(8,128)(2,1)S(1)}, bf16[2,32,256]{2,1,0:T(8,128)(2,1)S(1)}, u32[]{:S(2)}, u32[]{:S(2)}) collective-permute-start(bf16[2,32,256]{2,1,0:T(8,128)(2,1)S(1)} %fusion), channel_id=1, source_target_pairs={{0,24},{4,28},{8,16},{12,20},{16,8},{20,12},{24,0},{28,4},{1,25},{... | collective-permute-start | bytes 98312 | tf_op jit(solution)/shard_map/ppermute | solution.py:195
  23.2 4.8 %collective-permute-start.5 = (bf16[2,32,256]{2,1,0:T(8,128)(2,1)S(1)}, bf16[2,32,256]{2,1,0:T(8,128)(2,1)S(1)}, u32[]{:S(2)}, u32[]{:S(2)}) collective-permute-start(bf16[2,32,256]{2,1,0:T(8,128)(2,1)S(1)} %fusion), channel_id=1, source_target_pairs={{0,16},{4,20},{8,24},{12,28},{16,0},{20,4},{24,8},{28,12},{1,17},{... | collective-permute-start | bytes 98312 | tf_op jit(solution)/shard_map/ppermute | solution.py:195
  23.2 4.8 %collective-permute-start.4 = (bf16[2,32,256]{2,1,0:T(8,128)(2,1)S(1)}, bf16[2,32,256]{2,1,0:T(8,128)(2,1)S(1)}, u32[]{:S(2)}, u32[]{:S(2)}) collective-permute-start(bf16[2,32,256]{2,1,0:T(8,128)(2,1)S(1)} %fusion), channel_id=1, source_target_pairs={{0,8},{4,12},{8,0},{12,4},{16,24},{20,28},{24,16},{28,20},{1,9},{5... | collective-permute-start | bytes 98312 | tf_op jit(solution)/shard_map/ppermute | solution.py:195
  28.4 1.4 %collective-permute-start.7 = (bf16[2,32,768]{2,1,0:T(8,128)(2,1)S(1)}, bf16[2,32,768]{2,1,0:T(8,128)(2,1)S(1)}, u32[]{:S(2)}, u32[]{:S(2)}) collective-permute-start(bf16[2,32,768]{2,1,0:T(8,128)(2,1)S(1)} %expand.3), channel_id=1, source_target_pairs={{0,1},{1,0},{2,3},{3,2},{4,5},{5,4},{6,7},{7,6},{8,9},{9,8},{10,11... | collective-permute-start | bytes 294920 | tf_op jit(solution)/shard_map/ppermute | solution.py:195
  29.8 4.9 %collective-permute-start.8 = (bf16[2,32,768]{2,1,0:T(8,128)(2,1)S(1)}, bf16[2,32,768]{2,1,0:T(8,128)(2,1)S(1)}, u32[]{:S(2)}, u32[]{:S(2)}) collective-permute-start(bf16[2,32,768]{2,1,0:T(8,128)(2,1)S(1)} %add_convert_fusion.1), channel_id=1, source_target_pairs={{0,2},{1,3},{2,0},{3,1},{4,6},{5,7},{6,4},{7,5},{8,10},{9,11},{10,... | collective-permute-start | bytes 294920 | tf_op jit(solution)/shard_map/ppermute | solution.py:195
  34.7 1.8 %collective-permute-start.9 = (bf16[2,32,768]{2,1,0:T(8,128)(2,1)S(1)}, bf16[2,32,768]{2,1,0:T(8,128)(2,1)S(1)}, u32[]{:S(2)}, u32[]{:S(2)}) collective-permute-start(bf16[2,32,768]{2,1,0:T(8,128)(2,1)S(1)} %add_convert_fusion.lift_ref), channel_id=1, source_target_pairs={{0,1},{1,0},{2,3},{3,2},{4,5},{5,4},{6,7},{7,6},{8,9},{9,8},{10,11... | collective-permute-start | bytes 294920 | tf_op jit(solution)/shard_map/ppermute | solution.py:195

commit v3 on v2

v3 whole, which is shorter than its diff:
```python
import functools

import jax
import jax.numpy as jnp
from jax import lax
from jax.experimental import pallas as pl
from jax.experimental.pallas import tpu as pltpu
from jax.sharding import PartitionSpec as P

BF = jnp.bfloat16
F32 = jnp.float32
NT = (((1,), (1,)), ((), ()))
NN = (((1,), (0,)), ((), ()))
MIB = 1 << 20


def dot(left, right, dims):
    return lax.dot_general(left, right, dims, preferred_element_type=F32)


def project_kernel(res_hbm, bas_hbm, sent_ref, res_ref, bas_ref, sem):
    cols, comp = res_ref.shape[2:]
    vecs = bas_ref.shape[2]
    pair = 2 * vecs
    pairs = sem.shape[1]

    def copies(i):
        two = pl.ds(2 * i, 2)
        return (
            pltpu.make_async_copy(res_hbm.at[:, two], res_ref.at[:, two], sem.at[0, i]),
            pltpu.make_async_copy(bas_hbm.at[:, two], bas_ref.at[:, two], sem.at[1, i]),
        )

    for i in range(pairs):
        for copy in copies(i):
            copy.start()
    first = lax.broadcasted_iota(jnp.int32, (cols, pair), 1) < vecs
    for i in range(pairs):
        for copy in copies(i):
            copy.wait()
        res = res_ref[:, 2 * i : 2 * i + 2].reshape(4 * cols, comp).astype(BF)
        bas = bas_ref[:, 2 * i : 2 * i + 2].reshape(2 * pair, comp).astype(BF)
        prod = dot(res, bas, NT)

        def part(row, lane):
            lanes = slice(lane * pair, (lane + 1) * pair)
            top = prod[2 * row * cols : (2 * row + 1) * cols, lanes]
            low = prod[(2 * row + 1) * cols : (2 * row + 2) * cols, lanes]
            return jnp.where(first, top, low)

        lanes = slice(i * pair, (i + 1) * pair)
        re, im = part(0, 0) + part(1, 1), part(1, 0) - part(0, 1)
        for row, value in ((0, re), (1, im)):
            sent_ref[row, :, lanes] = value.astype(BF)


def hbm(value):
    return pltpu.with_memory_space_constraint(value, pltpu.HBM)


def whole():
    return pl.BlockSpec(memory_space=pltpu.VMEM)


def scalar():
    return pl.BlockSpec(memory_space=pltpu.SMEM)


def project(residual, basis):
    _, blocks, cols, comp = residual.shape
    vecs = basis.shape[2]
    return pl.pallas_call(
        project_kernel,
        in_specs=[pl.BlockSpec(memory_space=pltpu.HBM)] * 2,
        out_specs=whole(),
        out_shape=jax.ShapeDtypeStruct((2, cols, blocks * vecs), BF),
        scratch_shapes=[
            pltpu.VMEM(residual.shape, F32),
            pltpu.VMEM(basis.shape, F32),
            pltpu.SemaphoreType.DMA((2, blocks // 2)),
        ],
        compiler_params=pltpu.CompilerParams(vmem_limit_bytes=18 * MIB),
        cost_estimate=pl.CostEstimate(
            flops=16 * blocks * cols * vecs * comp, bytes_accessed=(residual.size + basis.size) * 4, transcendentals=0
        ),
        name="project",
    )(hbm(residual), hbm(basis))


def contract_kernel(active, own_ref, sister_ref, wgt_ref, *refs):
    *coarse_refs, out_ref = refs
    cols, depth = coarse_refs[0].shape[1:]
    count = own_ref.shape[2]

    @pl.when(active[0] == 1)
    def _():
        coarse = total([ref[...] for ref in coarse_refs]).astype(BF).reshape(2 * cols, depth)
        for i, eig_ref in enumerate((own_ref, sister_ref)):
            by_re = dot(coarse, eig_ref[0], NN)
            by_im = dot(coarse, eig_ref[1], NN)
            re = by_re[:cols] + by_im[cols:]
            im = by_re[cols:] - by_im[:cols]
            if i == 0:
                re, im = re * wgt_ref[...], im * wgt_ref[...]
            out_ref[0, :, i * count : (i + 1) * count] = re.astype(BF)
            out_ref[1, :, i * count : (i + 1) * count] = im.astype(BF)


def contract(active, coarse, own, sister, weights):
    _, cols, depth = coarse[0].shape
    count = own.shape[2]
    return pl.pallas_call(
        contract_kernel,
        in_specs=[scalar()] + [whole()] * 3 + [whole()] * len(coarse),
        out_specs=whole(),
        out_shape=jax.ShapeDtypeStruct((2, cols, 2 * count), BF),
        compiler_params=pltpu.CompilerParams(vmem_limit_bytes=4 * MIB),
        cost_estimate=pl.CostEstimate(flops=16 * cols * depth * count, bytes_accessed=own.size * 4, transcendentals=0),
        name="contract",
    )(active, own, sister, weights, *coarse)


def expand_kernel(own_first, active, own_ref, sister_ref, *refs):
    *wgt_refs, out_ref = refs
    cols = out_ref.shape[1]
    count = own_ref.shape[2]

    @pl.when(active[0] == 1)
    def _():
        whole_wgt = total([ref[...] for ref in wgt_refs]).astype(BF)
        re = im = None
        for i, eig_ref in enumerate((own_ref, sister_ref) if own_first else (sister_ref, own_ref)):
            weighted = whole_wgt[:, :, i * count : (i + 1) * count].reshape(2 * cols, count)
            by_re = dot(weighted, eig_ref[0], NT)
            by_im = dot(weighted, eig_ref[1], NT)
            re = by_re[:cols] - by_im[cols:] + (0 if re is None else re)
            im = by_re[cols:] + by_im[:cols] + (0 if im is None else im)
        out_ref[0] = re.astype(BF)
        out_ref[1] = im.astype(BF)


def expand(active, weighted, own, sister, own_first):
    cols = weighted[0].shape[1]
    depth, count = own.shape[1:]
    return pl.pallas_call(
        functools.partial(expand_kernel, own_first),
        in_specs=[scalar()] + [whole()] * 2 + [whole()] * len(weighted),
        out_specs=whole(),
        out_shape=jax.ShapeDtypeStruct((2, cols, depth), BF),
        compiler_params=pltpu.CompilerParams(vmem_limit_bytes=4 * MIB),
        cost_estimate=pl.CostEstimate(flops=16 * cols * depth * count, bytes_accessed=own.size * 4, transcendentals=0),
        name="expand",
    )(active, own, sister, *weighted)


def load_kernel(from_hbm, to_ref, sem):
    copy = pltpu.make_async_copy(from_hbm, to_ref, sem)
    copy.start()
    copy.wait()


def load(value):
    return pl.pallas_call(
        load_kernel,
        in_specs=[pl.BlockSpec(memory_space=pltpu.HBM)],
        out_specs=whole(),
        out_shape=pltpu.VMEM(value.shape, value.dtype),
        scratch_shapes=[pltpu.SemaphoreType.DMA],
        compiler_params=pltpu.CompilerParams(vmem_limit_bytes=4 * MIB),
        cost_estimate=pl.CostEstimate(flops=0, bytes_accessed=value.size * 4, transcendentals=0),
        name="load",
    )(hbm(value))


def prolong_kernel(active, sum_ref, arrived_ref, bas_ref, out_hbm, out_ref, sem):
    cols, comp = out_ref.shape[2:]
    pair = 2 * bas_ref.shape[2]
    pairs = sem.shape[0]
    first = lax.broadcasted_iota(jnp.int32, (cols, pair), 1) < pair // 2

    def copy(i):
        two = pl.ds(2 * i, 2)
        return pltpu.make_async_copy(out_ref.at[:, two], out_hbm.at[:, two], sem.at[i])

    for i in range(pairs):
        lanes = slice(i * pair, (i + 1) * pair)
        re, im = (jnp.where(active[0] == 1, arrived_ref[row, :, lanes], sum_ref[row, :, lanes]) for row in range(2))
        none = jnp.zeros_like(re)
        re0, re1 = jnp.where(first, re, none), jnp.where(first, none, re)
        im0, im1 = jnp.where(first, im, none), jnp.where(first, none, im)
        left = jnp.concatenate(
            [
                jnp.concatenate([re0, re1, im0, im1], axis=0),
                jnp.concatenate([-im0, -im1, re0, re1], axis=0),
            ],
            axis=1,
        )
        bas = bas_ref[:, 2 * i : 2 * i + 2].reshape(2 * pair, comp).astype(BF)
        out_ref[:, 2 * i : 2 * i + 2] = dot(left, bas, NN).reshape(2, 2, cols, comp)
        copy(i).start()
    for i in range(pairs):
        copy(i).wait()


def prolong(active, lifted, arrived, basis, shape):
    vecs, comp = basis.shape[2:]
    cols = lifted.shape[1]
    pairs = shape[1] // 2
    return pl.pallas_call(
        prolong_kernel,
        in_specs=[scalar()] + [whole()] * 3,
        out_specs=pl.BlockSpec(memory_space=pltpu.HBM),
        out_shape=jax.ShapeDtypeStruct(shape, F32),
        scratch_shapes=[pltpu.VMEM(shape, F32), pltpu.SemaphoreType.DMA((pairs,))],
        compiler_params=pltpu.CompilerParams(vmem_limit_bytes=8 * MIB),
        cost_estimate=pl.CostEstimate(flops=64 * pairs * cols * vecs * comp, bytes_accessed=pairs * cols * comp * 16, transcendentals=0),
        name="prolong",
    )(active, lifted, arrived, basis)


class Slice:
    def __init__(self, regions, shares):
        self.regions, self.shares = regions, shares

    def swap(self, value):
        return lax.ppermute(value, "eig", [(i, i ^ 1) for i in range(self.shares)])

    def cross(self, value, sender, region=0, chip=0):
        pairs = []
        for i in range(self.regions * self.shares):
            far = (i ^ (region * self.shares) ^ (2 * chip)) ^ 1
            pairs.append((i, far if i % 2 == sender else i ^ 1))
        return lax.ppermute(value, ("region", "eig"), pairs)

    def region_steps(self):
        step = 1
        while step < self.regions:
            four = step > 1 and 2 * step < self.regions
            yield [step, 2 * step, 3 * step] if four else [step]
            step *= 4 if four else 2

    def chip_steps(self):
        return range(1, self.shares // 2)


def total(terms):
    value = terms[0].astype(F32)
    for term in terms[1:]:
        value = value + term.astype(F32)
    return value


def add_kernel(scale_ref, *refs):
    *term_refs, out_ref = refs
    value = total([ref[...] for ref in term_refs])
    half = out_ref.shape[2] // 2
    if scale_ref is None:
        out_ref[...] = value.astype(BF)
    else:
        out_ref[:, :, :half] = value[:, :, :half].astype(BF)
        out_ref[:, :, half:] = (value[:, :, half:] * scale_ref[...]).astype(BF)


def add(terms, scale=None):
    kernel = functools.partial(add_kernel, None) if scale is None else add_kernel
    return pl.pallas_call(
        kernel,
        in_specs=([] if scale is None else [whole()]) + [whole()] * len(terms),
        out_specs=whole(),
        out_shape=jax.ShapeDtypeStruct(terms[0].shape, BF),
        compiler_params=pltpu.CompilerParams(vmem_limit_bytes=4 * MIB),
        cost_estimate=pl.CostEstimate(flops=terms[0].size * 2, bytes_accessed=terms[0].size * 4, transcendentals=0),
        name="add",
    )(*([] if scale is None else [scale]), *terms)


def shards(regions, shares, residual, basis, eigvecs, weights):
    place = Slice(regions, shares)
    core = (lax.axis_index("eig") % 2).astype(jnp.int32).reshape(1)
    blocks, vecs = basis.shape[1:3]
    count = eigvecs.shape[3]
    own = eigvecs.reshape(2, blocks * vecs, count)
    weights = weights.reshape(1, 1, count)

    part = project(residual, basis)
    chip_sum = add([part, place.swap(part)])
    sister = place.swap(lax.optimization_barrier((own, chip_sum))[0])
    holder = 1
    coarse = [chip_sum] + [place.cross(chip_sum, 0, chip=s) for s in place.chip_steps()]

    start = holder
    active = (core == holder).astype(jnp.int32)
    value = contract(active, coarse, own, sister, weights.reshape(1, count))
    steps = list(place.region_steps())
    for i, step in enumerate(steps):
        terms = [place.swap(value)] + [place.cross(value, holder, region=s) for s in step]
        holder = 1 - holder
        if i < len(steps) - 1:
            value = add(terms, weights if i == 0 else None)

    active = (core == holder).astype(jnp.int32)
    lifted = expand(active, terms, own, sister, holder == start)
    in_vmem = load(lax.optimization_barrier((basis, lifted))[0])
    terms = [place.swap(lifted)] + [place.cross(lifted, holder, chip=s) for s in place.chip_steps()]
    terms, in_vmem = lax.optimization_barrier((terms, in_vmem))
    lifted = add(terms)
    return prolong(active, lifted, place.swap(lifted), in_vmem, residual.shape)


def solution(mesh):
    split = P(None, "region", None, "eig")
    return jax.shard_map(
        functools.partial(shards, mesh.shape["region"], mesh.shape["eig"]),
        mesh=mesh,
        in_specs=(split, split, split, P("eig")),
        out_specs=split,
        check_vma=False,
    )
```

time: 38.4 us -> 35.1 us (0.914)
  waiting for transfers between devices: 16 us -> 11.3 us
  Pallas kernels: 10.4 us -> 12.2 us
    ppermute x10 -> x12, waiting for transfers between devices: 16 us -> 11.4 us  [the longest x6 8.84 us: cross(): return lax.ppermute(value, ('region', 'eig'), pairs)]
    pallas_call x5 -> x7, Pallas kernels: 4.49 us -> 6.32 us  [the longest x1 3.69 us: load(): pl.pallas_call(load_kernel, in_specs=[pl.BlockSpec(memory_space=pltpu.HBM...]
    ppermute x10 -> x12, starting transfers between devices: 11.6 us -> 11.3 us  [the longest x6 9.05 us: cross(): return lax.ppermute(value, ('region', 'eig'), pairs)]
  transfers between devices with their start and end apart: 10 -> 12, of which waited for: 8 -> 8; matrix products, arithmetic and copies ran while one was open for 0% -> 0% of each run, Pallas kernels for 5% -> 11%
where the time goes in v3:
time: 35.1 us; the launch traced here: 34.9 us
  Pallas kernels  12.2 us (35%)
  starting transfers between devices  11.3 us (32%)
  waiting for transfers between devices  11.3 us (32%)
    ppermute x6, starting transfers between devices, cross(): return lax.ppermute(value, ('region', 'eig'), pairs)  9.05 us
    ppermute x6, waiting for transfers between devices, cross(): return lax.ppermute(value, ('region', 'eig'), pairs)  8.84 us
    pallas_call x1, Pallas kernels, project(): pl.pallas_call(project_kernel, in_specs=[pl.BlockSpec(memory_space=pltpu....  5.92 us
    pallas_call x1, Pallas kernels, load(): pl.pallas_call(load_kernel, in_specs=[pl.BlockSpec(memory_space=pltpu.HBM...  3.69 us
    pallas_call x1, Pallas kernels, prolong(): pl.pallas_call(prolong_kernel, in_specs=[scalar()] + [whole()] * 3, out_s...  2.51 us
    ppermute x6, waiting for transfers between devices, swap(): return lax.ppermute(value, 'eig', [(i, i ^ 1) for i in range(self.shares)])  2.51 us
    ppermute x6, starting transfers between devices, swap(): return lax.ppermute(value, 'eig', [(i, i ^ 1) for i in range(self.shares)])  2.21 us
  transfers between devices with their start and end apart: 12, of which 8 were waited for; matrix products, arithmetic and copies ran while one was open for 0% of the time, Pallas kernels for 11%

profile of v3, /device:TPU:0, one launch (start us, length us, event | category | flops | bytes accessed | tf_op | source)
XLA Modules:
  0.0 34.9 jit_solution(3773855283874068119)
XLA Ops:
  0.0 0.0 copy-start
  0.0 0.0 copy-start.1
  0.0 5.9 %project.1.refs_0_ = bf16[2,32,1536]{2,1,0:T(8,128)(2,1)S(1)} custom-call(f32[2,24,32,768]{3,2,1,0:T(8,128)} %res_hbm.1, f32[2,24,64,768]{3,2,1,0:T(8,128)} %from_hbm), custom_call_target="tpu_custom_call" | custom-call | flops 603979776 | bytes 14155776 | tf_op jit(solution)/shard_map/project/pallas_call | solution.py:72
  5.9 0.5 %collective-permute-start = (bf16[2,32,1536]{2,1,0:T(8,128)(2,1)S(1)}, bf16[2,32,1536]{2,1,0:T(8,128)(2,1)S(1)}, u32[]{:S(2)}, u32[]{:S(2)}) collective-permute-start(bf16[2,32,1536]{2,1,0:T(8,128)(2,1)S(1)} %project.1.refs_0_), channel_id=1, source_target_pairs={{0,1},{1,0},{2,3},{3,2},{4,5},{5,4},{6,7},{7,6},{8,9},{9,8},{10,11... | collective-permute-start | bytes 589832 | tf_op jit(solution)/shard_map/ppermute | solution.py:226
  6.5 1.1 %collective-permute-done.refs_1_ = bf16[2,32,1536]{2,1,0:T(8,128)(2,1)S(1)} collective-permute-done((bf16[2,32,1536]{2,1,0:T(8,128)(2,1)S(1)}, bf16[2,32,1536]{2,1,0:T(8,128)(2,1)S(1)}, u32[]{:S(2)}, u32[]{:S(2)}) %collective-permute-start) | collective-permute-done | bytes 196640 | tf_op jit(solution)/shard_map/ppermute | solution.py:226
  7.6 0.0 copy-done
  7.6 0.4 %collective-permute-start.1 = (bf16[2,1536,256]{2,1,0:T(8,128)(2,1)S(1)}, bf16[2,1536,256]{2,1,0:T(8,128)(2,1)S(1)}, u32[]{:S(2)}, u32[]{:S(2)}) collective-permute-start(bf16[2,1536,256]{2,1,0:T(8,128)(2,1)S(1)} %bitcast.4), channel_id=1, source_target_pairs={{0,1},{1,0},{2,3},{3,2},{4,5},{5,4},{6,7},{7,6},{8,9},{9,8},{10,11... | collective-permute-start | bytes 4718600 | tf_op jit(solution)/shard_map/ppermute | solution.py:226
  8.0 2.6 %collective-permute-start.2 = (bf16[2,32,1536]{2,1,0:T(8,128)(2,1)S(1)}, bf16[2,32,1536]{2,1,0:T(8,128)(2,1)S(1)}, u32[]{:S(2)}, u32[]{:S(2)}) collective-permute-start(bf16[2,32,1536]{2,1,0:T(8,128)(2,1)S(1)} %add.8.refs_0_), channel_id=1, source_target_pairs={{0,3},{1,0},{2,1},{3,2},{4,7},{5,4},{6,5},{7,6},{8,11},{9,8},{10,9... | collective-permute-start | bytes 589832 | tf_op jit(solution)/shard_map/ppermute | solution.py:233
  10.6 3.2 %collective-permute-done.2.refs_1_ = bf16[2,32,1536]{2,1,0:T(8,128)(2,1)S(1)} collective-permute-done((bf16[2,32,1536]{2,1,0:T(8,128)(2,1)S(1)}, bf16[2,32,1536]{2,1,0:T(8,128)(2,1)S(1)}, u32[]{:S(2)}, u32[]{:S(2)}) %collective-permute-start.2) | collective-permute-done | bytes 196640 | tf_op jit(solution)/shard_map/ppermute | solution.py:233
  13.8 0.0 collective-permute-done.1.sister_ref
  13.8 0.0 copy-done.1
  13.8 1.0 %collective-permute-start.4 = (bf16[2,32,512]{2,1,0:T(8,128)(2,1)S(1)}, bf16[2,32,512]{2,1,0:T(8,128)(2,1)S(1)}, u32[]{:S(2)}, u32[]{:S(2)}) collective-permute-start(bf16[2,32,512]{2,1,0:T(8,128)(2,1)S(1)} %contract.1), channel_id=1, source_target_pairs={{0,1},{1,4},{2,3},{3,6},{4,5},{5,0},{6,7},{7,2},{8,9},{9,12},{10,1... | collective-permute-start | bytes 196616 | tf_op jit(solution)/shard_map/ppermute | solution.py:233
  14.9 0.6 %collective-permute-start.3 = (bf16[2,32,512]{2,1,0:T(8,128)(2,1)S(1)}, bf16[2,32,512]{2,1,0:T(8,128)(2,1)S(1)}, u32[]{:S(2)}, u32[]{:S(2)}) collective-permute-start(bf16[2,32,512]{2,1,0:T(8,128)(2,1)S(1)} %contract.1), channel_id=1, source_target_pairs={{0,1},{1,0},{2,3},{3,2},{4,5},{5,4},{6,7},{7,6},{8,9},{9,8},{10,11... | collective-permute-start | bytes 196616 | tf_op jit(solution)/shard_map/ppermute | solution.py:226
  15.5 2.9 %collective-permute-done.4.refs_1_ = bf16[2,32,512]{2,1,0:T(8,128)(2,1)S(1)} collective-permute-done((bf16[2,32,512]{2,1,0:T(8,128)(2,1)S(1)}, bf16[2,32,512]{2,1,0:T(8,128)(2,1)S(1)}, u32[]{:S(2)}, u32[]{:S(2)}) %collective-permute-start.4) | collective-permute-done | bytes 65568 | tf_op jit(solution)/shard_map/ppermute | solution.py:233
  18.4 0.0 collective-permute-done.3.refs_0_
  18.4 1.6 %collective-permute-start.8 = (bf16[2,32,512]{2,1,0:T(8,128)(2,1)S(1)}, bf16[2,32,512]{2,1,0:T(8,128)(2,1)S(1)}, u32[]{:S(2)}, u32[]{:S(2)}) collective-permute-start(bf16[2,32,512]{2,1,0:T(8,128)(2,1)S(1)} %add.9), channel_id=1, source_target_pairs={{0,25},{1,0},{2,27},{3,2},{4,29},{5,4},{6,31},{7,6},{8,17},{9,8},{... | collective-permute-start | bytes 196616 | tf_op jit(solution)/shard_map/ppermute | solution.py:233
  20.1 1.1 %collective-permute-start.7 = (bf16[2,32,512]{2,1,0:T(8,128)(2,1)S(1)}, bf16[2,32,512]{2,1,0:T(8,128)(2,1)S(1)}, u32[]{:S(2)}, u32[]{:S(2)}) collective-permute-start(bf16[2,32,512]{2,1,0:T(8,128)(2,1)S(1)} %add.9), channel_id=1, source_target_pairs={{0,17},{1,0},{2,19},{3,2},{4,21},{5,4},{6,23},{7,6},{8,25},{9,8},{... | collective-permute-start | bytes 196616 | tf_op jit(solution)/shard_map/ppermute | solution.py:233
  21.2 0.0 collective-permute-start.6
  21.2 0.5 %collective-permute-start.5 = (bf16[2,32,512]{2,1,0:T(8,128)(2,1)S(1)}, bf16[2,32,512]{2,1,0:T(8,128)(2,1)S(1)}, u32[]{:S(2)}, u32[]{:S(2)}) collective-permute-start(bf16[2,32,512]{2,1,0:T(8,128)(2,1)S(1)} %add.9), channel_id=1, source_target_pairs={{0,1},{1,0},{2,3},{3,2},{4,5},{5,4},{6,7},{7,6},{8,9},{9,8},{10,11... | collective-permute-start | bytes 196616 | tf_op jit(solution)/shard_map/ppermute | solution.py:226
  21.7 0.3 collective-permute-done.8.refs_3_
  22.0 1.1 %collective-permute-done.7.refs_2_ = bf16[2,32,512]{2,1,0:T(8,128)(2,1)S(1)} collective-permute-done((bf16[2,32,512]{2,1,0:T(8,128)(2,1)S(1)}, bf16[2,32,512]{2,1,0:T(8,128)(2,1)S(1)}, u32[]{:S(2)}, u32[]{:S(2)}) %collective-permute-start.7) | collective-permute-done | bytes 65568 | tf_op jit(solution)/shard_map/ppermute | solution.py:233
  23.1 0.6 %collective-permute-done.6.refs_1_ = bf16[2,32,512]{2,1,0:T(8,128)(2,1)S(1)} collective-permute-done((bf16[2,32,512]{2,1,0:T(8,128)(2,1)S(1)}, bf16[2,32,512]{2,1,0:T(8,128)(2,1)S(1)}, u32[]{:S(2)}, u32[]{:S(2)}) %collective-permute-start.6) | collective-permute-done | bytes 65568 | tf_op jit(solution)/shard_map/ppermute | solution.py:233
  23.7 0.0 collective-permute-done.5.refs_0_
  23.7 2.7 %collective-permute-start.10 = (bf16[2,32,1536]{2,1,0:T(8,128)(2,1)S(1)}, bf16[2,32,1536]{2,1,0:T(8,128)(2,1)S(1)}, u32[]{:S(2)}, u32[]{:S(2)}) collective-permute-start(bf16[2,32,1536]{2,1,0:T(8,128)(2,1)S(1)} %expand.1), channel_id=1, source_target_pairs={{0,1},{1,2},{2,3},{3,0},{4,5},{5,6},{6,7},{7,4},{8,9},{9,10},{10,1... | collective-permute-start | bytes 589832 | tf_op jit(solution)/shard_map/ppermute | solution.py:233
  26.4 0.1 collective-permute-start.9
  26.4 3.7 %load.1.bas_ref = f32[2,24,64,768]{3,2,1,0:T(8,128)S(1)} custom-call(f32[2,24,64,768]{3,2,1,0:T(8,128)} %from_hbm), custom_call_target="tpu_custom_call" | custom-call | bytes 9437184 | tf_op jit(solution)/shard_map/load/pallas_call | solution.py:163
  30.1 0.7 %collective-permute-done.10.refs_1_ = bf16[2,32,1536]{2,1,0:T(8,128)(2,1)S(1)} collective-permute-done((bf16[2,32,1536]{2,1,0:T(8,128)(2,1)S(1)}, bf16[2,32,1536]{2,1,0:T(8,128)(2,1)S(1)}, u32[]{:S(2)}, u32[]{:S(2)}) %collective-permute-start.10) | collective-permute-done | bytes 196640 | tf_op jit(solution)/shard_map/ppermute | solution.py:233
  30.8 0.0 collective-permute-done.9.refs_0_
  30.8 0.1 add.10.sum_ref
  30.9 0.1 collective-permute-start.11
  31.0 1.4 %collective-permute-done.11.arrived_ref = bf16[2,32,1536]{2,1,0:T(8,128)(2,1)S(1)} collective-permute-done((bf16[2,32,1536]{2,1,0:T(8,128)(2,1)S(1)}, bf16[2,32,1536]{2,1,0:T(8,128)(2,1)S(1)}, u32[]{:S(2)}, u32[]{:S(2)}) %collective-permute-start.11) | collective-permute-done | bytes 196640 | tf_op jit(solution)/shard_map/ppermute | solution.py:226
  32.4 2.5 %prolong.1 = f32[2,24,32,768]{3,2,1,0:T(8,128)} custom-call(s32[1]{0:T(128)} %bitcast.active, bf16[2,32,1536]{2,1,0:T(8,128)(2,1)S(1)} %add.10.sum_ref, bf16[2,32,1536]{2,1,0:T(8,128)(2,1)S(1)} %collective-permute-done.11.arrived_ref, f32[2,24,64,768]{3,2,1,0:T(8,128)S(1)} %load.1.bas_ref), custom_call_target="tpu_custom_call" | custom-call | flops 1207959552 | bytes 4718592 | tf_op jit(solution)/shard_map/prolong/pallas_call | solution.py:209
  (4 shorter events, 0.1 us)
Async XLA Ops:
  0.0 7.6 %copy-start = (bf16[2,24,64,256]{3,2,1,0:T(8,128)(2,1)S(1)}, bf16[2,24,64,256]{3,2,1,0:T(8,128)(2,1)}, u32[]{:S(2)}) copy-start(bf16[2,24,64,256]{3,2,1,0:T(8,128)(2,1)} %param.6) | copy-start | bytes 4718596
  0.0 13.8 %copy-start.1 = (f32[256]{0:T(256)S(1)}, f32[256]{0:T(256)}, u32[]{:S(2)}) copy-start(f32[256]{0:T(256)} %param.7) | copy-start | bytes 3076
  5.9 1.6 %collective-permute-start = (bf16[2,32,1536]{2,1,0:T(8,128)(2,1)S(1)}, bf16[2,32,1536]{2,1,0:T(8,128)(2,1)S(1)}, u32[]{:S(2)}, u32[]{:S(2)}) collective-permute-start(bf16[2,32,1536]{2,1,0:T(8,128)(2,1)S(1)} %project.1.refs_0_), channel_id=1, source_target_pairs={{0,1},{1,0},{2,3},{3,2},{4,5},{5,4},{6,7},{7,6},{8,9},{9,8},{10,11... | collective-permute-start | bytes 589832 | tf_op jit(solution)/shard_map/ppermute | solution.py:226
  7.6 6.3 %collective-permute-start.1 = (bf16[2,1536,256]{2,1,0:T(8,128)(2,1)S(1)}, bf16[2,1536,256]{2,1,0:T(8,128)(2,1)S(1)}, u32[]{:S(2)}, u32[]{:S(2)}) collective-permute-start(bf16[2,1536,256]{2,1,0:T(8,128)(2,1)S(1)} %bitcast.4), channel_id=1, source_target_pairs={{0,1},{1,0},{2,3},{3,2},{4,5},{5,4},{6,7},{7,6},{8,9},{9,8},{10,11... | collective-permute-start | bytes 4718600 | tf_op jit(solution)/shard_map/ppermute | solution.py:226
  8.0 5.8 %collective-permute-start.2 = (bf16[2,32,1536]{2,1,0:T(8,128)(2,1)S(1)}, bf16[2,32,1536]{2,1,0:T(8,128)(2,1)S(1)}, u32[]{:S(2)}, u32[]{:S(2)}) collective-permute-start(bf16[2,32,1536]{2,1,0:T(8,128)(2,1)S(1)} %add.8.refs_0_), channel_id=1, source_target_pairs={{0,3},{1,0},{2,1},{3,2},{4,7},{5,4},{6,5},{7,6},{8,11},{9,8},{10,9... | collective-permute-start | bytes 589832 | tf_op jit(solution)/shard_map/ppermute | solution.py:233
  13.8 4.6 %collective-permute-start.4 = (bf16[2,32,512]{2,1,0:T(8,128)(2,1)S(1)}, bf16[2,32,512]{2,1,0:T(8,128)(2,1)S(1)}, u32[]{:S(2)}, u32[]{:S(2)}) collective-permute-start(bf16[2,32,512]{2,1,0:T(8,128)(2,1)S(1)} %contract.1), channel_id=1, source_target_pairs={{0,1},{1,4},{2,3},{3,6},{4,5},{5,0},{6,7},{7,2},{8,9},{9,12},{10,1... | collective-permute-start | bytes 196616 | tf_op jit(solution)/shard_map/ppermute | solution.py:233
  14.9 3.5 %collective-permute-start.3 = (bf16[2,32,512]{2,1,0:T(8,128)(2,1)S(1)}, bf16[2,32,512]{2,1,0:T(8,128)(2,1)S(1)}, u32[]{:S(2)}, u32[]{:S(2)}) collective-permute-start(bf16[2,32,512]{2,1,0:T(8,128)(2,1)S(1)} %contract.1), channel_id=1, source_target_pairs={{0,1},{1,0},{2,3},{3,2},{4,5},{5,4},{6,7},{7,6},{8,9},{9,8},{10,11... | collective-permute-start | bytes 196616 | tf_op jit(solution)/shard_map/ppermute | solution.py:226
  18.4 3.6 %collective-permute-start.8 = (bf16[2,32,512]{2,1,0:T(8,128)(2,1)S(1)}, bf16[2,32,512]{2,1,0:T(8,128)(2,1)S(1)}, u32[]{:S(2)}, u32[]{:S(2)}) collective-permute-start(bf16[2,32,512]{2,1,0:T(8,128)(2,1)S(1)} %add.9), channel_id=1, source_target_pairs={{0,25},{1,0},{2,27},{3,2},{4,29},{5,4},{6,31},{7,6},{8,17},{9,8},{... | collective-permute-start | bytes 196616 | tf_op jit(solution)/shard_map/ppermute | solution.py:233
  20.1 3.0 %collective-permute-start.7 = (bf16[2,32,512]{2,1,0:T(8,128)(2,1)S(1)}, bf16[2,32,512]{2,1,0:T(8,128)(2,1)S(1)}, u32[]{:S(2)}, u32[]{:S(2)}) collective-permute-start(bf16[2,32,512]{2,1,0:T(8,128)(2,1)S(1)} %add.9), channel_id=1, source_target_pairs={{0,17},{1,0},{2,19},{3,2},{4,21},{5,4},{6,23},{7,6},{8,25},{9,8},{... | collective-permute-start | bytes 196616 | tf_op jit(solution)/shard_map/ppermute | solution.py:233
  21.2 2.5 %collective-permute-start.6 = (bf16[2,32,512]{2,1,0:T(8,128)(2,1)S(1)}, bf16[2,32,512]{2,1,0:T(8,128)(2,1)S(1)}, u32[]{:S(2)}, u32[]{:S(2)}) collective-permute-start(bf16[2,32,512]{2,1,0:T(8,128)(2,1)S(1)} %add.9), channel_id=1, source_target_pairs={{0,9},{1,0},{2,11},{3,2},{4,13},{5,4},{6,15},{7,6},{8,1},{9,8},{10... | collective-permute-start | bytes 196616 | tf_op jit(solution)/shard_map/ppermute | solution.py:233
  21.2 2.5 %collective-permute-start.5 = (bf16[2,32,512]{2,1,0:T(8,128)(2,1)S(1)}, bf16[2,32,512]{2,1,0:T(8,128)(2,1)S(1)}, u32[]{:S(2)}, u32[]{:S(2)}) collective-permute-start(bf16[2,32,512]{2,1,0:T(8,128)(2,1)S(1)} %add.9), channel_id=1, source_target_pairs={{0,1},{1,0},{2,3},{3,2},{4,5},{5,4},{6,7},{7,6},{8,9},{9,8},{10,11... | collective-permute-start | bytes 196616 | tf_op jit(solution)/shard_map/ppermute | solution.py:226
  23.7 7.1 %collective-permute-start.10 = (bf16[2,32,1536]{2,1,0:T(8,128)(2,1)S(1)}, bf16[2,32,1536]{2,1,0:T(8,128)(2,1)S(1)}, u32[]{:S(2)}, u32[]{:S(2)}) collective-permute-start(bf16[2,32,1536]{2,1,0:T(8,128)(2,1)S(1)} %expand.1), channel_id=1, source_target_pairs={{0,1},{1,2},{2,3},{3,0},{4,5},{5,6},{6,7},{7,4},{8,9},{9,10},{10,1... | collective-permute-start | bytes 589832 | tf_op jit(solution)/shard_map/ppermute | solution.py:233
  26.4 4.5 %collective-permute-start.9 = (bf16[2,32,1536]{2,1,0:T(8,128)(2,1)S(1)}, bf16[2,32,1536]{2,1,0:T(8,128)(2,1)S(1)}, u32[]{:S(2)}, u32[]{:S(2)}) collective-permute-start(bf16[2,32,1536]{2,1,0:T(8,128)(2,1)S(1)} %expand.1), channel_id=1, source_target_pairs={{0,1},{1,0},{2,3},{3,2},{4,5},{5,4},{6,7},{7,6},{8,9},{9,8},{10,11... | collective-permute-start | bytes 589832 | tf_op jit(solution)/shard_map/ppermute | solution.py:226
  30.9 1.5 %collective-permute-start.11 = (bf16[2,32,1536]{2,1,0:T(8,128)(2,1)S(1)}, bf16[2,32,1536]{2,1,0:T(8,128)(2,1)S(1)}, u32[]{:S(2)}, u32[]{:S(2)}) collective-permute-start(bf16[2,32,1536]{2,1,0:T(8,128)(2,1)S(1)} %add.10.sum_ref), channel_id=1, source_target_pairs={{0,1},{1,0},{2,3},{3,2},{4,5},{5,4},{6,7},{7,6},{8,9},{9,8},{10,11... | collective-permute-start | bytes 589832 | tf_op jit(solution)/shard_map/ppermute | solution.py:226

commit v4 on v3

--- a/solution.py
+++ b/solution.py
@@ -1,4 +1,5 @@
 import functools
+import math
 
 import jax
 import jax.numpy as jnp
@@ -153,29 +154,32 @@
     )(active, own, sister, *weighted)
 
 
-def load_kernel(from_hbm, to_ref, sem):
-    copy = pltpu.make_async_copy(from_hbm, to_ref, sem)
+def load_kernel(start, from_hbm, to_ref, sem):
+    copy = pltpu.make_async_copy(from_hbm.at[:, pl.ds(start, to_ref.shape[1])], to_ref, sem)
     copy.start()
     copy.wait()
 
 
-def load(value):
-    return pl.pallas_call(
-        load_kernel,
+def load(value, start, size, after):
+    shape = value.shape[:1] + (size,) + value.shape[2:]
+    return pl.pallas_call(
+        functools.partial(load_kernel, start),
         in_specs=[pl.BlockSpec(memory_space=pltpu.HBM)],
         out_specs=whole(),
-        out_shape=pltpu.VMEM(value.shape, value.dtype),
+        out_shape=pltpu.VMEM(shape, value.dtype),
         scratch_shapes=[pltpu.SemaphoreType.DMA],
         compiler_params=pltpu.CompilerParams(vmem_limit_bytes=4 * MIB),
-        cost_estimate=pl.CostEstimate(flops=0, bytes_accessed=value.size * 4, transcendentals=0),
+        cost_estimate=pl.CostEstimate(flops=0, bytes_accessed=math.prod(shape) * 4, transcendentals=0),
         name="load",
-    )(hbm(value))
-
-
-def prolong_kernel(active, sum_ref, arrived_ref, bas_ref, out_hbm, out_ref, sem):
+    )(hbm(lax.optimization_barrier((value, after))[0]))
+
+
+def prolong_kernel(here_ref, there_ref, *refs):
+    *bas_refs, out_hbm, out_ref, sem = refs
     cols, comp = out_ref.shape[2:]
-    pair = 2 * bas_ref.shape[2]
+    pair = 2 * bas_refs[0].shape[2]
     pairs = sem.shape[0]
+    head = bas_refs[0].shape[1] // 2
     first = lax.broadcasted_iota(jnp.int32, (cols, pair), 1) < pair // 2
 
     def copy(i):
@@ -184,7 +188,7 @@
 
     for i in range(pairs):
         lanes = slice(i * pair, (i + 1) * pair)
-        re, im = (jnp.where(active[0] == 1, arrived_ref[row, :, lanes], sum_ref[row, :, lanes]) for row in range(2))
+        re, im = (total([ref[row, :, lanes] for ref in (here_ref, there_ref)]).astype(BF) for row in range(2))
         none = jnp.zeros_like(re)
         re0, re1 = jnp.where(first, re, none), jnp.where(first, none, re)
         im0, im1 = jnp.where(first, im, none), jnp.where(first, none, im)
@@ -195,27 +199,28 @@
             ],
             axis=1,
         )
-        bas = bas_ref[:, 2 * i : 2 * i + 2].reshape(2 * pair, comp).astype(BF)
+        part, j = (0, i) if i < head else (1, i - head)
+        bas = bas_refs[part][:, 2 * j : 2 * j + 2].reshape(2 * pair, comp).astype(BF)
         out_ref[:, 2 * i : 2 * i + 2] = dot(left, bas, NN).reshape(2, 2, cols, comp)
         copy(i).start()
     for i in range(pairs):
         copy(i).wait()
 
 
-def prolong(active, lifted, arrived, basis, shape):
-    vecs, comp = basis.shape[2:]
-    cols = lifted.shape[1]
+def prolong(here, there, basis, shape):
+    vecs, comp = basis[0].shape[2:]
+    cols = here.shape[1]
     pairs = shape[1] // 2
     return pl.pallas_call(
         prolong_kernel,
-        in_specs=[scalar()] + [whole()] * 3,
+        in_specs=[whole()] * (2 + len(basis)),
         out_specs=pl.BlockSpec(memory_space=pltpu.HBM),
         out_shape=jax.ShapeDtypeStruct(shape, F32),
         scratch_shapes=[pltpu.VMEM(shape, F32), pltpu.SemaphoreType.DMA((pairs,))],
         compiler_params=pltpu.CompilerParams(vmem_limit_bytes=8 * MIB),
         cost_estimate=pl.CostEstimate(flops=64 * pairs * cols * vecs * comp, bytes_accessed=pairs * cols * comp * 16, transcendentals=0),
         name="prolong",
-    )(active, lifted, arrived, basis)
+    )(here, there, *basis)
 
 
 class Slice:
@@ -235,7 +240,7 @@
     def region_steps(self):
         step = 1
         while step < self.regions:
-            four = step > 1 and 2 * step < self.regions
+            four = 2 * step < self.regions
             yield [step, 2 * step, 3 * step] if four else [step]
             step *= 4 if four else 2
 
@@ -284,27 +289,30 @@
 
     part = project(residual, basis)
     chip_sum = add([part, place.swap(part)])
-    sister = place.swap(lax.optimization_barrier((own, chip_sum))[0])
+    sister = place.swap(lax.optimization_barrier((own, chip_sum[:1, :8, :128]))[0])
     holder = 1
+    head = 2 * (blocks // 3)
+    first = load(basis, 0, head, chip_sum)
     coarse = [chip_sum] + [place.cross(chip_sum, 0, chip=s) for s in place.chip_steps()]
+    coarse, first = lax.optimization_barrier((coarse, first))
 
     start = holder
     active = (core == holder).astype(jnp.int32)
     value = contract(active, coarse, own, sister, weights.reshape(1, count))
-    steps = list(place.region_steps())
+    steps = list(place.region_steps())[::-1]
     for i, step in enumerate(steps):
         terms = [place.swap(value)] + [place.cross(value, holder, region=s) for s in step]
         holder = 1 - holder
         if i < len(steps) - 1:
             value = add(terms, weights if i == 0 else None)
 
+    second = load(basis, head, blocks - head, value)
+    terms, second = lax.optimization_barrier((terms, second))
     active = (core == holder).astype(jnp.int32)
     lifted = expand(active, terms, own, sister, holder == start)
-    in_vmem = load(lax.optimization_barrier((basis, lifted))[0])
-    terms = [place.swap(lifted)] + [place.cross(lifted, holder, chip=s) for s in place.chip_steps()]
-    terms, in_vmem = lax.optimization_barrier((terms, in_vmem))
-    lifted = add(terms)
-    return prolong(active, lifted, place.swap(lifted), in_vmem, residual.shape)
+    terms = [place.cross(lifted, holder, chip=s) for s in place.chip_steps()]
+    here = jnp.where(core == holder, lifted, total(terms).astype(BF))
+    return prolong(here, place.swap(here), (first, second), residual.shape)
 
 
 def solution(mesh):

time: 35.1 us -> 34.5 us (0.983)
  Pallas kernels: 12.2 us -> 13.2 us
  waiting for transfers between devices: 11.3 us -> 10.5 us
  starting transfers between devices: 11.3 us -> 10.6 us
    ppermute x6, starting transfers between devices: 9.05 us -> 7.67 us  [cross(): return lax.ppermute(value, ('region', 'eig'), pairs)]
    ppermute x6, waiting for transfers between devices: 8.84 us -> 7.64 us  [cross(): return lax.ppermute(value, ('region', 'eig'), pairs)]
    pallas_call x2 -> x3, Pallas kernels: 6.2 us -> 7.32 us  [the longest x2 4.81 us: load(): pl.pallas_call(functools.partial(load_kernel, start), in_specs=[pl.BlockS...]
    ppermute x6 -> x5, starting transfers between devices: 2.21 us -> 2.88 us  [swap(): return lax.ppermute(value, 'eig', [(i, i ^ 1) for i in range(self.shares)])]
    ppermute x6 -> x5, waiting for transfers between devices: 2.51 us -> 2.82 us  [swap(): return lax.ppermute(value, 'eig', [(i, i ^ 1) for i in range(self.shares)])]
  transfers between devices with their start and end apart: 12 -> 11, of which waited for: 8 -> 5; matrix products, arithmetic and copies ran while one was open for 0% -> 0% of each run, Pallas kernels for 11% -> 31%
where the time goes in v4:
time: 34.5 us; the launch traced here: 34.4 us
  Pallas kernels  13.2 us (38%)
  starting transfers between devices  10.6 us (31%)
  waiting for transfers between devices  10.5 us (30%)
    ppermute x6, starting transfers between devices, cross(): return lax.ppermute(value, ('region', 'eig'), pairs)  7.67 us
    ppermute x6, waiting for transfers between devices, cross(): return lax.ppermute(value, ('region', 'eig'), pairs)  7.64 us
    pallas_call x1, Pallas kernels, project(): pl.pallas_call(project_kernel, in_specs=[pl.BlockSpec(memory_space=pltpu....  5.81 us
    pallas_call x2, Pallas kernels, load(): pl.pallas_call(functools.partial(load_kernel, start), in_specs=[pl.BlockS...  4.81 us
    ppermute x5, starting transfers between devices, swap(): return lax.ppermute(value, 'eig', [(i, i ^ 1) for i in range(self.shares)])  2.88 us
    ppermute x5, waiting for transfers between devices, swap(): return lax.ppermute(value, 'eig', [(i, i ^ 1) for i in range(self.shares)])  2.82 us
    pallas_call x1, Pallas kernels, prolong(): pl.pallas_call(prolong_kernel, in_specs=[whole()] * (2 + len(basis)), out...  2.52 us
  transfers between devices with their start and end apart: 11, of which 5 were waited for; matrix products, arithmetic and copies ran while one was open for 0% of the time, Pallas kernels for 31%

profile of v4, /device:TPU:0, one launch (start us, length us, event | category | flops | bytes accessed | tf_op | source)
XLA Modules:
  0.0 34.4 jit_solution(11212011333767725971)
XLA Ops:
  0.0 0.5 %collective-permute-start = (bf16[2,1536,256]{2,1,0:T(8,128)(2,1)}, bf16[2,1536,256]{2,1,0:T(8,128)(2,1)S(1)}, u32[]{:S(2)}, u32[]{:S(2)}) collective-permute-start(bf16[2,1536,256]{2,1,0:T(8,128)(2,1)} %bitcast.4), channel_id=1, source_target_pairs={{0,1},{1,0},{2,3},{3,2},{4,5},{5,4},{6,7},{7,6},{8,9},{9,8},{10,11... | collective-permute-start | bytes 4718600 | tf_op jit(solution)/shard_map/ppermute | solution.py:231
  0.5 5.8 %project.1.refs_0_ = bf16[2,32,1536]{2,1,0:T(8,128)(2,1)S(1)} custom-call(f32[2,24,32,768]{3,2,1,0:T(8,128)} %res_hbm.1, f32[2,24,64,768]{3,2,1,0:T(8,128)} %from_hbm.1), custom_call_target="tpu_custom_call" | custom-call | flops 603979776 | bytes 14155776 | tf_op jit(solution)/shard_map/project/pallas_call | solution.py:73
  6.3 0.1 collective-permute-start.1
  6.4 1.4 %collective-permute-done.1.refs_1_ = bf16[2,32,1536]{2,1,0:T(8,128)(2,1)S(1)} collective-permute-done((bf16[2,32,1536]{2,1,0:T(8,128)(2,1)S(1)}, bf16[2,32,1536]{2,1,0:T(8,128)(2,1)S(1)}, u32[]{:S(2)}, u32[]{:S(2)}) %collective-permute-start.1) | collective-permute-done | bytes 196640 | tf_op jit(solution)/shard_map/ppermute | solution.py:231
  7.8 2.7 %collective-permute-start.2 = (bf16[2,32,1536]{2,1,0:T(8,128)(2,1)S(1)}, bf16[2,32,1536]{2,1,0:T(8,128)(2,1)S(1)}, u32[]{:S(2)}, u32[]{:S(2)}) collective-permute-start(bf16[2,32,1536]{2,1,0:T(8,128)(2,1)S(1)} %add.7.refs_0_), channel_id=1, source_target_pairs={{0,3},{1,0},{2,1},{3,2},{4,7},{5,4},{6,5},{7,6},{8,11},{9,8},{10,9... | collective-permute-start | bytes 589832 | tf_op jit(solution)/shard_map/ppermute | solution.py:238
  10.5 0.0 copy-start
  10.5 0.0 copy-start.1
  10.5 2.9 %load.2.refs_0_ = f32[2,16,64,768]{3,2,1,0:T(8,128)S(1)} custom-call(f32[2,24,64,768]{3,2,1,0:T(8,128)} %from_hbm.1), custom_call_target="tpu_custom_call" | custom-call | bytes 6291456 | tf_op jit(solution)/shard_map/load/pallas_call | solution.py:165
  13.4 0.3 collective-permute-done.2.refs_1_
  13.7 0.0 collective-permute-done.sister_ref
  13.7 0.0 copy-done
  13.7 0.0 copy-done.1
  13.7 1.0 %collective-permute-start.4 = (bf16[2,32,512]{2,1,0:T(8,128)(2,1)S(1)}, bf16[2,32,512]{2,1,0:T(8,128)(2,1)S(1)}, u32[]{:S(2)}, u32[]{:S(2)}) collective-permute-start(bf16[2,32,512]{2,1,0:T(8,128)(2,1)S(1)} %contract.1), channel_id=1, source_target_pairs={{0,1},{1,16},{2,3},{3,18},{4,5},{5,20},{6,7},{7,22},{8,9},{9,24},{... | collective-permute-start | bytes 196616 | tf_op jit(solution)/shard_map/ppermute | solution.py:238
  14.7 1.7 %collective-permute-start.3 = (bf16[2,32,512]{2,1,0:T(8,128)(2,1)S(1)}, bf16[2,32,512]{2,1,0:T(8,128)(2,1)S(1)}, u32[]{:S(2)}, u32[]{:S(2)}) collective-permute-start(bf16[2,32,512]{2,1,0:T(8,128)(2,1)S(1)} %contract.1), channel_id=1, source_target_pairs={{0,1},{1,0},{2,3},{3,2},{4,5},{5,4},{6,7},{7,6},{8,9},{9,8},{10,11... | collective-permute-start | bytes 196616 | tf_op jit(solution)/shard_map/ppermute | solution.py:231
  16.5 2.9 %collective-permute-done.4.refs_1_ = bf16[2,32,512]{2,1,0:T(8,128)(2,1)S(1)} collective-permute-done((bf16[2,32,512]{2,1,0:T(8,128)(2,1)S(1)}, bf16[2,32,512]{2,1,0:T(8,128)(2,1)S(1)}, u32[]{:S(2)}, u32[]{:S(2)}) %collective-permute-start.4) | collective-permute-done | bytes 65568 | tf_op jit(solution)/shard_map/ppermute | solution.py:238
  19.4 0.0 collective-permute-done.3.refs_0_
  19.4 1.1 %collective-permute-start.8 = (bf16[2,32,512]{2,1,0:T(8,128)(2,1)S(1)}, bf16[2,32,512]{2,1,0:T(8,128)(2,1)S(1)}, u32[]{:S(2)}, u32[]{:S(2)}) collective-permute-start(bf16[2,32,512]{2,1,0:T(8,128)(2,1)S(1)} %add.8), channel_id=1, source_target_pairs={{0,13},{1,0},{2,15},{3,2},{4,9},{5,4},{6,11},{7,6},{8,5},{9,8},{10... | collective-permute-start | bytes 196616 | tf_op jit(solution)/shard_map/ppermute | solution.py:238
  20.5 0.7 %collective-permute-start.7 = (bf16[2,32,512]{2,1,0:T(8,128)(2,1)S(1)}, bf16[2,32,512]{2,1,0:T(8,128)(2,1)S(1)}, u32[]{:S(2)}, u32[]{:S(2)}) collective-permute-start(bf16[2,32,512]{2,1,0:T(8,128)(2,1)S(1)} %add.8), channel_id=1, source_target_pairs={{0,9},{1,0},{2,11},{3,2},{4,13},{5,4},{6,15},{7,6},{8,1},{9,8},{10... | collective-permute-start | bytes 196616 | tf_op jit(solution)/shard_map/ppermute | solution.py:238
  21.1 0.0 collective-permute-start.6
  21.1 0.5 %collective-permute-start.5 = (bf16[2,32,512]{2,1,0:T(8,128)(2,1)S(1)}, bf16[2,32,512]{2,1,0:T(8,128)(2,1)S(1)}, u32[]{:S(2)}, u32[]{:S(2)}) collective-permute-start(bf16[2,32,512]{2,1,0:T(8,128)(2,1)S(1)} %add.8), channel_id=1, source_target_pairs={{0,1},{1,0},{2,3},{3,2},{4,5},{5,4},{6,7},{7,6},{8,9},{9,8},{10,11... | collective-permute-start | bytes 196616 | tf_op jit(solution)/shard_map/ppermute | solution.py:231
  21.7 1.9 %load.3.refs_1_ = f32[2,8,64,768]{3,2,1,0:T(8,128)S(1)} custom-call(f32[2,24,64,768]{3,2,1,0:T(8,128)} %from_hbm.1), custom_call_target="tpu_custom_call" | custom-call | bytes 3145728 | tf_op jit(solution)/shard_map/load/pallas_call | solution.py:165
  23.6 0.0 collective-permute-done.8.refs_3_
  23.6 0.0 collective-permute-done.7.refs_2_
  23.6 0.0 collective-permute-done.6.refs_1_
  23.6 0.0 collective-permute-done.5.refs_0_
  23.6 2.2 %collective-permute-start.9 = (bf16[2,32,1536]{2,1,0:T(8,128)(2,1)S(1)}, bf16[2,32,1536]{2,1,0:T(8,128)(2,1)S(1)}, u32[]{:S(2)}, u32[]{:S(2)}) collective-permute-start(bf16[2,32,1536]{2,1,0:T(8,128)(2,1)S(1)} %expand.1), channel_id=1, source_target_pairs={{0,1},{1,2},{2,3},{3,0},{4,5},{5,6},{6,7},{7,4},{8,9},{9,10},{10,1... | collective-permute-start | bytes 589832 | tf_op jit(solution)/shard_map/ppermute | solution.py:238
  25.9 4.5 %collective-permute-done.9 = bf16[2,32,1536]{2,1,0:T(8,128)(2,1)S(1)} collective-permute-done((bf16[2,32,1536]{2,1,0:T(8,128)(2,1)S(1)}, bf16[2,32,1536]{2,1,0:T(8,128)(2,1)S(1)}, u32[]{:S(2)}, u32[]{:S(2)}) %collective-permute-start.9) | collective-permute-done | bytes 196640 | tf_op jit(solution)/shard_map/ppermute | solution.py:238
  30.4 0.1 collective-permute-start.10
  30.4 1.4 %collective-permute-done.10.there_ref = bf16[2,32,1536]{2,1,0:T(8,128)(2,1)S(1)} collective-permute-done((bf16[2,32,1536]{2,1,0:T(8,128)(2,1)S(1)}, bf16[2,32,1536]{2,1,0:T(8,128)(2,1)S(1)}, u32[]{:S(2)}, u32[]{:S(2)}) %collective-permute-start.10) | collective-permute-done | bytes 196640 | tf_op jit(solution)/shard_map/ppermute | solution.py:231
  31.9 2.5 %prolong.1 = f32[2,24,32,768]{3,2,1,0:T(8,128)} custom-call(bf16[2,32,1536]{2,1,0:T(8,128)(2,1)S(1)} %broadcast_select_fusion.here_ref, bf16[2,32,1536]{2,1,0:T(8,128)(2,1)S(1)} %collective-permute-done.10.there_ref, f32[2,16,64,768]{3,2,1,0:T(8,128)S(1)} %load.2.refs_0_, f32[2,8,64,768]{3,2,1,0:T(8,128)S(1)} %load.3.refs_1_), custom_call_target="tpu_custom_call" | custom-call | flops 1207959552 | bytes 4718592 | tf_op jit(solution)/shard_map/prolong/pallas_call | solution.py:214
  (5 shorter events, 0.1 us)
Async XLA Ops:
  0.0 13.7 %collective-permute-start = (bf16[2,1536,256]{2,1,0:T(8,128)(2,1)}, bf16[2,1536,256]{2,1,0:T(8,128)(2,1)S(1)}, u32[]{:S(2)}, u32[]{:S(2)}) collective-permute-start(bf16[2,1536,256]{2,1,0:T(8,128)(2,1)} %bitcast.4), channel_id=1, source_target_pairs={{0,1},{1,0},{2,3},{3,2},{4,5},{5,4},{6,7},{7,6},{8,9},{9,8},{10,11... | collective-permute-start | bytes 4718600 | tf_op jit(solution)/shard_map/ppermute | solution.py:231
  6.3 1.5 %collective-permute-start.1 = (bf16[2,32,1536]{2,1,0:T(8,128)(2,1)S(1)}, bf16[2,32,1536]{2,1,0:T(8,128)(2,1)S(1)}, u32[]{:S(2)}, u32[]{:S(2)}) collective-permute-start(bf16[2,32,1536]{2,1,0:T(8,128)(2,1)S(1)} %project.1.refs_0_), channel_id=1, source_target_pairs={{0,1},{1,0},{2,3},{3,2},{4,5},{5,4},{6,7},{7,6},{8,9},{9,8},{10,11... | collective-permute-start | bytes 589832 | tf_op jit(solution)/shard_map/ppermute | solution.py:231
  7.8 5.9 %collective-permute-start.2 = (bf16[2,32,1536]{2,1,0:T(8,128)(2,1)S(1)}, bf16[2,32,1536]{2,1,0:T(8,128)(2,1)S(1)}, u32[]{:S(2)}, u32[]{:S(2)}) collective-permute-start(bf16[2,32,1536]{2,1,0:T(8,128)(2,1)S(1)} %add.7.refs_0_), channel_id=1, source_target_pairs={{0,3},{1,0},{2,1},{3,2},{4,7},{5,4},{6,5},{7,6},{8,11},{9,8},{10,9... | collective-permute-start | bytes 589832 | tf_op jit(solution)/shard_map/ppermute | solution.py:238
  10.5 3.2 %copy-start = (bf16[2,24,64,256]{3,2,1,0:T(8,128)(2,1)S(1)}, bf16[2,24,64,256]{3,2,1,0:T(8,128)(2,1)}, u32[]{:S(2)}) copy-start(bf16[2,24,64,256]{3,2,1,0:T(8,128)(2,1)} %param.6) | copy-start | bytes 4718596
  10.5 3.2 %copy-start.1 = (f32[256]{0:T(256)S(1)}, f32[256]{0:T(256)}, u32[]{:S(2)}) copy-start(f32[256]{0:T(256)} %param.7) | copy-start | bytes 3076
  13.7 5.6 %collective-permute-start.4 = (bf16[2,32,512]{2,1,0:T(8,128)(2,1)S(1)}, bf16[2,32,512]{2,1,0:T(8,128)(2,1)S(1)}, u32[]{:S(2)}, u32[]{:S(2)}) collective-permute-start(bf16[2,32,512]{2,1,0:T(8,128)(2,1)S(1)} %contract.1), channel_id=1, source_target_pairs={{0,1},{1,16},{2,3},{3,18},{4,5},{5,20},{6,7},{7,22},{8,9},{9,24},{... | collective-permute-start | bytes 196616 | tf_op jit(solution)/shard_map/ppermute | solution.py:238
  14.7 4.6 %collective-permute-start.3 = (bf16[2,32,512]{2,1,0:T(8,128)(2,1)S(1)}, bf16[2,32,512]{2,1,0:T(8,128)(2,1)S(1)}, u32[]{:S(2)}, u32[]{:S(2)}) collective-permute-start(bf16[2,32,512]{2,1,0:T(8,128)(2,1)S(1)} %contract.1), channel_id=1, source_target_pairs={{0,1},{1,0},{2,3},{3,2},{4,5},{5,4},{6,7},{7,6},{8,9},{9,8},{10,11... | collective-permute-start | bytes 196616 | tf_op jit(solution)/shard_map/ppermute | solution.py:231
  19.4 4.2 %collective-permute-start.8 = (bf16[2,32,512]{2,1,0:T(8,128)(2,1)S(1)}, bf16[2,32,512]{2,1,0:T(8,128)(2,1)S(1)}, u32[]{:S(2)}, u32[]{:S(2)}) collective-permute-start(bf16[2,32,512]{2,1,0:T(8,128)(2,1)S(1)} %add.8), channel_id=1, source_target_pairs={{0,13},{1,0},{2,15},{3,2},{4,9},{5,4},{6,11},{7,6},{8,5},{9,8},{10... | collective-permute-start | bytes 196616 | tf_op jit(solution)/shard_map/ppermute | solution.py:238
  20.5 3.1 %collective-permute-start.7 = (bf16[2,32,512]{2,1,0:T(8,128)(2,1)S(1)}, bf16[2,32,512]{2,1,0:T(8,128)(2,1)S(1)}, u32[]{:S(2)}, u32[]{:S(2)}) collective-permute-start(bf16[2,32,512]{2,1,0:T(8,128)(2,1)S(1)} %add.8), channel_id=1, source_target_pairs={{0,9},{1,0},{2,11},{3,2},{4,13},{5,4},{6,15},{7,6},{8,1},{9,8},{10... | collective-permute-start | bytes 196616 | tf_op jit(solution)/shard_map/ppermute | solution.py:238
  21.1 2.4 %collective-permute-start.6 = (bf16[2,32,512]{2,1,0:T(8,128)(2,1)S(1)}, bf16[2,32,512]{2,1,0:T(8,128)(2,1)S(1)}, u32[]{:S(2)}, u32[]{:S(2)}) collective-permute-start(bf16[2,32,512]{2,1,0:T(8,128)(2,1)S(1)} %add.8), channel_id=1, source_target_pairs={{0,5},{1,0},{2,7},{3,2},{4,1},{5,4},{6,3},{7,6},{8,13},{9,8},{10,1... | collective-permute-start | bytes 196616 | tf_op jit(solution)/shard_map/ppermute | solution.py:238
  21.1 2.4 %collective-permute-start.5 = (bf16[2,32,512]{2,1,0:T(8,128)(2,1)S(1)}, bf16[2,32,512]{2,1,0:T(8,128)(2,1)S(1)}, u32[]{:S(2)}, u32[]{:S(2)}) collective-permute-start(bf16[2,32,512]{2,1,0:T(8,128)(2,1)S(1)} %add.8), channel_id=1, source_target_pairs={{0,1},{1,0},{2,3},{3,2},{4,5},{5,4},{6,7},{7,6},{8,9},{9,8},{10,11... | collective-permute-start | bytes 196616 | tf_op jit(solution)/shard_map/ppermute | solution.py:231
  23.6 6.7 %collective-permute-start.9 = (bf16[2,32,1536]{2,1,0:T(8,128)(2,1)S(1)}, bf16[2,32,1536]{2,1,0:T(8,128)(2,1)S(1)}, u32[]{:S(2)}, u32[]{:S(2)}) collective-permute-start(bf16[2,32,1536]{2,1,0:T(8,128)(2,1)S(1)} %expand.1), channel_id=1, source_target_pairs={{0,1},{1,2},{2,3},{3,0},{4,5},{5,6},{6,7},{7,4},{8,9},{9,10},{10,1... | collective-permute-start | bytes 589832 | tf_op jit(solution)/shard_map/ppermute | solution.py:238
  30.4 1.5 %collective-permute-start.10 = (bf16[2,32,1536]{2,1,0:T(8,128)(2,1)S(1)}, bf16[2,32,1536]{2,1,0:T(8,128)(2,1)S(1)}, u32[]{:S(2)}, u32[]{:S(2)}) collective-permute-start(bf16[2,32,1536]{2,1,0:T(8,128)(2,1)S(1)} %broadcast_select_fusion.here_ref), channel_id=1, source_target_pairs={{0,1},{1,0},{2,3},{3,2},{4,5},{5,4},{6,7},{7,6},{8,9},{9,8},{10,11... | collective-permute-start | bytes 589832 | tf_op jit(solution)/shard_map/ppermute | solution.py:231

commit v5 on v4

--- a/solution.py
+++ b/solution.py
@@ -121,10 +121,36 @@
     )(active, own, sister, weights, *coarse)
 
 
+def turn_kernel(active, *refs):
+    half = len(refs) // 2
+    depth, count = refs[0].shape[1:]
+
+    @pl.when(active[0] == 1)
+    def _():
+        for from_ref, to_ref in zip(refs[:half], refs[half:]):
+            for part in range(from_ref.shape[0]):
+                for row in range(0, depth, count):
+                    to_ref[part, :, row : row + count] = from_ref[part, row : row + count, :].T
+
+
+def turn(active, arrays, after):
+    arrays = lax.optimization_barrier((arrays, after))[0]
+    shapes = [(a.shape[0], a.shape[2], a.shape[1]) for a in arrays]
+    return pl.pallas_call(
+        turn_kernel,
+        in_specs=[scalar()] + [whole()] * len(arrays),
+        out_specs=[whole()] * len(arrays),
+        out_shape=[pltpu.VMEM(shape, a.dtype) for shape, a in zip(shapes, arrays)],
+        compiler_params=pltpu.CompilerParams(vmem_limit_bytes=4 * MIB),
+        cost_estimate=pl.CostEstimate(flops=0, bytes_accessed=sum(a.size for a in arrays) * 4, transcendentals=0),
+        name="turn",
+    )(active, *arrays)
+
+
 def expand_kernel(own_first, active, own_ref, sister_ref, *refs):
     *wgt_refs, out_ref = refs
     cols = out_ref.shape[1]
-    count = own_ref.shape[2]
+    count = own_ref.shape[1]
 
     @pl.when(active[0] == 1)
     def _():
@@ -132,8 +158,8 @@
         re = im = None
         for i, eig_ref in enumerate((own_ref, sister_ref) if own_first else (sister_ref, own_ref)):
             weighted = whole_wgt[:, :, i * count : (i + 1) * count].reshape(2 * cols, count)
-            by_re = dot(weighted, eig_ref[0], NT)
-            by_im = dot(weighted, eig_ref[1], NT)
+            by_re = dot(weighted, eig_ref[0], NN)
+            by_im = dot(weighted, eig_ref[1], NN)
             re = by_re[:cols] - by_im[cols:] + (0 if re is None else re)
             im = by_re[cols:] + by_im[:cols] + (0 if im is None else im)
         out_ref[0] = re.astype(BF)
@@ -142,7 +168,7 @@
 
 def expand(active, weighted, own, sister, own_first):
     cols = weighted[0].shape[1]
-    depth, count = own.shape[1:]
+    count, depth = own.shape[1:]
     return pl.pallas_call(
         functools.partial(expand_kernel, own_first),
         in_specs=[scalar()] + [whole()] * 2 + [whole()] * len(weighted),
@@ -303,13 +329,17 @@
     for i, step in enumerate(steps):
         terms = [place.swap(value)] + [place.cross(value, holder, region=s) for s in step]
         holder = 1 - holder
+        if i == 0:
+            last = (start + len(steps)) % 2
+            active = (core == last).astype(jnp.int32)
+            turned = turn(active, [own, sister], value)
+            terms, turned = lax.optimization_barrier((terms, turned))
         if i < len(steps) - 1:
             value = add(terms, weights if i == 0 else None)
 
     second = load(basis, head, blocks - head, value)
     terms, second = lax.optimization_barrier((terms, second))
-    active = (core == holder).astype(jnp.int32)
-    lifted = expand(active, terms, own, sister, holder == start)
+    lifted = expand(active, terms, *turned, holder == start)
     terms = [place.cross(lifted, holder, chip=s) for s in place.chip_steps()]
     here = jnp.where(core == holder, lifted, total(terms).astype(BF))
     return prolong(here, place.swap(here), (first, second), residual.shape)

time: 34.5 us -> 34.1 us (0.988)
  starting transfers between devices: 10.6 us -> 10.1 us
    ppermute x6, starting transfers between devices: 7.67 us -> 7.26 us  [cross(): return lax.ppermute(value, ('region', 'eig'), pairs)]
where the time goes in v5:
time: 34.1 us; the launch traced here: 34 us
  Pallas kernels  13.2 us (39%)
  waiting for transfers between devices  10.5 us (31%)
  starting transfers between devices  10.1 us (30%)
    ppermute x6, waiting for transfers between devices, cross(): return lax.ppermute(value, ('region', 'eig'), pairs)  7.64 us
    ppermute x6, starting transfers between devices, cross(): return lax.ppermute(value, ('region', 'eig'), pairs)  7.26 us
    pallas_call x1, Pallas kernels, project(): pl.pallas_call(project_kernel, in_specs=[pl.BlockSpec(memory_space=pltpu....  5.81 us
    pallas_call x2, Pallas kernels, load(): pl.pallas_call(functools.partial(load_kernel, start), in_specs=[pl.BlockS...  4.81 us
    ppermute x5, starting transfers between devices, swap(): return lax.ppermute(value, 'eig', [(i, i ^ 1) for i in range(self.shares)])  2.88 us
    ppermute x5, waiting for transfers between devices, swap(): return lax.ppermute(value, 'eig', [(i, i ^ 1) for i in range(self.shares)])  2.82 us
    pallas_call x1, Pallas kernels, prolong(): pl.pallas_call(prolong_kernel, in_specs=[whole()] * (2 + len(basis)), out...  2.52 us
  transfers between devices with their start and end apart: 11, of which 5 were waited for; matrix products, arithmetic and copies ran while one was open for 0% of the time, Pallas kernels for 31%

profile of v5, /device:TPU:0, one launch (start us, length us, event | category | flops | bytes accessed | tf_op | source)
XLA Modules:
  0.0 34.0 jit_solution(6295772934261558292)
XLA Ops:
  0.0 0.5 %collective-permute-start = (bf16[2,1536,256]{2,1,0:T(8,128)(2,1)}, bf16[2,1536,256]{2,1,0:T(8,128)(2,1)S(1)}, u32[]{:S(2)}, u32[]{:S(2)}) collective-permute-start(bf16[2,1536,256]{2,1,0:T(8,128)(2,1)} %bitcast.4), channel_id=1, source_target_pairs={{0,1},{1,0},{2,3},{3,2},{4,5},{5,4},{6,7},{7,6},{8,9},{9,8},{10,11... | collective-permute-start | bytes 4718600 | tf_op jit(solution)/shard_map/ppermute | solution.py:257
  0.5 5.8 %project.1.refs_0_ = bf16[2,32,1536]{2,1,0:T(8,128)(2,1)S(1)} custom-call(f32[2,24,32,768]{3,2,1,0:T(8,128)} %res_hbm.1, f32[2,24,64,768]{3,2,1,0:T(8,128)} %from_hbm.1), custom_call_target="tpu_custom_call" | custom-call | flops 603979776 | bytes 14155776 | tf_op jit(solution)/shard_map/project/pallas_call | solution.py:73
  6.3 0.1 collective-permute-start.1
  6.4 1.4 %collective-permute-done.1.refs_1_ = bf16[2,32,1536]{2,1,0:T(8,128)(2,1)S(1)} collective-permute-done((bf16[2,32,1536]{2,1,0:T(8,128)(2,1)S(1)}, bf16[2,32,1536]{2,1,0:T(8,128)(2,1)S(1)}, u32[]{:S(2)}, u32[]{:S(2)}) %collective-permute-start.1) | collective-permute-done | bytes 196640 | tf_op jit(solution)/shard_map/ppermute | solution.py:257
  7.8 2.7 %collective-permute-start.2 = (bf16[2,32,1536]{2,1,0:T(8,128)(2,1)S(1)}, bf16[2,32,1536]{2,1,0:T(8,128)(2,1)S(1)}, u32[]{:S(2)}, u32[]{:S(2)}) collective-permute-start(bf16[2,32,1536]{2,1,0:T(8,128)(2,1)S(1)} %add.7.refs_0_), channel_id=1, source_target_pairs={{0,3},{1,0},{2,1},{3,2},{4,7},{5,4},{6,5},{7,6},{8,11},{9,8},{10,9... | collective-permute-start | bytes 589832 | tf_op jit(solution)/shard_map/ppermute | solution.py:264
  10.5 0.0 copy-start
  10.5 0.0 copy-start.1
  10.5 2.9 %load.2.refs_0_ = f32[2,16,64,768]{3,2,1,0:T(8,128)S(1)} custom-call(f32[2,24,64,768]{3,2,1,0:T(8,128)} %from_hbm.1), custom_call_target="tpu_custom_call" | custom-call | bytes 6291456 | tf_op jit(solution)/shard_map/load/pallas_call | solution.py:191
  13.4 0.3 collective-permute-done.2.refs_1_
  13.7 0.0 collective-permute-done.sister_ref.refs_1_
  13.7 0.0 copy-done
  13.7 0.0 copy-done.1
  13.7 1.0 %collective-permute-start.4 = (bf16[2,32,512]{2,1,0:T(8,128)(2,1)S(1)}, bf16[2,32,512]{2,1,0:T(8,128)(2,1)S(1)}, u32[]{:S(2)}, u32[]{:S(2)}) collective-permute-start(bf16[2,32,512]{2,1,0:T(8,128)(2,1)S(1)} %contract.1), channel_id=1, source_target_pairs={{0,1},{1,16},{2,3},{3,18},{4,5},{5,20},{6,7},{7,22},{8,9},{9,24},{... | collective-permute-start | bytes 196616 | tf_op jit(solution)/shard_map/ppermute | solution.py:264
  14.7 1.7 %collective-permute-start.3 = (bf16[2,32,512]{2,1,0:T(8,128)(2,1)S(1)}, bf16[2,32,512]{2,1,0:T(8,128)(2,1)S(1)}, u32[]{:S(2)}, u32[]{:S(2)}) collective-permute-start(bf16[2,32,512]{2,1,0:T(8,128)(2,1)S(1)} %contract.1), channel_id=1, source_target_pairs={{0,1},{1,0},{2,3},{3,2},{4,5},{5,4},{6,7},{7,6},{8,9},{9,8},{10,11... | collective-permute-start | bytes 196616 | tf_op jit(solution)/shard_map/ppermute | solution.py:257
  16.5 2.9 %collective-permute-done.4.refs_1_ = bf16[2,32,512]{2,1,0:T(8,128)(2,1)S(1)} collective-permute-done((bf16[2,32,512]{2,1,0:T(8,128)(2,1)S(1)}, bf16[2,32,512]{2,1,0:T(8,128)(2,1)S(1)}, u32[]{:S(2)}, u32[]{:S(2)}) %collective-permute-start.4) | collective-permute-done | bytes 65568 | tf_op jit(solution)/shard_map/ppermute | solution.py:264
  19.4 0.0 collective-permute-done.3.refs_0_
  19.4 1.1 %collective-permute-start.8 = (bf16[2,32,512]{2,1,0:T(8,128)(2,1)S(1)}, bf16[2,32,512]{2,1,0:T(8,128)(2,1)S(1)}, u32[]{:S(2)}, u32[]{:S(2)}) collective-permute-start(bf16[2,32,512]{2,1,0:T(8,128)(2,1)S(1)} %add.8), channel_id=1, source_target_pairs={{0,13},{1,0},{2,15},{3,2},{4,9},{5,4},{6,11},{7,6},{8,5},{9,8},{10... | collective-permute-start | bytes 196616 | tf_op jit(solution)/shard_map/ppermute | solution.py:264
  20.5 0.7 %collective-permute-start.7 = (bf16[2,32,512]{2,1,0:T(8,128)(2,1)S(1)}, bf16[2,32,512]{2,1,0:T(8,128)(2,1)S(1)}, u32[]{:S(2)}, u32[]{:S(2)}) collective-permute-start(bf16[2,32,512]{2,1,0:T(8,128)(2,1)S(1)} %add.8), channel_id=1, source_target_pairs={{0,9},{1,0},{2,11},{3,2},{4,13},{5,4},{6,15},{7,6},{8,1},{9,8},{10... | collective-permute-start | bytes 196616 | tf_op jit(solution)/shard_map/ppermute | solution.py:264
  21.1 0.0 collective-permute-start.6
  21.1 0.5 %collective-permute-start.5 = (bf16[2,32,512]{2,1,0:T(8,128)(2,1)S(1)}, bf16[2,32,512]{2,1,0:T(8,128)(2,1)S(1)}, u32[]{:S(2)}, u32[]{:S(2)}) collective-permute-start(bf16[2,32,512]{2,1,0:T(8,128)(2,1)S(1)} %add.8), channel_id=1, source_target_pairs={{0,1},{1,0},{2,3},{3,2},{4,5},{5,4},{6,7},{7,6},{8,9},{9,8},{10,11... | collective-permute-start | bytes 196616 | tf_op jit(solution)/shard_map/ppermute | solution.py:257
  21.7 1.9 %load.3.refs_1_ = f32[2,8,64,768]{3,2,1,0:T(8,128)S(1)} custom-call(f32[2,24,64,768]{3,2,1,0:T(8,128)} %from_hbm.1), custom_call_target="tpu_custom_call" | custom-call | bytes 3145728 | tf_op jit(solution)/shard_map/load/pallas_call | solution.py:191
  23.6 0.0 collective-permute-done.8.refs_3_
  23.6 0.0 collective-permute-done.7.refs_2_
  23.6 0.0 collective-permute-done.6.refs_1_
  23.6 0.0 collective-permute-done.5.refs_0_
  23.6 1.8 %collective-permute-start.9 = (bf16[2,32,1536]{2,1,0:T(8,128)(2,1)S(1)}, bf16[2,32,1536]{2,1,0:T(8,128)(2,1)S(1)}, u32[]{:S(2)}, u32[]{:S(2)}) collective-permute-start(bf16[2,32,1536]{2,1,0:T(8,128)(2,1)S(1)} %expand.1), channel_id=1, source_target_pairs={{0,1},{1,2},{2,3},{3,0},{4,5},{5,6},{6,7},{7,4},{8,9},{9,10},{10,1... | collective-permute-start | bytes 589832 | tf_op jit(solution)/shard_map/ppermute | solution.py:264
  25.4 4.5 %collective-permute-done.9 = bf16[2,32,1536]{2,1,0:T(8,128)(2,1)S(1)} collective-permute-done((bf16[2,32,1536]{2,1,0:T(8,128)(2,1)S(1)}, bf16[2,32,1536]{2,1,0:T(8,128)(2,1)S(1)}, u32[]{:S(2)}, u32[]{:S(2)}) %collective-permute-start.9) | collective-permute-done | bytes 196640 | tf_op jit(solution)/shard_map/ppermute | solution.py:264
  29.9 0.1 collective-permute-start.10
  30.0 1.4 %collective-permute-done.10.there_ref = bf16[2,32,1536]{2,1,0:T(8,128)(2,1)S(1)} collective-permute-done((bf16[2,32,1536]{2,1,0:T(8,128)(2,1)S(1)}, bf16[2,32,1536]{2,1,0:T(8,128)(2,1)S(1)}, u32[]{:S(2)}, u32[]{:S(2)}) %collective-permute-start.10) | collective-permute-done | bytes 196640 | tf_op jit(solution)/shard_map/ppermute | solution.py:257
  31.5 2.5 %prolong.1 = f32[2,24,32,768]{3,2,1,0:T(8,128)} custom-call(bf16[2,32,1536]{2,1,0:T(8,128)(2,1)S(1)} %broadcast_select_fusion.here_ref, bf16[2,32,1536]{2,1,0:T(8,128)(2,1)S(1)} %collective-permute-done.10.there_ref, f32[2,16,64,768]{3,2,1,0:T(8,128)S(1)} %load.2.refs_0_, f32[2,8,64,768]{3,2,1,0:T(8,128)S(1)} %load.3.refs_1_), custom_call_target="tpu_custom_call" | custom-call | flops 1207959552 | bytes 4718592 | tf_op jit(solution)/shard_map/prolong/pallas_call | solution.py:240
  (6 shorter events, 0.1 us)
Async XLA Ops:
  0.0 13.7 %collective-permute-start = (bf16[2,1536,256]{2,1,0:T(8,128)(2,1)}, bf16[2,1536,256]{2,1,0:T(8,128)(2,1)S(1)}, u32[]{:S(2)}, u32[]{:S(2)}) collective-permute-start(bf16[2,1536,256]{2,1,0:T(8,128)(2,1)} %bitcast.4), channel_id=1, source_target_pairs={{0,1},{1,0},{2,3},{3,2},{4,5},{5,4},{6,7},{7,6},{8,9},{9,8},{10,11... | collective-permute-start | bytes 4718600 | tf_op jit(solution)/shard_map/ppermute | solution.py:257
  6.3 1.5 %collective-permute-start.1 = (bf16[2,32,1536]{2,1,0:T(8,128)(2,1)S(1)}, bf16[2,32,1536]{2,1,0:T(8,128)(2,1)S(1)}, u32[]{:S(2)}, u32[]{:S(2)}) collective-permute-start(bf16[2,32,1536]{2,1,0:T(8,128)(2,1)S(1)} %project.1.refs_0_), channel_id=1, source_target_pairs={{0,1},{1,0},{2,3},{3,2},{4,5},{5,4},{6,7},{7,6},{8,9},{9,8},{10,11... | collective-permute-start | bytes 589832 | tf_op jit(solution)/shard_map/ppermute | solution.py:257
  7.8 5.9 %collective-permute-start.2 = (bf16[2,32,1536]{2,1,0:T(8,128)(2,1)S(1)}, bf16[2,32,1536]{2,1,0:T(8,128)(2,1)S(1)}, u32[]{:S(2)}, u32[]{:S(2)}) collective-permute-start(bf16[2,32,1536]{2,1,0:T(8,128)(2,1)S(1)} %add.7.refs_0_), channel_id=1, source_target_pairs={{0,3},{1,0},{2,1},{3,2},{4,7},{5,4},{6,5},{7,6},{8,11},{9,8},{10,9... | collective-permute-start | bytes 589832 | tf_op jit(solution)/shard_map/ppermute | solution.py:264
  10.5 3.2 %copy-start = (bf16[2,24,64,256]{3,2,1,0:T(8,128)(2,1)S(1)}, bf16[2,24,64,256]{3,2,1,0:T(8,128)(2,1)}, u32[]{:S(2)}) copy-start(bf16[2,24,64,256]{3,2,1,0:T(8,128)(2,1)} %param.6) | copy-start | bytes 4718596
  10.5 3.2 %copy-start.1 = (f32[256]{0:T(256)S(1)}, f32[256]{0:T(256)}, u32[]{:S(2)}) copy-start(f32[256]{0:T(256)} %param.7) | copy-start | bytes 3076
  13.7 5.6 %collective-permute-start.4 = (bf16[2,32,512]{2,1,0:T(8,128)(2,1)S(1)}, bf16[2,32,512]{2,1,0:T(8,128)(2,1)S(1)}, u32[]{:S(2)}, u32[]{:S(2)}) collective-permute-start(bf16[2,32,512]{2,1,0:T(8,128)(2,1)S(1)} %contract.1), channel_id=1, source_target_pairs={{0,1},{1,16},{2,3},{3,18},{4,5},{5,20},{6,7},{7,22},{8,9},{9,24},{... | collective-permute-start | bytes 196616 | tf_op jit(solution)/shard_map/ppermute | solution.py:264
  14.7 4.6 %collective-permute-start.3 = (bf16[2,32,512]{2,1,0:T(8,128)(2,1)S(1)}, bf16[2,32,512]{2,1,0:T(8,128)(2,1)S(1)}, u32[]{:S(2)}, u32[]{:S(2)}) collective-permute-start(bf16[2,32,512]{2,1,0:T(8,128)(2,1)S(1)} %contract.1), channel_id=1, source_target_pairs={{0,1},{1,0},{2,3},{3,2},{4,5},{5,4},{6,7},{7,6},{8,9},{9,8},{10,11... | collective-permute-start | bytes 196616 | tf_op jit(solution)/shard_map/ppermute | solution.py:257
  19.4 4.2 %collective-permute-start.8 = (bf16[2,32,512]{2,1,0:T(8,128)(2,1)S(1)}, bf16[2,32,512]{2,1,0:T(8,128)(2,1)S(1)}, u32[]{:S(2)}, u32[]{:S(2)}) collective-permute-start(bf16[2,32,512]{2,1,0:T(8,128)(2,1)S(1)} %add.8), channel_id=1, source_target_pairs={{0,13},{1,0},{2,15},{3,2},{4,9},{5,4},{6,11},{7,6},{8,5},{9,8},{10... | collective-permute-start | bytes 196616 | tf_op jit(solution)/shard_map/ppermute | solution.py:264
  20.5 3.1 %collective-permute-start.7 = (bf16[2,32,512]{2,1,0:T(8,128)(2,1)S(1)}, bf16[2,32,512]{2,1,0:T(8,128)(2,1)S(1)}, u32[]{:S(2)}, u32[]{:S(2)}) collective-permute-start(bf16[2,32,512]{2,1,0:T(8,128)(2,1)S(1)} %add.8), channel_id=1, source_target_pairs={{0,9},{1,0},{2,11},{3,2},{4,13},{5,4},{6,15},{7,6},{8,1},{9,8},{10... | collective-permute-start | bytes 196616 | tf_op jit(solution)/shard_map/ppermute | solution.py:264
  21.1 2.4 %collective-permute-start.6 = (bf16[2,32,512]{2,1,0:T(8,128)(2,1)S(1)}, bf16[2,32,512]{2,1,0:T(8,128)(2,1)S(1)}, u32[]{:S(2)}, u32[]{:S(2)}) collective-permute-start(bf16[2,32,512]{2,1,0:T(8,128)(2,1)S(1)} %add.8), channel_id=1, source_target_pairs={{0,5},{1,0},{2,7},{3,2},{4,1},{5,4},{6,3},{7,6},{8,13},{9,8},{10,1... | collective-permute-start | bytes 196616 | tf_op jit(solution)/shard_map/ppermute | solution.py:264
  21.1 2.4 %collective-permute-start.5 = (bf16[2,32,512]{2,1,0:T(8,128)(2,1)S(1)}, bf16[2,32,512]{2,1,0:T(8,128)(2,1)S(1)}, u32[]{:S(2)}, u32[]{:S(2)}) collective-permute-start(bf16[2,32,512]{2,1,0:T(8,128)(2,1)S(1)} %add.8), channel_id=1, source_target_pairs={{0,1},{1,0},{2,3},{3,2},{4,5},{5,4},{6,7},{7,6},{8,9},{9,8},{10,11... | collective-permute-start | bytes 196616 | tf_op jit(solution)/shard_map/ppermute | solution.py:257
  23.6 6.3 %collective-permute-start.9 = (bf16[2,32,1536]{2,1,0:T(8,128)(2,1)S(1)}, bf16[2,32,1536]{2,1,0:T(8,128)(2,1)S(1)}, u32[]{:S(2)}, u32[]{:S(2)}) collective-permute-start(bf16[2,32,1536]{2,1,0:T(8,128)(2,1)S(1)} %expand.1), channel_id=1, source_target_pairs={{0,1},{1,2},{2,3},{3,0},{4,5},{5,6},{6,7},{7,4},{8,9},{9,10},{10,1... | collective-permute-start | bytes 589832 | tf_op jit(solution)/shard_map/ppermute | solution.py:264
  29.9 1.5 %collective-permute-start.10 = (bf16[2,32,1536]{2,1,0:T(8,128)(2,1)S(1)}, bf16[2,32,1536]{2,1,0:T(8,128)(2,1)S(1)}, u32[]{:S(2)}, u32[]{:S(2)}) collective-permute-start(bf16[2,32,1536]{2,1,0:T(8,128)(2,1)S(1)} %broadcast_select_fusion.here_ref), channel_id=1, source_target_pairs={{0,1},{1,0},{2,3},{3,2},{4,5},{5,4},{6,7},{7,6},{8,9},{9,8},{10,11... | collective-permute-start | bytes 589832 | tf_op jit(solution)/shard_map/ppermute | solution.py:257

commit v6 on v5

--- a/solution.py
+++ b/solution.py
@@ -267,7 +267,7 @@
         step = 1
         while step < self.regions:
             four = 2 * step < self.regions
-            yield [step, 2 * step, 3 * step] if four else [step]
+            yield [2 * step, step, 3 * step] if four else [step]
             step *= 4 if four else 2
 
     def chip_steps(self):
@@ -316,10 +316,10 @@
     part = project(residual, basis)
     chip_sum = add([part, place.swap(part)])
     sister = place.swap(lax.optimization_barrier((own, chip_sum[:1, :8, :128]))[0])
-    holder = 1
+    holder = 0
     head = 2 * (blocks // 3)
     first = load(basis, 0, head, chip_sum)
-    coarse = [chip_sum] + [place.cross(chip_sum, 0, chip=s) for s in place.chip_steps()]
+    coarse = [chip_sum] + [place.cross(chip_sum, 1 - holder, chip=s) for s in place.chip_steps()]
     coarse, first = lax.optimization_barrier((coarse, first))
 
     start = holder

time: 34.1 us -> 33.9 us (level)
  starting transfers between devices: 10.1 us -> 7.04 us
  Pallas kernels: 13.2 us -> 15.4 us
  waiting for transfers between devices: 10.5 us -> 11.2 us
    ppermute x6, starting transfers between devices: 7.26 us -> 4.96 us  [cross(): return lax.ppermute(value, ('region', 'eig'), pairs)]
    ppermute x6, waiting for transfers between devices: 7.64 us -> 8.71 us  [cross(): return lax.ppermute(value, ('region', 'eig'), pairs)]
    pallas_call x1, Pallas kernels: 0.01 us -> 0.86 us  [turn(): pl.pallas_call(turn_kernel, in_specs=[scalar()] + [whole()] * len(arrays)...]
    ppermute x5, starting transfers between devices: 2.88 us -> 2.08 us  [swap(): return lax.ppermute(value, 'eig', [(i, i ^ 1) for i in range(self.shares)])]
    pallas_call x1, Pallas kernels: 0.01 us -> 0.67 us  [contract(): pl.pallas_call(contract_kernel, in_specs=[scalar()] + [whole()] * 3 + [wh...]
    pallas_call x1, Pallas kernels: 0.01 us -> 0.66 us  [expand(): pl.pallas_call(functools.partial(expand_kernel, own_first), in_specs=[sca...]
    ppermute x5, waiting for transfers between devices: 2.82 us -> 2.46 us  [swap(): return lax.ppermute(value, 'eig', [(i, i ^ 1) for i in range(self.shares)])]
  transfers between devices with their start and end apart: 11 -> 11, of which waited for: 5 -> 8; matrix products, arithmetic and copies ran while one was open for 0% -> 0% of each run, Pallas kernels for 31% -> 34%
where the time goes in v6:
time: 33.9 us; the launch traced here: 33.7 us
  Pallas kernels  15.4 us (45%)
  waiting for transfers between devices  11.2 us (33%)
  starting transfers between devices  7.04 us (21%)
    ppermute x6, waiting for transfers between devices, cross(): return lax.ppermute(value, ('region', 'eig'), pairs)  8.71 us
    pallas_call x1, Pallas kernels, project(): pl.pallas_call(project_kernel, in_specs=[pl.BlockSpec(memory_space=pltpu....  5.81 us
    ppermute x6, starting transfers between devices, cross(): return lax.ppermute(value, ('region', 'eig'), pairs)  4.96 us
    pallas_call x2, Pallas kernels, load(): pl.pallas_call(functools.partial(load_kernel, start), in_specs=[pl.BlockS...  4.81 us
    pallas_call x1, Pallas kernels, prolong(): pl.pallas_call(prolong_kernel, in_specs=[whole()] * (2 + len(basis)), out...  2.52 us
    ppermute x5, waiting for transfers between devices, swap(): return lax.ppermute(value, 'eig', [(i, i ^ 1) for i in range(self.shares)])  2.46 us
    ppermute x5, starting transfers between devices, swap(): return lax.ppermute(value, 'eig', [(i, i ^ 1) for i in range(self.shares)])  2.08 us
    pallas_call x1, Pallas kernels, turn(): pl.pallas_call(turn_kernel, in_specs=[scalar()] + [whole()] * len(arrays)...  0.86 us
  transfers between devices with their start and end apart: 11, of which 8 were waited for; matrix products, arithmetic and copies ran while one was open for 0% of the time, Pallas kernels for 34%

profile of v6, /device:TPU:0, one launch (start us, length us, event | category | flops | bytes accessed | tf_op | source)
XLA Modules:
  0.0 33.7 jit_solution(8009500781024124662)
XLA Ops:
  0.0 0.5 %collective-permute-start = (bf16[2,1536,256]{2,1,0:T(8,128)(2,1)}, bf16[2,1536,256]{2,1,0:T(8,128)(2,1)S(1)}, u32[]{:S(2)}, u32[]{:S(2)}) collective-permute-start(bf16[2,1536,256]{2,1,0:T(8,128)(2,1)} %bitcast.4), channel_id=1, source_target_pairs={{0,1},{1,0},{2,3},{3,2},{4,5},{5,4},{6,7},{7,6},{8,9},{9,8},{10,11... | collective-permute-start | bytes 4718600 | tf_op jit(solution)/shard_map/ppermute | solution.py:257
  0.5 5.8 %project.1.refs_0_ = bf16[2,32,1536]{2,1,0:T(8,128)(2,1)S(1)} custom-call(f32[2,24,32,768]{3,2,1,0:T(8,128)} %res_hbm.1, f32[2,24,64,768]{3,2,1,0:T(8,128)} %from_hbm.1), custom_call_target="tpu_custom_call" | custom-call | flops 603979776 | bytes 14155776 | tf_op jit(solution)/shard_map/project/pallas_call | solution.py:73
  6.3 0.1 collective-permute-start.1
  6.4 1.4 %collective-permute-done.1.refs_1_ = bf16[2,32,1536]{2,1,0:T(8,128)(2,1)S(1)} collective-permute-done((bf16[2,32,1536]{2,1,0:T(8,128)(2,1)S(1)}, bf16[2,32,1536]{2,1,0:T(8,128)(2,1)S(1)}, u32[]{:S(2)}, u32[]{:S(2)}) %collective-permute-start.1) | collective-permute-done | bytes 196640 | tf_op jit(solution)/shard_map/ppermute | solution.py:257
  7.8 0.2 collective-permute-start.2
  8.0 0.0 copy-start
  8.0 0.0 copy-start.1
  8.0 2.9 %load.2.refs_0_ = f32[2,16,64,768]{3,2,1,0:T(8,128)S(1)} custom-call(f32[2,24,64,768]{3,2,1,0:T(8,128)} %from_hbm.1), custom_call_target="tpu_custom_call" | custom-call | bytes 6291456 | tf_op jit(solution)/shard_map/load/pallas_call | solution.py:191
  10.9 2.9 %collective-permute-done.2.refs_1_ = bf16[2,32,1536]{2,1,0:T(8,128)(2,1)S(1)} collective-permute-done((bf16[2,32,1536]{2,1,0:T(8,128)(2,1)S(1)}, bf16[2,32,1536]{2,1,0:T(8,128)(2,1)S(1)}, u32[]{:S(2)}, u32[]{:S(2)}) %collective-permute-start.2) | collective-permute-done | bytes 196640 | tf_op jit(solution)/shard_map/ppermute | solution.py:264
  13.9 0.0 collective-permute-done.sister_ref.refs_1_
  13.9 0.0 copy-done
  13.9 0.0 copy-done.1
  13.9 0.7 %contract.1 = bf16[2,32,512]{2,1,0:T(8,128)(2,1)S(1)} custom-call(s32[1]{0:T(128)} %bitcast.active, bf16[2,1536,256]{2,1,0:T(8,128)(2,1)S(1)} %bitcast.5, bf16[2,1536,256]{2,1,0:T(8,128)(2,1)S(1)} %collective-permute-done.sister_ref.refs_1_, f32[1,256]{1,0:T(1,128)S(1)} %bitcast.7, bf16[2,32,1536]{2,1,0:T(8,128)(2,1)S(1)} %add.7.refs_0_, ...), custom_call_target="tpu_custom_call" | custom-call | flops 201326592 | bytes 3145728 | tf_op jit(solution)/shard_map/contract/pallas_call | solution.py:113
  14.6 1.5 %collective-permute-start.4 = (bf16[2,32,512]{2,1,0:T(8,128)(2,1)S(1)}, bf16[2,32,512]{2,1,0:T(8,128)(2,1)S(1)}, u32[]{:S(2)}, u32[]{:S(2)}) collective-permute-start(bf16[2,32,512]{2,1,0:T(8,128)(2,1)S(1)} %contract.1), channel_id=1, source_target_pairs={{0,17},{1,0},{2,19},{3,2},{4,21},{5,4},{6,23},{7,6},{8,25},{9,8},{... | collective-permute-start | bytes 196616 | tf_op jit(solution)/shard_map/ppermute | solution.py:264
  16.1 0.0 collective-permute-start.3
  16.1 0.9 %turn.1 = (bf16[2,256,1536]{2,1,0:T(8,128)(2,1)S(1)}, bf16[2,256,1536]{2,1,0:T(8,128)(2,1)S(1)}) custom-call(s32[1]{0:T(128)} %bitcast.active, bf16[2,1536,256]{2,1,0:T(8,128)(2,1)S(1)} %bitcast.6, bf16[2,1536,256]{2,1,0:T(8,128)(2,1)S(1)} %collective-permute-done.sister_ref.refs_1_), custom_call_target="tpu_custom_call" | custom-call | bytes 6291456 | tf_op jit(solution)/shard_map/turn/pallas_call | solution.py:139
  16.9 1.0 %collective-permute-done.4.refs_1_ = bf16[2,32,512]{2,1,0:T(8,128)(2,1)S(1)} collective-permute-done((bf16[2,32,512]{2,1,0:T(8,128)(2,1)S(1)}, bf16[2,32,512]{2,1,0:T(8,128)(2,1)S(1)}, u32[]{:S(2)}, u32[]{:S(2)}) %collective-permute-start.4) | collective-permute-done | bytes 65568 | tf_op jit(solution)/shard_map/ppermute | solution.py:264
  18.0 0.0 collective-permute-done.3.refs_0_
  18.0 1.6 %collective-permute-start.8 = (bf16[2,32,512]{2,1,0:T(8,128)(2,1)S(1)}, bf16[2,32,512]{2,1,0:T(8,128)(2,1)S(1)}, u32[]{:S(2)}, u32[]{:S(2)}) collective-permute-start(bf16[2,32,512]{2,1,0:T(8,128)(2,1)S(1)} %add.8), channel_id=1, source_target_pairs={{0,1},{1,12},{2,3},{3,14},{4,5},{5,8},{6,7},{7,10},{8,9},{9,4},{10... | collective-permute-start | bytes 196616 | tf_op jit(solution)/shard_map/ppermute | solution.py:264
  19.6 1.5 %collective-permute-start.7 = (bf16[2,32,512]{2,1,0:T(8,128)(2,1)S(1)}, bf16[2,32,512]{2,1,0:T(8,128)(2,1)S(1)}, u32[]{:S(2)}, u32[]{:S(2)}) collective-permute-start(bf16[2,32,512]{2,1,0:T(8,128)(2,1)S(1)} %add.8), channel_id=1, source_target_pairs={{0,1},{1,4},{2,3},{3,6},{4,5},{5,0},{6,7},{7,2},{8,9},{9,12},{10,1... | collective-permute-start | bytes 196616 | tf_op jit(solution)/shard_map/ppermute | solution.py:264
  21.1 0.1 collective-permute-start.6
  21.2 0.2 collective-permute-start.5
  21.3 1.9 %load.3.refs_1_ = f32[2,8,64,768]{3,2,1,0:T(8,128)S(1)} custom-call(f32[2,24,64,768]{3,2,1,0:T(8,128)} %from_hbm.1), custom_call_target="tpu_custom_call" | custom-call | bytes 3145728 | tf_op jit(solution)/shard_map/load/pallas_call | solution.py:191
  23.3 0.5 %collective-permute-done.8.refs_3_ = bf16[2,32,512]{2,1,0:T(8,128)(2,1)S(1)} collective-permute-done((bf16[2,32,512]{2,1,0:T(8,128)(2,1)S(1)}, bf16[2,32,512]{2,1,0:T(8,128)(2,1)S(1)}, u32[]{:S(2)}, u32[]{:S(2)}) %collective-permute-start.8) | collective-permute-done | bytes 65568 | tf_op jit(solution)/shard_map/ppermute | solution.py:264
  23.8 0.2 collective-permute-done.7.refs_2_
  24.0 0.8 %collective-permute-done.6.refs_1_ = bf16[2,32,512]{2,1,0:T(8,128)(2,1)S(1)} collective-permute-done((bf16[2,32,512]{2,1,0:T(8,128)(2,1)S(1)}, bf16[2,32,512]{2,1,0:T(8,128)(2,1)S(1)}, u32[]{:S(2)}, u32[]{:S(2)}) %collective-permute-start.6) | collective-permute-done | bytes 65568 | tf_op jit(solution)/shard_map/ppermute | solution.py:264
  24.8 0.0 collective-permute-done.5.refs_0_
  24.8 0.7 %expand.1 = bf16[2,32,1536]{2,1,0:T(8,128)(2,1)S(1)} custom-call(s32[1]{0:T(128)} %bitcast.active, bf16[2,256,1536]{2,1,0:T(8,128)(2,1)S(1)} %get-tuple-element.30.own_ref, bf16[2,256,1536]{2,1,0:T(8,128)(2,1)S(1)} %get-tuple-element.31.sister_ref, bf16[2,32,512]{2,1,0:T(8,128)(2,1)S(1)} %collective-permute-done.5.refs_0_, ...), custom_call_target="tpu_custom_call" | custom-call | flops 201326592 | bytes 3145728 | tf_op jit(solution)/shard_map/expand/pallas_call | solution.py:172
  25.5 0.1 collective-permute-start.9
  25.6 3.2 %collective-permute-done.9 = bf16[2,32,1536]{2,1,0:T(8,128)(2,1)S(1)} collective-permute-done((bf16[2,32,1536]{2,1,0:T(8,128)(2,1)S(1)}, bf16[2,32,1536]{2,1,0:T(8,128)(2,1)S(1)}, u32[]{:S(2)}, u32[]{:S(2)}) %collective-permute-start.9) | collective-permute-done | bytes 196640 | tf_op jit(solution)/shard_map/ppermute | solution.py:264
  28.8 1.4 %collective-permute-start.10 = (bf16[2,32,1536]{2,1,0:T(8,128)(2,1)S(1)}, bf16[2,32,1536]{2,1,0:T(8,128)(2,1)S(1)}, u32[]{:S(2)}, u32[]{:S(2)}) collective-permute-start(bf16[2,32,1536]{2,1,0:T(8,128)(2,1)S(1)} %broadcast_select_fusion.here_ref), channel_id=1, source_target_pairs={{0,1},{1,0},{2,3},{3,2},{4,5},{5,4},{6,7},{7,6},{8,9},{9,8},{10,11... | collective-permute-start | bytes 589832 | tf_op jit(solution)/shard_map/ppermute | solution.py:257
  30.1 1.1 %collective-permute-done.10.there_ref = bf16[2,32,1536]{2,1,0:T(8,128)(2,1)S(1)} collective-permute-done((bf16[2,32,1536]{2,1,0:T(8,128)(2,1)S(1)}, bf16[2,32,1536]{2,1,0:T(8,128)(2,1)S(1)}, u32[]{:S(2)}, u32[]{:S(2)}) %collective-permute-start.10) | collective-permute-done | bytes 196640 | tf_op jit(solution)/shard_map/ppermute | solution.py:257
  31.2 2.5 %prolong.1 = f32[2,24,32,768]{3,2,1,0:T(8,128)} custom-call(bf16[2,32,1536]{2,1,0:T(8,128)(2,1)S(1)} %broadcast_select_fusion.here_ref, bf16[2,32,1536]{2,1,0:T(8,128)(2,1)S(1)} %collective-permute-done.10.there_ref, f32[2,16,64,768]{3,2,1,0:T(8,128)S(1)} %load.2.refs_0_, f32[2,8,64,768]{3,2,1,0:T(8,128)S(1)} %load.3.refs_1_), custom_call_target="tpu_custom_call" | custom-call | flops 1207959552 | bytes 4718592 | tf_op jit(solution)/shard_map/prolong/pallas_call | solution.py:240
  (3 shorter events, 0.1 us)
Async XLA Ops:
  0.0 13.9 %collective-permute-start = (bf16[2,1536,256]{2,1,0:T(8,128)(2,1)}, bf16[2,1536,256]{2,1,0:T(8,128)(2,1)S(1)}, u32[]{:S(2)}, u32[]{:S(2)}) collective-permute-start(bf16[2,1536,256]{2,1,0:T(8,128)(2,1)} %bitcast.4), channel_id=1, source_target_pairs={{0,1},{1,0},{2,3},{3,2},{4,5},{5,4},{6,7},{7,6},{8,9},{9,8},{10,11... | collective-permute-start | bytes 4718600 | tf_op jit(solution)/shard_map/ppermute | solution.py:257
  6.3 1.5 %collective-permute-start.1 = (bf16[2,32,1536]{2,1,0:T(8,128)(2,1)S(1)}, bf16[2,32,1536]{2,1,0:T(8,128)(2,1)S(1)}, u32[]{:S(2)}, u32[]{:S(2)}) collective-permute-start(bf16[2,32,1536]{2,1,0:T(8,128)(2,1)S(1)} %project.1.refs_0_), channel_id=1, source_target_pairs={{0,1},{1,0},{2,3},{3,2},{4,5},{5,4},{6,7},{7,6},{8,9},{9,8},{10,11... | collective-permute-start | bytes 589832 | tf_op jit(solution)/shard_map/ppermute | solution.py:257
  7.8 6.0 %collective-permute-start.2 = (bf16[2,32,1536]{2,1,0:T(8,128)(2,1)S(1)}, bf16[2,32,1536]{2,1,0:T(8,128)(2,1)S(1)}, u32[]{:S(2)}, u32[]{:S(2)}) collective-permute-start(bf16[2,32,1536]{2,1,0:T(8,128)(2,1)S(1)} %add.7.refs_0_), channel_id=1, source_target_pairs={{0,1},{1,2},{2,3},{3,0},{4,5},{5,6},{6,7},{7,4},{8,9},{9,10},{10,1... | collective-permute-start | bytes 589832 | tf_op jit(solution)/shard_map/ppermute | solution.py:264
  8.0 5.8 %copy-start = (bf16[2,24,64,256]{3,2,1,0:T(8,128)(2,1)S(1)}, bf16[2,24,64,256]{3,2,1,0:T(8,128)(2,1)}, u32[]{:S(2)}) copy-start(bf16[2,24,64,256]{3,2,1,0:T(8,128)(2,1)} %param.6) | copy-start | bytes 4718596
  8.0 5.8 %copy-start.1 = (f32[256]{0:T(256)S(1)}, f32[256]{0:T(256)}, u32[]{:S(2)}) copy-start(f32[256]{0:T(256)} %param.7) | copy-start | bytes 3076
  14.6 3.4 %collective-permute-start.4 = (bf16[2,32,512]{2,1,0:T(8,128)(2,1)S(1)}, bf16[2,32,512]{2,1,0:T(8,128)(2,1)S(1)}, u32[]{:S(2)}, u32[]{:S(2)}) collective-permute-start(bf16[2,32,512]{2,1,0:T(8,128)(2,1)S(1)} %contract.1), channel_id=1, source_target_pairs={{0,17},{1,0},{2,19},{3,2},{4,21},{5,4},{6,23},{7,6},{8,25},{9,8},{... | collective-permute-start | bytes 196616 | tf_op jit(solution)/shard_map/ppermute | solution.py:264
  16.1 1.9 %collective-permute-start.3 = (bf16[2,32,512]{2,1,0:T(8,128)(2,1)S(1)}, bf16[2,32,512]{2,1,0:T(8,128)(2,1)S(1)}, u32[]{:S(2)}, u32[]{:S(2)}) collective-permute-start(bf16[2,32,512]{2,1,0:T(8,128)(2,1)S(1)} %contract.1), channel_id=1, source_target_pairs={{0,1},{1,0},{2,3},{3,2},{4,5},{5,4},{6,7},{7,6},{8,9},{9,8},{10,11... | collective-permute-start | bytes 196616 | tf_op jit(solution)/shard_map/ppermute | solution.py:257
  18.0 5.8 %collective-permute-start.8 = (bf16[2,32,512]{2,1,0:T(8,128)(2,1)S(1)}, bf16[2,32,512]{2,1,0:T(8,128)(2,1)S(1)}, u32[]{:S(2)}, u32[]{:S(2)}) collective-permute-start(bf16[2,32,512]{2,1,0:T(8,128)(2,1)S(1)} %add.8), channel_id=1, source_target_pairs={{0,1},{1,12},{2,3},{3,14},{4,5},{5,8},{6,7},{7,10},{8,9},{9,4},{10... | collective-permute-start | bytes 196616 | tf_op jit(solution)/shard_map/ppermute | solution.py:264
  19.6 4.4 %collective-permute-start.7 = (bf16[2,32,512]{2,1,0:T(8,128)(2,1)S(1)}, bf16[2,32,512]{2,1,0:T(8,128)(2,1)S(1)}, u32[]{:S(2)}, u32[]{:S(2)}) collective-permute-start(bf16[2,32,512]{2,1,0:T(8,128)(2,1)S(1)} %add.8), channel_id=1, source_target_pairs={{0,1},{1,4},{2,3},{3,6},{4,5},{5,0},{6,7},{7,2},{8,9},{9,12},{10,1... | collective-permute-start | bytes 196616 | tf_op jit(solution)/shard_map/ppermute | solution.py:264
  21.1 3.7 %collective-permute-start.6 = (bf16[2,32,512]{2,1,0:T(8,128)(2,1)S(1)}, bf16[2,32,512]{2,1,0:T(8,128)(2,1)S(1)}, u32[]{:S(2)}, u32[]{:S(2)}) collective-permute-start(bf16[2,32,512]{2,1,0:T(8,128)(2,1)S(1)} %add.8), channel_id=1, source_target_pairs={{0,1},{1,8},{2,3},{3,10},{4,5},{5,12},{6,7},{7,14},{8,9},{9,0},{10... | collective-permute-start | bytes 196616 | tf_op jit(solution)/shard_map/ppermute | solution.py:264
  21.2 3.6 %collective-permute-start.5 = (bf16[2,32,512]{2,1,0:T(8,128)(2,1)S(1)}, bf16[2,32,512]{2,1,0:T(8,128)(2,1)S(1)}, u32[]{:S(2)}, u32[]{:S(2)}) collective-permute-start(bf16[2,32,512]{2,1,0:T(8,128)(2,1)S(1)} %add.8), channel_id=1, source_target_pairs={{0,1},{1,0},{2,3},{3,2},{4,5},{5,4},{6,7},{7,6},{8,9},{9,8},{10,11... | collective-permute-start | bytes 196616 | tf_op jit(solution)/shard_map/ppermute | solution.py:257
  25.5 3.2 %collective-permute-start.9 = (bf16[2,32,1536]{2,1,0:T(8,128)(2,1)S(1)}, bf16[2,32,1536]{2,1,0:T(8,128)(2,1)S(1)}, u32[]{:S(2)}, u32[]{:S(2)}) collective-permute-start(bf16[2,32,1536]{2,1,0:T(8,128)(2,1)S(1)} %expand.1), channel_id=1, source_target_pairs={{0,3},{1,0},{2,1},{3,2},{4,7},{5,4},{6,5},{7,6},{8,11},{9,8},{10,9... | collective-permute-start | bytes 589832 | tf_op jit(solution)/shard_map/ppermute | solution.py:264
  28.8 2.4 %collective-permute-start.10 = (bf16[2,32,1536]{2,1,0:T(8,128)(2,1)S(1)}, bf16[2,32,1536]{2,1,0:T(8,128)(2,1)S(1)}, u32[]{:S(2)}, u32[]{:S(2)}) collective-permute-start(bf16[2,32,1536]{2,1,0:T(8,128)(2,1)S(1)} %broadcast_select_fusion.here_ref), channel_id=1, source_target_pairs={{0,1},{1,0},{2,3},{3,2},{4,5},{5,4},{6,7},{7,6},{8,9},{9,8},{10,11... | collective-permute-start | bytes 589832 | tf_op jit(solution)/shard_map/ppermute | solution.py:257

commit v7 on v6

--- a/solution.py
+++ b/solution.py
@@ -315,7 +315,7 @@
 
     part = project(residual, basis)
     chip_sum = add([part, place.swap(part)])
-    sister = place.swap(lax.optimization_barrier((own, chip_sum[:1, :8, :128]))[0])
+    sister = place.swap(own)
     holder = 0
     head = 2 * (blocks // 3)
     first = load(basis, 0, head, chip_sum)
@@ -334,8 +334,9 @@
             active = (core == last).astype(jnp.int32)
             turned = turn(active, [own, sister], value)
             terms, turned = lax.optimization_barrier((terms, turned))
-        if i < len(steps) - 1:
+        if i == 0 or i < len(steps) - 1:
             value = add(terms, weights if i == 0 else None)
+            terms = [value]
 
     second = load(basis, head, blocks - head, value)
     terms, second = lax.optimization_barrier((terms, second))

time: 33.9 us -> 33.9 us (level)
  no operation moved by 1% of the time
where the time goes in v7:
time: 33.9 us; the launch traced here: 33.7 us
  Pallas kernels  15.4 us (45%)
  waiting for transfers between devices  11.2 us (33%)
  starting transfers between devices  7.04 us (21%)
    ppermute x6, waiting for transfers between devices, cross(): return lax.ppermute(value, ('region', 'eig'), pairs)  8.71 us
    pallas_call x1, Pallas kernels, project(): pl.pallas_call(project_kernel, in_specs=[pl.BlockSpec(memory_space=pltpu....  5.81 us
    ppermute x6, starting transfers between devices, cross(): return lax.ppermute(value, ('region', 'eig'), pairs)  4.96 us
    pallas_call x2, Pallas kernels, load(): pl.pallas_call(functools.partial(load_kernel, start), in_specs=[pl.BlockS...  4.81 us
    pallas_call x1, Pallas kernels, prolong(): pl.pallas_call(prolong_kernel, in_specs=[whole()] * (2 + len(basis)), out...  2.52 us
    ppermute x5, waiting for transfers between devices, swap(): return lax.ppermute(value, 'eig', [(i, i ^ 1) for i in range(self.shares)])  2.46 us
    ppermute x5, starting transfers between devices, swap(): return lax.ppermute(value, 'eig', [(i, i ^ 1) for i in range(self.shares)])  2.08 us
    pallas_call x1, Pallas kernels, turn(): pl.pallas_call(turn_kernel, in_specs=[scalar()] + [whole()] * len(arrays)...  0.86 us
  transfers between devices with their start and end apart: 11, of which 8 were waited for; matrix products, arithmetic and copies ran while one was open for 0% of the time, Pallas kernels for 34%

profile of v7, /device:TPU:0, one launch (start us, length us, event | category | flops | bytes accessed | tf_op | source)
XLA Modules:
  0.0 33.7 jit_solution(8009500781024124662)
XLA Ops:
  0.0 0.5 %collective-permute-start = (bf16[2,1536,256]{2,1,0:T(8,128)(2,1)}, bf16[2,1536,256]{2,1,0:T(8,128)(2,1)S(1)}, u32[]{:S(2)}, u32[]{:S(2)}) collective-permute-start(bf16[2,1536,256]{2,1,0:T(8,128)(2,1)} %bitcast.4), channel_id=1, source_target_pairs={{0,1},{1,0},{2,3},{3,2},{4,5},{5,4},{6,7},{7,6},{8,9},{9,8},{10,11... | collective-permute-start | bytes 4718600 | tf_op jit(solution)/shard_map/ppermute | solution.py:257
  0.5 5.8 %project.1.refs_0_ = bf16[2,32,1536]{2,1,0:T(8,128)(2,1)S(1)} custom-call(f32[2,24,32,768]{3,2,1,0:T(8,128)} %res_hbm.1, f32[2,24,64,768]{3,2,1,0:T(8,128)} %from_hbm.1), custom_call_target="tpu_custom_call" | custom-call | flops 603979776 | bytes 14155776 | tf_op jit(solution)/shard_map/project/pallas_call | solution.py:73
  6.3 0.1 collective-permute-start.1
  6.4 1.4 %collective-permute-done.1.refs_1_ = bf16[2,32,1536]{2,1,0:T(8,128)(2,1)S(1)} collective-permute-done((bf16[2,32,1536]{2,1,0:T(8,128)(2,1)S(1)}, bf16[2,32,1536]{2,1,0:T(8,128)(2,1)S(1)}, u32[]{:S(2)}, u32[]{:S(2)}) %collective-permute-start.1) | collective-permute-done | bytes 196640 | tf_op jit(solution)/shard_map/ppermute | solution.py:257
  7.8 0.2 collective-permute-start.2
  8.0 0.0 copy-start
  8.0 0.0 copy-start.1
  8.0 2.9 %load.2.refs_0_ = f32[2,16,64,768]{3,2,1,0:T(8,128)S(1)} custom-call(f32[2,24,64,768]{3,2,1,0:T(8,128)} %from_hbm.1), custom_call_target="tpu_custom_call" | custom-call | bytes 6291456 | tf_op jit(solution)/shard_map/load/pallas_call | solution.py:191
  10.9 2.9 %collective-permute-done.2.refs_1_ = bf16[2,32,1536]{2,1,0:T(8,128)(2,1)S(1)} collective-permute-done((bf16[2,32,1536]{2,1,0:T(8,128)(2,1)S(1)}, bf16[2,32,1536]{2,1,0:T(8,128)(2,1)S(1)}, u32[]{:S(2)}, u32[]{:S(2)}) %collective-permute-start.2) | collective-permute-done | bytes 196640 | tf_op jit(solution)/shard_map/ppermute | solution.py:264
  13.9 0.0 collective-permute-done.sister_ref.refs_1_
  13.9 0.0 copy-done
  13.9 0.0 copy-done.1
  13.9 0.7 %contract.1 = bf16[2,32,512]{2,1,0:T(8,128)(2,1)S(1)} custom-call(s32[1]{0:T(128)} %bitcast.active, bf16[2,1536,256]{2,1,0:T(8,128)(2,1)S(1)} %bitcast.5, bf16[2,1536,256]{2,1,0:T(8,128)(2,1)S(1)} %collective-permute-done.sister_ref.refs_1_, f32[1,256]{1,0:T(1,128)S(1)} %bitcast.7, bf16[2,32,1536]{2,1,0:T(8,128)(2,1)S(1)} %add.7.refs_0_, ...), custom_call_target="tpu_custom_call" | custom-call | flops 201326592 | bytes 3145728 | tf_op jit(solution)/shard_map/contract/pallas_call | solution.py:113
  14.6 1.5 %collective-permute-start.4 = (bf16[2,32,512]{2,1,0:T(8,128)(2,1)S(1)}, bf16[2,32,512]{2,1,0:T(8,128)(2,1)S(1)}, u32[]{:S(2)}, u32[]{:S(2)}) collective-permute-start(bf16[2,32,512]{2,1,0:T(8,128)(2,1)S(1)} %contract.1), channel_id=1, source_target_pairs={{0,17},{1,0},{2,19},{3,2},{4,21},{5,4},{6,23},{7,6},{8,25},{9,8},{... | collective-permute-start | bytes 196616 | tf_op jit(solution)/shard_map/ppermute | solution.py:264
  16.1 0.0 collective-permute-start.3
  16.1 0.9 %turn.1 = (bf16[2,256,1536]{2,1,0:T(8,128)(2,1)S(1)}, bf16[2,256,1536]{2,1,0:T(8,128)(2,1)S(1)}) custom-call(s32[1]{0:T(128)} %bitcast.active, bf16[2,1536,256]{2,1,0:T(8,128)(2,1)S(1)} %bitcast.6, bf16[2,1536,256]{2,1,0:T(8,128)(2,1)S(1)} %collective-permute-done.sister_ref.refs_1_), custom_call_target="tpu_custom_call" | custom-call | bytes 6291456 | tf_op jit(solution)/shard_map/turn/pallas_call | solution.py:139
  16.9 1.0 %collective-permute-done.4.refs_1_ = bf16[2,32,512]{2,1,0:T(8,128)(2,1)S(1)} collective-permute-done((bf16[2,32,512]{2,1,0:T(8,128)(2,1)S(1)}, bf16[2,32,512]{2,1,0:T(8,128)(2,1)S(1)}, u32[]{:S(2)}, u32[]{:S(2)}) %collective-permute-start.4) | collective-permute-done | bytes 65568 | tf_op jit(solution)/shard_map/ppermute | solution.py:264
  18.0 0.0 collective-permute-done.3.refs_0_
  18.0 1.6 %collective-permute-start.8 = (bf16[2,32,512]{2,1,0:T(8,128)(2,1)S(1)}, bf16[2,32,512]{2,1,0:T(8,128)(2,1)S(1)}, u32[]{:S(2)}, u32[]{:S(2)}) collective-permute-start(bf16[2,32,512]{2,1,0:T(8,128)(2,1)S(1)} %add.8), channel_id=1, source_target_pairs={{0,1},{1,12},{2,3},{3,14},{4,5},{5,8},{6,7},{7,10},{8,9},{9,4},{10... | collective-permute-start | bytes 196616 | tf_op jit(solution)/shard_map/ppermute | solution.py:264
  19.6 1.5 %collective-permute-start.7 = (bf16[2,32,512]{2,1,0:T(8,128)(2,1)S(1)}, bf16[2,32,512]{2,1,0:T(8,128)(2,1)S(1)}, u32[]{:S(2)}, u32[]{:S(2)}) collective-permute-start(bf16[2,32,512]{2,1,0:T(8,128)(2,1)S(1)} %add.8), channel_id=1, source_target_pairs={{0,1},{1,4},{2,3},{3,6},{4,5},{5,0},{6,7},{7,2},{8,9},{9,12},{10,1... | collective-permute-start | bytes 196616 | tf_op jit(solution)/shard_map/ppermute | solution.py:264
  21.1 0.1 collective-permute-start.6
  21.2 0.2 collective-permute-start.5
  21.3 1.9 %load.3.refs_1_ = f32[2,8,64,768]{3,2,1,0:T(8,128)S(1)} custom-call(f32[2,24,64,768]{3,2,1,0:T(8,128)} %from_hbm.1), custom_call_target="tpu_custom_call" | custom-call | bytes 3145728 | tf_op jit(solution)/shard_map/load/pallas_call | solution.py:191
  23.3 0.5 %collective-permute-done.8.refs_3_ = bf16[2,32,512]{2,1,0:T(8,128)(2,1)S(1)} collective-permute-done((bf16[2,32,512]{2,1,0:T(8,128)(2,1)S(1)}, bf16[2,32,512]{2,1,0:T(8,128)(2,1)S(1)}, u32[]{:S(2)}, u32[]{:S(2)}) %collective-permute-start.8) | collective-permute-done | bytes 65568 | tf_op jit(solution)/shard_map/ppermute | solution.py:264
  23.8 0.2 collective-permute-done.7.refs_2_
  24.0 0.8 %collective-permute-done.6.refs_1_ = bf16[2,32,512]{2,1,0:T(8,128)(2,1)S(1)} collective-permute-done((bf16[2,32,512]{2,1,0:T(8,128)(2,1)S(1)}, bf16[2,32,512]{2,1,0:T(8,128)(2,1)S(1)}, u32[]{:S(2)}, u32[]{:S(2)}) %collective-permute-start.6) | collective-permute-done | bytes 65568 | tf_op jit(solution)/shard_map/ppermute | solution.py:264
  24.8 0.0 collective-permute-done.5.refs_0_
  24.8 0.7 %expand.1 = bf16[2,32,1536]{2,1,0:T(8,128)(2,1)S(1)} custom-call(s32[1]{0:T(128)} %bitcast.active, bf16[2,256,1536]{2,1,0:T(8,128)(2,1)S(1)} %get-tuple-element.30.own_ref, bf16[2,256,1536]{2,1,0:T(8,128)(2,1)S(1)} %get-tuple-element.31.sister_ref, bf16[2,32,512]{2,1,0:T(8,128)(2,1)S(1)} %collective-permute-done.5.refs_0_, ...), custom_call_target="tpu_custom_call" | custom-call | flops 201326592 | bytes 3145728 | tf_op jit(solution)/shard_map/expand/pallas_call | solution.py:172
  25.5 0.1 collective-permute-start.9
  25.6 3.2 %collective-permute-done.9 = bf16[2,32,1536]{2,1,0:T(8,128)(2,1)S(1)} collective-permute-done((bf16[2,32,1536]{2,1,0:T(8,128)(2,1)S(1)}, bf16[2,32,1536]{2,1,0:T(8,128)(2,1)S(1)}, u32[]{:S(2)}, u32[]{:S(2)}) %collective-permute-start.9) | collective-permute-done | bytes 196640 | tf_op jit(solution)/shard_map/ppermute | solution.py:264
  28.8 1.4 %collective-permute-start.10 = (bf16[2,32,1536]{2,1,0:T(8,128)(2,1)S(1)}, bf16[2,32,1536]{2,1,0:T(8,128)(2,1)S(1)}, u32[]{:S(2)}, u32[]{:S(2)}) collective-permute-start(bf16[2,32,1536]{2,1,0:T(8,128)(2,1)S(1)} %broadcast_select_fusion.here_ref), channel_id=1, source_target_pairs={{0,1},{1,0},{2,3},{3,2},{4,5},{5,4},{6,7},{7,6},{8,9},{9,8},{10,11... | collective-permute-start | bytes 589832 | tf_op jit(solution)/shard_map/ppermute | solution.py:257
  30.1 1.1 %collective-permute-done.10.there_ref = bf16[2,32,1536]{2,1,0:T(8,128)(2,1)S(1)} collective-permute-done((bf16[2,32,1536]{2,1,0:T(8,128)(2,1)S(1)}, bf16[2,32,1536]{2,1,0:T(8,128)(2,1)S(1)}, u32[]{:S(2)}, u32[]{:S(2)}) %collective-permute-start.10) | collective-permute-done | bytes 196640 | tf_op jit(solution)/shard_map/ppermute | solution.py:257
  31.2 2.5 %prolong.1 = f32[2,24,32,768]{3,2,1,0:T(8,128)} custom-call(bf16[2,32,1536]{2,1,0:T(8,128)(2,1)S(1)} %broadcast_select_fusion.here_ref, bf16[2,32,1536]{2,1,0:T(8,128)(2,1)S(1)} %collective-permute-done.10.there_ref, f32[2,16,64,768]{3,2,1,0:T(8,128)S(1)} %load.2.refs_0_, f32[2,8,64,768]{3,2,1,0:T(8,128)S(1)} %load.3.refs_1_), custom_call_target="tpu_custom_call" | custom-call | flops 1207959552 | bytes 4718592 | tf_op jit(solution)/shard_map/prolong/pallas_call | solution.py:240
  (3 shorter events, 0.1 us)
Async XLA Ops:
  0.0 13.9 %collective-permute-start = (bf16[2,1536,256]{2,1,0:T(8,128)(2,1)}, bf16[2,1536,256]{2,1,0:T(8,128)(2,1)S(1)}, u32[]{:S(2)}, u32[]{:S(2)}) collective-permute-start(bf16[2,1536,256]{2,1,0:T(8,128)(2,1)} %bitcast.4), channel_id=1, source_target_pairs={{0,1},{1,0},{2,3},{3,2},{4,5},{5,4},{6,7},{7,6},{8,9},{9,8},{10,11... | collective-permute-start | bytes 4718600 | tf_op jit(solution)/shard_map/ppermute | solution.py:257
  6.3 1.5 %collective-permute-start.1 = (bf16[2,32,1536]{2,1,0:T(8,128)(2,1)S(1)}, bf16[2,32,1536]{2,1,0:T(8,128)(2,1)S(1)}, u32[]{:S(2)}, u32[]{:S(2)}) collective-permute-start(bf16[2,32,1536]{2,1,0:T(8,128)(2,1)S(1)} %project.1.refs_0_), channel_id=1, source_target_pairs={{0,1},{1,0},{2,3},{3,2},{4,5},{5,4},{6,7},{7,6},{8,9},{9,8},{10,11... | collective-permute-start | bytes 589832 | tf_op jit(solution)/shard_map/ppermute | solution.py:257
  7.8 6.0 %collective-permute-start.2 = (bf16[2,32,1536]{2,1,0:T(8,128)(2,1)S(1)}, bf16[2,32,1536]{2,1,0:T(8,128)(2,1)S(1)}, u32[]{:S(2)}, u32[]{:S(2)}) collective-permute-start(bf16[2,32,1536]{2,1,0:T(8,128)(2,1)S(1)} %add.7.refs_0_), channel_id=1, source_target_pairs={{0,1},{1,2},{2,3},{3,0},{4,5},{5,6},{6,7},{7,4},{8,9},{9,10},{10,1... | collective-permute-start | bytes 589832 | tf_op jit(solution)/shard_map/ppermute | solution.py:264
  8.0 5.8 %copy-start = (bf16[2,24,64,256]{3,2,1,0:T(8,128)(2,1)S(1)}, bf16[2,24,64,256]{3,2,1,0:T(8,128)(2,1)}, u32[]{:S(2)}) copy-start(bf16[2,24,64,256]{3,2,1,0:T(8,128)(2,1)} %param.6) | copy-start | bytes 4718596
  8.0 5.8 %copy-start.1 = (f32[256]{0:T(256)S(1)}, f32[256]{0:T(256)}, u32[]{:S(2)}) copy-start(f32[256]{0:T(256)} %param.7) | copy-start | bytes 3076
  14.6 3.4 %collective-permute-start.4 = (bf16[2,32,512]{2,1,0:T(8,128)(2,1)S(1)}, bf16[2,32,512]{2,1,0:T(8,128)(2,1)S(1)}, u32[]{:S(2)}, u32[]{:S(2)}) collective-permute-start(bf16[2,32,512]{2,1,0:T(8,128)(2,1)S(1)} %contract.1), channel_id=1, source_target_pairs={{0,17},{1,0},{2,19},{3,2},{4,21},{5,4},{6,23},{7,6},{8,25},{9,8},{... | collective-permute-start | bytes 196616 | tf_op jit(solution)/shard_map/ppermute | solution.py:264
  16.1 1.9 %collective-permute-start.3 = (bf16[2,32,512]{2,1,0:T(8,128)(2,1)S(1)}, bf16[2,32,512]{2,1,0:T(8,128)(2,1)S(1)}, u32[]{:S(2)}, u32[]{:S(2)}) collective-permute-start(bf16[2,32,512]{2,1,0:T(8,128)(2,1)S(1)} %contract.1), channel_id=1, source_target_pairs={{0,1},{1,0},{2,3},{3,2},{4,5},{5,4},{6,7},{7,6},{8,9},{9,8},{10,11... | collective-permute-start | bytes 196616 | tf_op jit(solution)/shard_map/ppermute | solution.py:257
  18.0 5.8 %collective-permute-start.8 = (bf16[2,32,512]{2,1,0:T(8,128)(2,1)S(1)}, bf16[2,32,512]{2,1,0:T(8,128)(2,1)S(1)}, u32[]{:S(2)}, u32[]{:S(2)}) collective-permute-start(bf16[2,32,512]{2,1,0:T(8,128)(2,1)S(1)} %add.8), channel_id=1, source_target_pairs={{0,1},{1,12},{2,3},{3,14},{4,5},{5,8},{6,7},{7,10},{8,9},{9,4},{10... | collective-permute-start | bytes 196616 | tf_op jit(solution)/shard_map/ppermute | solution.py:264
  19.6 4.4 %collective-permute-start.7 = (bf16[2,32,512]{2,1,0:T(8,128)(2,1)S(1)}, bf16[2,32,512]{2,1,0:T(8,128)(2,1)S(1)}, u32[]{:S(2)}, u32[]{:S(2)}) collective-permute-start(bf16[2,32,512]{2,1,0:T(8,128)(2,1)S(1)} %add.8), channel_id=1, source_target_pairs={{0,1},{1,4},{2,3},{3,6},{4,5},{5,0},{6,7},{7,2},{8,9},{9,12},{10,1... | collective-permute-start | bytes 196616 | tf_op jit(solution)/shard_map/ppermute | solution.py:264
  21.1 3.7 %collective-permute-start.6 = (bf16[2,32,512]{2,1,0:T(8,128)(2,1)S(1)}, bf16[2,32,512]{2,1,0:T(8,128)(2,1)S(1)}, u32[]{:S(2)}, u32[]{:S(2)}) collective-permute-start(bf16[2,32,512]{2,1,0:T(8,128)(2,1)S(1)} %add.8), channel_id=1, source_target_pairs={{0,1},{1,8},{2,3},{3,10},{4,5},{5,12},{6,7},{7,14},{8,9},{9,0},{10... | collective-permute-start | bytes 196616 | tf_op jit(solution)/shard_map/ppermute | solution.py:264
  21.2 3.6 %collective-permute-start.5 = (bf16[2,32,512]{2,1,0:T(8,128)(2,1)S(1)}, bf16[2,32,512]{2,1,0:T(8,128)(2,1)S(1)}, u32[]{:S(2)}, u32[]{:S(2)}) collective-permute-start(bf16[2,32,512]{2,1,0:T(8,128)(2,1)S(1)} %add.8), channel_id=1, source_target_pairs={{0,1},{1,0},{2,3},{3,2},{4,5},{5,4},{6,7},{7,6},{8,9},{9,8},{10,11... | collective-permute-start | bytes 196616 | tf_op jit(solution)/shard_map/ppermute | solution.py:257
  25.5 3.2 %collective-permute-start.9 = (bf16[2,32,1536]{2,1,0:T(8,128)(2,1)S(1)}, bf16[2,32,1536]{2,1,0:T(8,128)(2,1)S(1)}, u32[]{:S(2)}, u32[]{:S(2)}) collective-permute-start(bf16[2,32,1536]{2,1,0:T(8,128)(2,1)S(1)} %expand.1), channel_id=1, source_target_pairs={{0,3},{1,0},{2,1},{3,2},{4,7},{5,4},{6,5},{7,6},{8,11},{9,8},{10,9... | collective-permute-start | bytes 589832 | tf_op jit(solution)/shard_map/ppermute | solution.py:264
  28.8 2.4 %collective-permute-start.10 = (bf16[2,32,1536]{2,1,0:T(8,128)(2,1)S(1)}, bf16[2,32,1536]{2,1,0:T(8,128)(2,1)S(1)}, u32[]{:S(2)}, u32[]{:S(2)}) collective-permute-start(bf16[2,32,1536]{2,1,0:T(8,128)(2,1)S(1)} %broadcast_select_fusion.here_ref), channel_id=1, source_target_pairs={{0,1},{1,0},{2,3},{3,2},{4,5},{5,4},{6,7},{7,6},{8,9},{9,8},{10,11... | collective-permute-start | bytes 589832 | tf_op jit(solution)/shard_map/ppermute | solution.py:257

commit v8 on v7

--- a/solution.py
+++ b/solution.py
@@ -317,7 +317,7 @@
     chip_sum = add([part, place.swap(part)])
     sister = place.swap(own)
     holder = 0
-    head = 2 * (blocks // 3)
+    head = 2 * (blocks * 5 // 24)
     first = load(basis, 0, head, chip_sum)
     coarse = [chip_sum] + [place.cross(chip_sum, 1 - holder, chip=s) for s in place.chip_steps()]
     coarse, first = lax.optimization_barrier((coarse, first))

time: 33.9 us -> 33.9 us (level)
  starting transfers between devices: 7.04 us -> 7.54 us
  waiting for transfers between devices: 11.2 us -> 10.7 us
    ppermute x6, waiting for transfers between devices: 8.71 us -> 8.21 us  [cross(): return lax.ppermute(value, ('region', 'eig'), pairs)]
    ppermute x6, starting transfers between devices: 4.96 us -> 5.41 us  [cross(): return lax.ppermute(value, ('region', 'eig'), pairs)]
  transfers between devices with their start and end apart: 11 -> 11, of which waited for: 8 -> 6; matrix products, arithmetic and copies ran while one was open for 0% -> 0% of each run, Pallas kernels for 34% -> 34%
where the time goes in v8:
time: 33.9 us; the launch traced here: 33.7 us
  Pallas kernels  15.4 us (45%)
  waiting for transfers between devices  10.7 us (32%)
  starting transfers between devices  7.54 us (22%)
    ppermute x6, waiting for transfers between devices, cross(): return lax.ppermute(value, ('region', 'eig'), pairs)  8.21 us
    pallas_call x1, Pallas kernels, project(): pl.pallas_call(project_kernel, in_specs=[pl.BlockSpec(memory_space=pltpu....  5.81 us
    ppermute x6, starting transfers between devices, cross(): return lax.ppermute(value, ('region', 'eig'), pairs)  5.41 us
    pallas_call x2, Pallas kernels, load(): pl.pallas_call(functools.partial(load_kernel, start), in_specs=[pl.BlockS...  4.81 us
    pallas_call x1, Pallas kernels, prolong(): pl.pallas_call(prolong_kernel, in_specs=[whole()] * (2 + len(basis)), out...  2.52 us
    ppermute x5, waiting for transfers between devices, swap(): return lax.ppermute(value, 'eig', [(i, i ^ 1) for i in range(self.shares)])  2.46 us
    ppermute x5, starting transfers between devices, swap(): return lax.ppermute(value, 'eig', [(i, i ^ 1) for i in range(self.shares)])  2.13 us
    pallas_call x1, Pallas kernels, turn(): pl.pallas_call(turn_kernel, in_specs=[scalar()] + [whole()] * len(arrays)...  0.86 us
  transfers between devices with their start and end apart: 11, of which 6 were waited for; matrix products, arithmetic and copies ran while one was open for 0% of the time, Pallas kernels for 34%

profile of v8, /device:TPU:0, one launch (start us, length us, event | category | flops | bytes accessed | tf_op | source)
XLA Modules:
  0.0 33.7 jit_solution(7583161909474313673)
XLA Ops:
  0.0 0.5 %collective-permute-start = (bf16[2,1536,256]{2,1,0:T(8,128)(2,1)}, bf16[2,1536,256]{2,1,0:T(8,128)(2,1)S(1)}, u32[]{:S(2)}, u32[]{:S(2)}) collective-permute-start(bf16[2,1536,256]{2,1,0:T(8,128)(2,1)} %bitcast.4), channel_id=1, source_target_pairs={{0,1},{1,0},{2,3},{3,2},{4,5},{5,4},{6,7},{7,6},{8,9},{9,8},{10,11... | collective-permute-start | bytes 4718600 | tf_op jit(solution)/shard_map/ppermute | solution.py:257
  0.5 5.8 %project.1.refs_0_ = bf16[2,32,1536]{2,1,0:T(8,128)(2,1)S(1)} custom-call(f32[2,24,32,768]{3,2,1,0:T(8,128)} %res_hbm.1, f32[2,24,64,768]{3,2,1,0:T(8,128)} %from_hbm.1), custom_call_target="tpu_custom_call" | custom-call | flops 603979776 | bytes 14155776 | tf_op jit(solution)/shard_map/project/pallas_call | solution.py:73
  6.3 0.1 collective-permute-start.1
  6.4 1.4 %collective-permute-done.1.refs_1_ = bf16[2,32,1536]{2,1,0:T(8,128)(2,1)S(1)} collective-permute-done((bf16[2,32,1536]{2,1,0:T(8,128)(2,1)S(1)}, bf16[2,32,1536]{2,1,0:T(8,128)(2,1)S(1)}, u32[]{:S(2)}, u32[]{:S(2)}) %collective-permute-start.1) | collective-permute-done | bytes 196640 | tf_op jit(solution)/shard_map/ppermute | solution.py:257
  7.8 0.2 collective-permute-start.2
  8.0 0.0 copy-start
  8.0 0.0 copy-start.1
  8.0 2.2 %load.2.refs_0_ = f32[2,10,64,768]{3,2,1,0:T(8,128)S(1)} custom-call(f32[2,24,64,768]{3,2,1,0:T(8,128)} %from_hbm.1), custom_call_target="tpu_custom_call" | custom-call | bytes 3932160 | tf_op jit(solution)/shard_map/load/pallas_call | solution.py:191
  10.3 3.6 %collective-permute-done.2.refs_1_ = bf16[2,32,1536]{2,1,0:T(8,128)(2,1)S(1)} collective-permute-done((bf16[2,32,1536]{2,1,0:T(8,128)(2,1)S(1)}, bf16[2,32,1536]{2,1,0:T(8,128)(2,1)S(1)}, u32[]{:S(2)}, u32[]{:S(2)}) %collective-permute-start.2) | collective-permute-done | bytes 196640 | tf_op jit(solution)/shard_map/ppermute | solution.py:264
  13.9 0.0 collective-permute-done.sister_ref.refs_1_
  13.9 0.0 copy-done
  13.9 0.0 copy-done.1
  13.9 0.7 %contract.1 = bf16[2,32,512]{2,1,0:T(8,128)(2,1)S(1)} custom-call(s32[1]{0:T(128)} %bitcast.active, bf16[2,1536,256]{2,1,0:T(8,128)(2,1)S(1)} %bitcast.5, bf16[2,1536,256]{2,1,0:T(8,128)(2,1)S(1)} %collective-permute-done.sister_ref.refs_1_, f32[1,256]{1,0:T(1,128)S(1)} %bitcast.7, bf16[2,32,1536]{2,1,0:T(8,128)(2,1)S(1)} %add.7.refs_0_, ...), custom_call_target="tpu_custom_call" | custom-call | flops 201326592 | bytes 3145728 | tf_op jit(solution)/shard_map/contract/pallas_call | solution.py:113
  14.6 1.0 %collective-permute-start.4 = (bf16[2,32,512]{2,1,0:T(8,128)(2,1)S(1)}, bf16[2,32,512]{2,1,0:T(8,128)(2,1)S(1)}, u32[]{:S(2)}, u32[]{:S(2)}) collective-permute-start(bf16[2,32,512]{2,1,0:T(8,128)(2,1)S(1)} %contract.1), channel_id=1, source_target_pairs={{0,17},{1,0},{2,19},{3,2},{4,21},{5,4},{6,23},{7,6},{8,25},{9,8},{... | collective-permute-start | bytes 196616 | tf_op jit(solution)/shard_map/ppermute | solution.py:264
  15.5 0.0 collective-permute-start.3
  15.5 0.9 %turn.1 = (bf16[2,256,1536]{2,1,0:T(8,128)(2,1)S(1)}, bf16[2,256,1536]{2,1,0:T(8,128)(2,1)S(1)}) custom-call(s32[1]{0:T(128)} %bitcast.active, bf16[2,1536,256]{2,1,0:T(8,128)(2,1)S(1)} %bitcast.6, bf16[2,1536,256]{2,1,0:T(8,128)(2,1)S(1)} %collective-permute-done.sister_ref.refs_1_), custom_call_target="tpu_custom_call" | custom-call | bytes 6291456 | tf_op jit(solution)/shard_map/turn/pallas_call | solution.py:139
  16.4 1.0 %collective-permute-done.4.refs_1_ = bf16[2,32,512]{2,1,0:T(8,128)(2,1)S(1)} collective-permute-done((bf16[2,32,512]{2,1,0:T(8,128)(2,1)S(1)}, bf16[2,32,512]{2,1,0:T(8,128)(2,1)S(1)}, u32[]{:S(2)}, u32[]{:S(2)}) %collective-permute-start.4) | collective-permute-done | bytes 65568 | tf_op jit(solution)/shard_map/ppermute | solution.py:264
  17.4 0.0 collective-permute-done.3.refs_0_
  17.5 2.1 %collective-permute-start.8 = (bf16[2,32,512]{2,1,0:T(8,128)(2,1)S(1)}, bf16[2,32,512]{2,1,0:T(8,128)(2,1)S(1)}, u32[]{:S(2)}, u32[]{:S(2)}) collective-permute-start(bf16[2,32,512]{2,1,0:T(8,128)(2,1)S(1)} %add.8), channel_id=1, source_target_pairs={{0,1},{1,12},{2,3},{3,14},{4,5},{5,8},{6,7},{7,10},{8,9},{9,4},{10... | collective-permute-start | bytes 196616 | tf_op jit(solution)/shard_map/ppermute | solution.py:264
  19.6 1.0 %collective-permute-start.7 = (bf16[2,32,512]{2,1,0:T(8,128)(2,1)S(1)}, bf16[2,32,512]{2,1,0:T(8,128)(2,1)S(1)}, u32[]{:S(2)}, u32[]{:S(2)}) collective-permute-start(bf16[2,32,512]{2,1,0:T(8,128)(2,1)S(1)} %add.8), channel_id=1, source_target_pairs={{0,1},{1,4},{2,3},{3,6},{4,5},{5,0},{6,7},{7,2},{8,9},{9,12},{10,1... | collective-permute-start | bytes 196616 | tf_op jit(solution)/shard_map/ppermute | solution.py:264
  20.6 0.6 %collective-permute-start.6 = (bf16[2,32,512]{2,1,0:T(8,128)(2,1)S(1)}, bf16[2,32,512]{2,1,0:T(8,128)(2,1)S(1)}, u32[]{:S(2)}, u32[]{:S(2)}) collective-permute-start(bf16[2,32,512]{2,1,0:T(8,128)(2,1)S(1)} %add.8), channel_id=1, source_target_pairs={{0,1},{1,8},{2,3},{3,10},{4,5},{5,12},{6,7},{7,14},{8,9},{9,0},{10... | collective-permute-start | bytes 196616 | tf_op jit(solution)/shard_map/ppermute | solution.py:264
  21.2 0.2 collective-permute-start.5
  21.3 2.6 %load.3.refs_1_ = f32[2,14,64,768]{3,2,1,0:T(8,128)S(1)} custom-call(f32[2,24,64,768]{3,2,1,0:T(8,128)} %from_hbm.1), custom_call_target="tpu_custom_call" | custom-call | bytes 5505024 | tf_op jit(solution)/shard_map/load/pallas_call | solution.py:191
  23.9 0.0 collective-permute-done.8.refs_3_
  23.9 0.0 collective-permute-done.7.refs_2_
  24.0 0.3 %collective-permute-done.6.refs_1_ = bf16[2,32,512]{2,1,0:T(8,128)(2,1)S(1)} collective-permute-done((bf16[2,32,512]{2,1,0:T(8,128)(2,1)S(1)}, bf16[2,32,512]{2,1,0:T(8,128)(2,1)S(1)}, u32[]{:S(2)}, u32[]{:S(2)}) %collective-permute-start.6) | collective-permute-done | bytes 65568 | tf_op jit(solution)/shard_map/ppermute | solution.py:264
  24.3 0.0 collective-permute-done.5.refs_0_
  24.3 0.7 %expand.1 = bf16[2,32,1536]{2,1,0:T(8,128)(2,1)S(1)} custom-call(s32[1]{0:T(128)} %bitcast.active, bf16[2,256,1536]{2,1,0:T(8,128)(2,1)S(1)} %get-tuple-element.30.own_ref, bf16[2,256,1536]{2,1,0:T(8,128)(2,1)S(1)} %get-tuple-element.31.sister_ref, bf16[2,32,512]{2,1,0:T(8,128)(2,1)S(1)} %collective-permute-done.5.refs_0_, ...), custom_call_target="tpu_custom_call" | custom-call | flops 201326592 | bytes 3145728 | tf_op jit(solution)/shard_map/expand/pallas_call | solution.py:172
  25.0 0.5 %collective-permute-start.9 = (bf16[2,32,1536]{2,1,0:T(8,128)(2,1)S(1)}, bf16[2,32,1536]{2,1,0:T(8,128)(2,1)S(1)}, u32[]{:S(2)}, u32[]{:S(2)}) collective-permute-start(bf16[2,32,1536]{2,1,0:T(8,128)(2,1)S(1)} %expand.1), channel_id=1, source_target_pairs={{0,3},{1,0},{2,1},{3,2},{4,7},{5,4},{6,5},{7,6},{8,11},{9,8},{10,9... | collective-permute-start | bytes 589832 | tf_op jit(solution)/shard_map/ppermute | solution.py:264
  25.5 3.2 %collective-permute-done.9 = bf16[2,32,1536]{2,1,0:T(8,128)(2,1)S(1)} collective-permute-done((bf16[2,32,1536]{2,1,0:T(8,128)(2,1)S(1)}, bf16[2,32,1536]{2,1,0:T(8,128)(2,1)S(1)}, u32[]{:S(2)}, u32[]{:S(2)}) %collective-permute-start.9) | collective-permute-done | bytes 196640 | tf_op jit(solution)/shard_map/ppermute | solution.py:264
  28.7 1.4 %collective-permute-start.10 = (bf16[2,32,1536]{2,1,0:T(8,128)(2,1)S(1)}, bf16[2,32,1536]{2,1,0:T(8,128)(2,1)S(1)}, u32[]{:S(2)}, u32[]{:S(2)}) collective-permute-start(bf16[2,32,1536]{2,1,0:T(8,128)(2,1)S(1)} %broadcast_select_fusion.here_ref), channel_id=1, source_target_pairs={{0,1},{1,0},{2,3},{3,2},{4,5},{5,4},{6,7},{7,6},{8,9},{9,8},{10,11... | collective-permute-start | bytes 589832 | tf_op jit(solution)/shard_map/ppermute | solution.py:257
  30.1 1.1 %collective-permute-done.10.there_ref = bf16[2,32,1536]{2,1,0:T(8,128)(2,1)S(1)} collective-permute-done((bf16[2,32,1536]{2,1,0:T(8,128)(2,1)S(1)}, bf16[2,32,1536]{2,1,0:T(8,128)(2,1)S(1)}, u32[]{:S(2)}, u32[]{:S(2)}) %collective-permute-start.10) | collective-permute-done | bytes 196640 | tf_op jit(solution)/shard_map/ppermute | solution.py:257
  31.2 2.5 %prolong.1 = f32[2,24,32,768]{3,2,1,0:T(8,128)} custom-call(bf16[2,32,1536]{2,1,0:T(8,128)(2,1)S(1)} %broadcast_select_fusion.here_ref, bf16[2,32,1536]{2,1,0:T(8,128)(2,1)S(1)} %collective-permute-done.10.there_ref, f32[2,10,64,768]{3,2,1,0:T(8,128)S(1)} %load.2.refs_0_, f32[2,14,64,768]{3,2,1,0:T(8,128)S(1)} %load.3.refs_1_), custom_call_target="tpu_custom_call" | custom-call | flops 1207959552 | bytes 4718592 | tf_op jit(solution)/shard_map/prolong/pallas_call | solution.py:240
  (3 shorter events, 0.1 us)
Async XLA Ops:
  0.0 13.9 %collective-permute-start = (bf16[2,1536,256]{2,1,0:T(8,128)(2,1)}, bf16[2,1536,256]{2,1,0:T(8,128)(2,1)S(1)}, u32[]{:S(2)}, u32[]{:S(2)}) collective-permute-start(bf16[2,1536,256]{2,1,0:T(8,128)(2,1)} %bitcast.4), channel_id=1, source_target_pairs={{0,1},{1,0},{2,3},{3,2},{4,5},{5,4},{6,7},{7,6},{8,9},{9,8},{10,11... | collective-permute-start | bytes 4718600 | tf_op jit(solution)/shard_map/ppermute | solution.py:257
  6.3 1.5 %collective-permute-start.1 = (bf16[2,32,1536]{2,1,0:T(8,128)(2,1)S(1)}, bf16[2,32,1536]{2,1,0:T(8,128)(2,1)S(1)}, u32[]{:S(2)}, u32[]{:S(2)}) collective-permute-start(bf16[2,32,1536]{2,1,0:T(8,128)(2,1)S(1)} %project.1.refs_0_), channel_id=1, source_target_pairs={{0,1},{1,0},{2,3},{3,2},{4,5},{5,4},{6,7},{7,6},{8,9},{9,8},{10,11... | collective-permute-start | bytes 589832 | tf_op jit(solution)/shard_map/ppermute | solution.py:257
  7.8 6.0 %collective-permute-start.2 = (bf16[2,32,1536]{2,1,0:T(8,128)(2,1)S(1)}, bf16[2,32,1536]{2,1,0:T(8,128)(2,1)S(1)}, u32[]{:S(2)}, u32[]{:S(2)}) collective-permute-start(bf16[2,32,1536]{2,1,0:T(8,128)(2,1)S(1)} %add.7.refs_0_), channel_id=1, source_target_pairs={{0,1},{1,2},{2,3},{3,0},{4,5},{5,6},{6,7},{7,4},{8,9},{9,10},{10,1... | collective-permute-start | bytes 589832 | tf_op jit(solution)/shard_map/ppermute | solution.py:264
  8.0 5.8 %copy-start = (bf16[2,24,64,256]{3,2,1,0:T(8,128)(2,1)S(1)}, bf16[2,24,64,256]{3,2,1,0:T(8,128)(2,1)}, u32[]{:S(2)}) copy-start(bf16[2,24,64,256]{3,2,1,0:T(8,128)(2,1)} %param.6) | copy-start | bytes 4718596
  8.0 5.8 %copy-start.1 = (f32[256]{0:T(256)S(1)}, f32[256]{0:T(256)}, u32[]{:S(2)}) copy-start(f32[256]{0:T(256)} %param.7) | copy-start | bytes 3076
  14.6 2.9 %collective-permute-start.4 = (bf16[2,32,512]{2,1,0:T(8,128)(2,1)S(1)}, bf16[2,32,512]{2,1,0:T(8,128)(2,1)S(1)}, u32[]{:S(2)}, u32[]{:S(2)}) collective-permute-start(bf16[2,32,512]{2,1,0:T(8,128)(2,1)S(1)} %contract.1), channel_id=1, source_target_pairs={{0,17},{1,0},{2,19},{3,2},{4,21},{5,4},{6,23},{7,6},{8,25},{9,8},{... | collective-permute-start | bytes 196616 | tf_op jit(solution)/shard_map/ppermute | solution.py:264
  15.5 1.9 %collective-permute-start.3 = (bf16[2,32,512]{2,1,0:T(8,128)(2,1)S(1)}, bf16[2,32,512]{2,1,0:T(8,128)(2,1)S(1)}, u32[]{:S(2)}, u32[]{:S(2)}) collective-permute-start(bf16[2,32,512]{2,1,0:T(8,128)(2,1)S(1)} %contract.1), channel_id=1, source_target_pairs={{0,1},{1,0},{2,3},{3,2},{4,5},{5,4},{6,7},{7,6},{8,9},{9,8},{10,11... | collective-permute-start | bytes 196616 | tf_op jit(solution)/shard_map/ppermute | solution.py:257
  17.5 6.5 %collective-permute-start.8 = (bf16[2,32,512]{2,1,0:T(8,128)(2,1)S(1)}, bf16[2,32,512]{2,1,0:T(8,128)(2,1)S(1)}, u32[]{:S(2)}, u32[]{:S(2)}) collective-permute-start(bf16[2,32,512]{2,1,0:T(8,128)(2,1)S(1)} %add.8), channel_id=1, source_target_pairs={{0,1},{1,12},{2,3},{3,14},{4,5},{5,8},{6,7},{7,10},{8,9},{9,4},{10... | collective-permute-start | bytes 196616 | tf_op jit(solution)/shard_map/ppermute | solution.py:264
  19.6 4.4 %collective-permute-start.7 = (bf16[2,32,512]{2,1,0:T(8,128)(2,1)S(1)}, bf16[2,32,512]{2,1,0:T(8,128)(2,1)S(1)}, u32[]{:S(2)}, u32[]{:S(2)}) collective-permute-start(bf16[2,32,512]{2,1,0:T(8,128)(2,1)S(1)} %add.8), channel_id=1, source_target_pairs={{0,1},{1,4},{2,3},{3,6},{4,5},{5,0},{6,7},{7,2},{8,9},{9,12},{10,1... | collective-permute-start | bytes 196616 | tf_op jit(solution)/shard_map/ppermute | solution.py:264
  20.6 3.7 %collective-permute-start.6 = (bf16[2,32,512]{2,1,0:T(8,128)(2,1)S(1)}, bf16[2,32,512]{2,1,0:T(8,128)(2,1)S(1)}, u32[]{:S(2)}, u32[]{:S(2)}) collective-permute-start(bf16[2,32,512]{2,1,0:T(8,128)(2,1)S(1)} %add.8), channel_id=1, source_target_pairs={{0,1},{1,8},{2,3},{3,10},{4,5},{5,12},{6,7},{7,14},{8,9},{9,0},{10... | collective-permute-start | bytes 196616 | tf_op jit(solution)/shard_map/ppermute | solution.py:264
  21.2 3.1 %collective-permute-start.5 = (bf16[2,32,512]{2,1,0:T(8,128)(2,1)S(1)}, bf16[2,32,512]{2,1,0:T(8,128)(2,1)S(1)}, u32[]{:S(2)}, u32[]{:S(2)}) collective-permute-start(bf16[2,32,512]{2,1,0:T(8,128)(2,1)S(1)} %add.8), channel_id=1, source_target_pairs={{0,1},{1,0},{2,3},{3,2},{4,5},{5,4},{6,7},{7,6},{8,9},{9,8},{10,11... | collective-permute-start | bytes 196616 | tf_op jit(solution)/shard_map/ppermute | solution.py:257
  25.0 3.7 %collective-permute-start.9 = (bf16[2,32,1536]{2,1,0:T(8,128)(2,1)S(1)}, bf16[2,32,1536]{2,1,0:T(8,128)(2,1)S(1)}, u32[]{:S(2)}, u32[]{:S(2)}) collective-permute-start(bf16[2,32,1536]{2,1,0:T(8,128)(2,1)S(1)} %expand.1), channel_id=1, source_target_pairs={{0,3},{1,0},{2,1},{3,2},{4,7},{5,4},{6,5},{7,6},{8,11},{9,8},{10,9... | collective-permute-start | bytes 589832 | tf_op jit(solution)/shard_map/ppermute | solution.py:264
  28.7 2.5 %collective-permute-start.10 = (bf16[2,32,1536]{2,1,0:T(8,128)(2,1)S(1)}, bf16[2,32,1536]{2,1,0:T(8,128)(2,1)S(1)}, u32[]{:S(2)}, u32[]{:S(2)}) collective-permute-start(bf16[2,32,1536]{2,1,0:T(8,128)(2,1)S(1)} %broadcast_select_fusion.here_ref), channel_id=1, source_target_pairs={{0,1},{1,0},{2,3},{3,2},{4,5},{5,4},{6,7},{7,6},{8,9},{9,8},{10,11... | collective-permute-start | bytes 589832 | tf_op jit(solution)/shard_map/ppermute | solution.py:257

commit v9 on v7

--- a/solution.py
+++ b/solution.py
@@ -320,27 +320,24 @@
     head = 2 * (blocks // 3)
     first = load(basis, 0, head, chip_sum)
     coarse = [chip_sum] + [place.cross(chip_sum, 1 - holder, chip=s) for s in place.chip_steps()]
-    coarse, first = lax.optimization_barrier((coarse, first))
+    steps = list(place.region_steps())[::-1]
+    last = (core == (holder + len(steps)) % 2).astype(jnp.int32)
+    turned = turn(last, [own, sister], first)
+    coarse, first, turned = lax.optimization_barrier((coarse, first, turned))
 
     start = holder
     active = (core == holder).astype(jnp.int32)
     value = contract(active, coarse, own, sister, weights.reshape(1, count))
-    steps = list(place.region_steps())[::-1]
     for i, step in enumerate(steps):
         terms = [place.swap(value)] + [place.cross(value, holder, region=s) for s in step]
         holder = 1 - holder
-        if i == 0:
-            last = (start + len(steps)) % 2
-            active = (core == last).astype(jnp.int32)
-            turned = turn(active, [own, sister], value)
-            terms, turned = lax.optimization_barrier((terms, turned))
         if i == 0 or i < len(steps) - 1:
             value = add(terms, weights if i == 0 else None)
             terms = [value]
 
     second = load(basis, head, blocks - head, value)
     terms, second = lax.optimization_barrier((terms, second))
-    lifted = expand(active, terms, *turned, holder == start)
+    lifted = expand(last, terms, *turned, holder == start)
     terms = [place.cross(lifted, holder, chip=s) for s in place.chip_steps()]
     here = jnp.where(core == holder, lifted, total(terms).astype(BF))
     return prolong(here, place.swap(here), (first, second), residual.shape)

time: 33.9 us -> 33.8 us (level)
    ppermute x5, starting transfers between devices: 2.08 us -> 1.56 us  [swap(): return lax.ppermute(value, 'eig', [(i, i ^ 1) for i in range(self.shares)])]
    ppermute x6, starting transfers between devices: 4.96 us -> 5.37 us  [cross(): return lax.ppermute(value, ('region', 'eig'), pairs)]
where the time goes in v9:
time: 33.8 us; the launch traced here: 33.7 us
  Pallas kernels  15.4 us (46%)
  waiting for transfers between devices  11 us (33%)
  starting transfers between devices  6.93 us (21%)
    ppermute x6, waiting for transfers between devices, cross(): return lax.ppermute(value, ('region', 'eig'), pairs)  8.53 us
    pallas_call x1, Pallas kernels, project(): pl.pallas_call(project_kernel, in_specs=[pl.BlockSpec(memory_space=pltpu....  5.81 us
    ppermute x6, starting transfers between devices, cross(): return lax.ppermute(value, ('region', 'eig'), pairs)  5.37 us
    pallas_call x2, Pallas kernels, load(): pl.pallas_call(functools.partial(load_kernel, start), in_specs=[pl.BlockS...  4.81 us
    pallas_call x1, Pallas kernels, prolong(): pl.pallas_call(prolong_kernel, in_specs=[whole()] * (2 + len(basis)), out...  2.52 us
    ppermute x5, waiting for transfers between devices, swap(): return lax.ppermute(value, 'eig', [(i, i ^ 1) for i in range(self.shares)])  2.46 us
    ppermute x5, starting transfers between devices, swap(): return lax.ppermute(value, 'eig', [(i, i ^ 1) for i in range(self.shares)])  1.56 us
    pallas_call x1, Pallas kernels, turn(): pl.pallas_call(turn_kernel, in_specs=[scalar()] + [whole()] * len(arrays)...  0.86 us
  transfers between devices with their start and end apart: 11, of which 8 were waited for; matrix products, arithmetic and copies ran while one was open for 0% of the time, Pallas kernels for 34%

profile of v9, /device:TPU:0, one launch (start us, length us, event | category | flops | bytes accessed | tf_op | source)
XLA Modules:
  0.0 33.7 jit_solution(15278798192302177507)
XLA Ops:
  0.0 0.5 %collective-permute-start.2 = (bf16[2,1536,256]{2,1,0:T(8,128)(2,1)}, bf16[2,1536,256]{2,1,0:T(8,128)(2,1)S(1)}, u32[]{:S(2)}, u32[]{:S(2)}) collective-permute-start(bf16[2,1536,256]{2,1,0:T(8,128)(2,1)} %bitcast.4), channel_id=1, source_target_pairs={{0,1},{1,0},{2,3},{3,2},{4,5},{5,4},{6,7},{7,6},{8,9},{9,8},{10,11... | collective-permute-start | bytes 4718600 | tf_op jit(solution)/shard_map/ppermute | solution.py:257
  0.5 5.8 %project.1.refs_0_ = bf16[2,32,1536]{2,1,0:T(8,128)(2,1)S(1)} custom-call(f32[2,24,32,768]{3,2,1,0:T(8,128)} %res_hbm.1, f32[2,24,64,768]{3,2,1,0:T(8,128)} %from_hbm.1), custom_call_target="tpu_custom_call" | custom-call | flops 603979776 | bytes 14155776 | tf_op jit(solution)/shard_map/project/pallas_call | solution.py:73
  6.3 0.1 collective-permute-start
  6.4 1.4 %collective-permute-done.refs_1_ = bf16[2,32,1536]{2,1,0:T(8,128)(2,1)S(1)} collective-permute-done((bf16[2,32,1536]{2,1,0:T(8,128)(2,1)S(1)}, bf16[2,32,1536]{2,1,0:T(8,128)(2,1)S(1)}, u32[]{:S(2)}, u32[]{:S(2)}) %collective-permute-start) | collective-permute-done | bytes 196640 | tf_op jit(solution)/shard_map/ppermute | solution.py:257
  7.8 0.2 collective-permute-start.1
  8.0 0.0 copy-start
  8.0 2.9 %load.2.refs_0_ = f32[2,16,64,768]{3,2,1,0:T(8,128)S(1)} custom-call(f32[2,24,64,768]{3,2,1,0:T(8,128)} %from_hbm.1), custom_call_target="tpu_custom_call" | custom-call | bytes 6291456 | tf_op jit(solution)/shard_map/load/pallas_call | solution.py:191
  10.9 0.0 copy-start.1
  11.0 0.0 collective-permute-done.2.refs_1_.sister_ref
  11.0 0.3 copy-done
  11.2 0.9 %turn.1 = (bf16[2,256,1536]{2,1,0:T(8,128)(2,1)S(1)}, bf16[2,256,1536]{2,1,0:T(8,128)(2,1)S(1)}) custom-call(s32[1]{0:T(128)} %bitcast.active, bf16[2,1536,256]{2,1,0:T(8,128)(2,1)S(1)} %bitcast.5, bf16[2,1536,256]{2,1,0:T(8,128)(2,1)S(1)} %collective-permute-done.2.refs_1_.sister_ref), custom_call_target="tpu_custom_call" | custom-call | bytes 6291456 | tf_op jit(solution)/shard_map/turn/pallas_call | solution.py:139
  12.1 1.8 %collective-permute-done.1.refs_1_ = bf16[2,32,1536]{2,1,0:T(8,128)(2,1)S(1)} collective-permute-done((bf16[2,32,1536]{2,1,0:T(8,128)(2,1)S(1)}, bf16[2,32,1536]{2,1,0:T(8,128)(2,1)S(1)}, u32[]{:S(2)}, u32[]{:S(2)}) %collective-permute-start.1) | collective-permute-done | bytes 196640 | tf_op jit(solution)/shard_map/ppermute | solution.py:264
  13.9 0.0 copy-done.1
  13.9 0.7 %contract.1 = bf16[2,32,512]{2,1,0:T(8,128)(2,1)S(1)} custom-call(s32[1]{0:T(128)} %bitcast.active, bf16[2,1536,256]{2,1,0:T(8,128)(2,1)S(1)} %bitcast.6, bf16[2,1536,256]{2,1,0:T(8,128)(2,1)S(1)} %collective-permute-done.2.refs_1_.sister_ref, f32[1,256]{1,0:T(1,128)S(1)} %bitcast.7, bf16[2,32,1536]{2,1,0:T(8,128)(2,1)S(1)} %add.7.refs_0_, ...), custom_call_target="tpu_custom_call" | custom-call | flops 201326592 | bytes 3145728 | tf_op jit(solution)/shard_map/contract/pallas_call | solution.py:113
  14.5 2.0 %collective-permute-start.4 = (bf16[2,32,512]{2,1,0:T(8,128)(2,1)S(1)}, bf16[2,32,512]{2,1,0:T(8,128)(2,1)S(1)}, u32[]{:S(2)}, u32[]{:S(2)}) collective-permute-start(bf16[2,32,512]{2,1,0:T(8,128)(2,1)S(1)} %contract.1), channel_id=1, source_target_pairs={{0,17},{1,0},{2,19},{3,2},{4,21},{5,4},{6,23},{7,6},{8,25},{9,8},{... | collective-permute-start | bytes 196616 | tf_op jit(solution)/shard_map/ppermute | solution.py:264
  16.5 0.0 collective-permute-start.3
  16.5 1.9 %collective-permute-done.4.refs_1_ = bf16[2,32,512]{2,1,0:T(8,128)(2,1)S(1)} collective-permute-done((bf16[2,32,512]{2,1,0:T(8,128)(2,1)S(1)}, bf16[2,32,512]{2,1,0:T(8,128)(2,1)S(1)}, u32[]{:S(2)}, u32[]{:S(2)}) %collective-permute-start.4) | collective-permute-done | bytes 65568 | tf_op jit(solution)/shard_map/ppermute | solution.py:264
  18.4 0.0 collective-permute-done.3.refs_0_
  18.5 1.1 %collective-permute-start.8 = (bf16[2,32,512]{2,1,0:T(8,128)(2,1)S(1)}, bf16[2,32,512]{2,1,0:T(8,128)(2,1)S(1)}, u32[]{:S(2)}, u32[]{:S(2)}) collective-permute-start(bf16[2,32,512]{2,1,0:T(8,128)(2,1)S(1)} %add.8), channel_id=1, source_target_pairs={{0,1},{1,12},{2,3},{3,14},{4,5},{5,8},{6,7},{7,10},{8,9},{9,4},{10... | collective-permute-start | bytes 196616 | tf_op jit(solution)/shard_map/ppermute | solution.py:264
  19.6 2.0 %collective-permute-start.7 = (bf16[2,32,512]{2,1,0:T(8,128)(2,1)S(1)}, bf16[2,32,512]{2,1,0:T(8,128)(2,1)S(1)}, u32[]{:S(2)}, u32[]{:S(2)}) collective-permute-start(bf16[2,32,512]{2,1,0:T(8,128)(2,1)S(1)} %add.8), channel_id=1, source_target_pairs={{0,1},{1,4},{2,3},{3,6},{4,5},{5,0},{6,7},{7,2},{8,9},{9,12},{10,1... | collective-permute-start | bytes 196616 | tf_op jit(solution)/shard_map/ppermute | solution.py:264
  21.6 0.0 collective-permute-start.6
  21.6 0.1 collective-permute-start.5
  21.7 1.9 %load.3.refs_1_ = f32[2,8,64,768]{3,2,1,0:T(8,128)S(1)} custom-call(f32[2,24,64,768]{3,2,1,0:T(8,128)} %from_hbm.1), custom_call_target="tpu_custom_call" | custom-call | bytes 3145728 | tf_op jit(solution)/shard_map/load/pallas_call | solution.py:191
  23.6 0.1 collective-permute-done.8.refs_3_
  23.7 0.6 %collective-permute-done.7.refs_2_ = bf16[2,32,512]{2,1,0:T(8,128)(2,1)S(1)} collective-permute-done((bf16[2,32,512]{2,1,0:T(8,128)(2,1)S(1)}, bf16[2,32,512]{2,1,0:T(8,128)(2,1)S(1)}, u32[]{:S(2)}, u32[]{:S(2)}) %collective-permute-start.7) | collective-permute-done | bytes 65568 | tf_op jit(solution)/shard_map/ppermute | solution.py:264
  24.3 0.9 %collective-permute-done.6.refs_1_ = bf16[2,32,512]{2,1,0:T(8,128)(2,1)S(1)} collective-permute-done((bf16[2,32,512]{2,1,0:T(8,128)(2,1)S(1)}, bf16[2,32,512]{2,1,0:T(8,128)(2,1)S(1)}, u32[]{:S(2)}, u32[]{:S(2)}) %collective-permute-start.6) | collective-permute-done | bytes 65568 | tf_op jit(solution)/shard_map/ppermute | solution.py:264
  25.3 0.0 collective-permute-done.5.refs_0_
  25.3 0.7 %expand.1 = bf16[2,32,1536]{2,1,0:T(8,128)(2,1)S(1)} custom-call(s32[1]{0:T(128)} %bitcast.active, bf16[2,256,1536]{2,1,0:T(8,128)(2,1)S(1)} %get-tuple-element.26.own_ref, bf16[2,256,1536]{2,1,0:T(8,128)(2,1)S(1)} %get-tuple-element.27.sister_ref, bf16[2,32,512]{2,1,0:T(8,128)(2,1)S(1)} %collective-permute-done.5.refs_0_, ...), custom_call_target="tpu_custom_call" | custom-call | flops 201326592 | bytes 3145728 | tf_op jit(solution)/shard_map/expand/pallas_call | solution.py:172
  26.0 0.1 collective-permute-start.9
  26.0 3.2 %collective-permute-done.9 = bf16[2,32,1536]{2,1,0:T(8,128)(2,1)S(1)} collective-permute-done((bf16[2,32,1536]{2,1,0:T(8,128)(2,1)S(1)}, bf16[2,32,1536]{2,1,0:T(8,128)(2,1)S(1)}, u32[]{:S(2)}, u32[]{:S(2)}) %collective-permute-start.9) | collective-permute-done | bytes 196640 | tf_op jit(solution)/shard_map/ppermute | solution.py:264
  29.2 0.9 %collective-permute-start.10 = (bf16[2,32,1536]{2,1,0:T(8,128)(2,1)S(1)}, bf16[2,32,1536]{2,1,0:T(8,128)(2,1)S(1)}, u32[]{:S(2)}, u32[]{:S(2)}) collective-permute-start(bf16[2,32,1536]{2,1,0:T(8,128)(2,1)S(1)} %broadcast_select_fusion.here_ref), channel_id=1, source_target_pairs={{0,1},{1,0},{2,3},{3,2},{4,5},{5,4},{6,7},{7,6},{8,9},{9,8},{10,11... | collective-permute-start | bytes 589832 | tf_op jit(solution)/shard_map/ppermute | solution.py:257
  30.1 1.1 %collective-permute-done.10.there_ref = bf16[2,32,1536]{2,1,0:T(8,128)(2,1)S(1)} collective-permute-done((bf16[2,32,1536]{2,1,0:T(8,128)(2,1)S(1)}, bf16[2,32,1536]{2,1,0:T(8,128)(2,1)S(1)}, u32[]{:S(2)}, u32[]{:S(2)}) %collective-permute-start.10) | collective-permute-done | bytes 196640 | tf_op jit(solution)/shard_map/ppermute | solution.py:257
  31.2 2.5 %prolong.1 = f32[2,24,32,768]{3,2,1,0:T(8,128)} custom-call(bf16[2,32,1536]{2,1,0:T(8,128)(2,1)S(1)} %broadcast_select_fusion.here_ref, bf16[2,32,1536]{2,1,0:T(8,128)(2,1)S(1)} %collective-permute-done.10.there_ref, f32[2,16,64,768]{3,2,1,0:T(8,128)S(1)} %load.2.refs_0_, f32[2,8,64,768]{3,2,1,0:T(8,128)S(1)} %load.3.refs_1_), custom_call_target="tpu_custom_call" | custom-call | flops 1207959552 | bytes 4718592 | tf_op jit(solution)/shard_map/prolong/pallas_call | solution.py:240
  (3 shorter events, 0.1 us)
Async XLA Ops:
  0.0 11.0 %collective-permute-start.2 = (bf16[2,1536,256]{2,1,0:T(8,128)(2,1)}, bf16[2,1536,256]{2,1,0:T(8,128)(2,1)S(1)}, u32[]{:S(2)}, u32[]{:S(2)}) collective-permute-start(bf16[2,1536,256]{2,1,0:T(8,128)(2,1)} %bitcast.4), channel_id=1, source_target_pairs={{0,1},{1,0},{2,3},{3,2},{4,5},{5,4},{6,7},{7,6},{8,9},{9,8},{10,11... | collective-permute-start | bytes 4718600 | tf_op jit(solution)/shard_map/ppermute | solution.py:257
  6.3 1.5 %collective-permute-start = (bf16[2,32,1536]{2,1,0:T(8,128)(2,1)S(1)}, bf16[2,32,1536]{2,1,0:T(8,128)(2,1)S(1)}, u32[]{:S(2)}, u32[]{:S(2)}) collective-permute-start(bf16[2,32,1536]{2,1,0:T(8,128)(2,1)S(1)} %project.1.refs_0_), channel_id=1, source_target_pairs={{0,1},{1,0},{2,3},{3,2},{4,5},{5,4},{6,7},{7,6},{8,9},{9,8},{10,11... | collective-permute-start | bytes 589832 | tf_op jit(solution)/shard_map/ppermute | solution.py:257
  7.8 6.0 %collective-permute-start.1 = (bf16[2,32,1536]{2,1,0:T(8,128)(2,1)S(1)}, bf16[2,32,1536]{2,1,0:T(8,128)(2,1)S(1)}, u32[]{:S(2)}, u32[]{:S(2)}) collective-permute-start(bf16[2,32,1536]{2,1,0:T(8,128)(2,1)S(1)} %add.7.refs_0_), channel_id=1, source_target_pairs={{0,1},{1,2},{2,3},{3,0},{4,5},{5,6},{6,7},{7,4},{8,9},{9,10},{10,1... | collective-permute-start | bytes 589832 | tf_op jit(solution)/shard_map/ppermute | solution.py:264
  8.0 3.2 %copy-start = (bf16[2,24,64,256]{3,2,1,0:T(8,128)(2,1)S(1)}, bf16[2,24,64,256]{3,2,1,0:T(8,128)(2,1)}, u32[]{:S(2)}) copy-start(bf16[2,24,64,256]{3,2,1,0:T(8,128)(2,1)} %param.6) | copy-start | bytes 4718596
  10.9 2.9 %copy-start.1 = (f32[256]{0:T(256)S(1)}, f32[256]{0:T(256)}, u32[]{:S(2)}) copy-start(f32[256]{0:T(256)} %param.7) | copy-start | bytes 3076
  14.5 3.9 %collective-permute-start.4 = (bf16[2,32,512]{2,1,0:T(8,128)(2,1)S(1)}, bf16[2,32,512]{2,1,0:T(8,128)(2,1)S(1)}, u32[]{:S(2)}, u32[]{:S(2)}) collective-permute-start(bf16[2,32,512]{2,1,0:T(8,128)(2,1)S(1)} %contract.1), channel_id=1, source_target_pairs={{0,17},{1,0},{2,19},{3,2},{4,21},{5,4},{6,23},{7,6},{8,25},{9,8},{... | collective-permute-start | bytes 196616 | tf_op jit(solution)/shard_map/ppermute | solution.py:264
  16.5 1.9 %collective-permute-start.3 = (bf16[2,32,512]{2,1,0:T(8,128)(2,1)S(1)}, bf16[2,32,512]{2,1,0:T(8,128)(2,1)S(1)}, u32[]{:S(2)}, u32[]{:S(2)}) collective-permute-start(bf16[2,32,512]{2,1,0:T(8,128)(2,1)S(1)} %contract.1), channel_id=1, source_target_pairs={{0,1},{1,0},{2,3},{3,2},{4,5},{5,4},{6,7},{7,6},{8,9},{9,8},{10,11... | collective-permute-start | bytes 196616 | tf_op jit(solution)/shard_map/ppermute | solution.py:257
  18.5 5.3 %collective-permute-start.8 = (bf16[2,32,512]{2,1,0:T(8,128)(2,1)S(1)}, bf16[2,32,512]{2,1,0:T(8,128)(2,1)S(1)}, u32[]{:S(2)}, u32[]{:S(2)}) collective-permute-start(bf16[2,32,512]{2,1,0:T(8,128)(2,1)S(1)} %add.8), channel_id=1, source_target_pairs={{0,1},{1,12},{2,3},{3,14},{4,5},{5,8},{6,7},{7,10},{8,9},{9,4},{10... | collective-permute-start | bytes 196616 | tf_op jit(solution)/shard_map/ppermute | solution.py:264
  19.6 4.8 %collective-permute-start.7 = (bf16[2,32,512]{2,1,0:T(8,128)(2,1)S(1)}, bf16[2,32,512]{2,1,0:T(8,128)(2,1)S(1)}, u32[]{:S(2)}, u32[]{:S(2)}) collective-permute-start(bf16[2,32,512]{2,1,0:T(8,128)(2,1)S(1)} %add.8), channel_id=1, source_target_pairs={{0,1},{1,4},{2,3},{3,6},{4,5},{5,0},{6,7},{7,2},{8,9},{9,12},{10,1... | collective-permute-start | bytes 196616 | tf_op jit(solution)/shard_map/ppermute | solution.py:264
  21.6 3.7 %collective-permute-start.6 = (bf16[2,32,512]{2,1,0:T(8,128)(2,1)S(1)}, bf16[2,32,512]{2,1,0:T(8,128)(2,1)S(1)}, u32[]{:S(2)}, u32[]{:S(2)}) collective-permute-start(bf16[2,32,512]{2,1,0:T(8,128)(2,1)S(1)} %add.8), channel_id=1, source_target_pairs={{0,1},{1,8},{2,3},{3,10},{4,5},{5,12},{6,7},{7,14},{8,9},{9,0},{10... | collective-permute-start | bytes 196616 | tf_op jit(solution)/shard_map/ppermute | solution.py:264
  21.6 3.7 %collective-permute-start.5 = (bf16[2,32,512]{2,1,0:T(8,128)(2,1)S(1)}, bf16[2,32,512]{2,1,0:T(8,128)(2,1)S(1)}, u32[]{:S(2)}, u32[]{:S(2)}) collective-permute-start(bf16[2,32,512]{2,1,0:T(8,128)(2,1)S(1)} %add.8), channel_id=1, source_target_pairs={{0,1},{1,0},{2,3},{3,2},{4,5},{5,4},{6,7},{7,6},{8,9},{9,8},{10,11... | collective-permute-start | bytes 196616 | tf_op jit(solution)/shard_map/ppermute | solution.py:257
  26.0 3.2 %collective-permute-start.9 = (bf16[2,32,1536]{2,1,0:T(8,128)(2,1)S(1)}, bf16[2,32,1536]{2,1,0:T(8,128)(2,1)S(1)}, u32[]{:S(2)}, u32[]{:S(2)}) collective-permute-start(bf16[2,32,1536]{2,1,0:T(8,128)(2,1)S(1)} %expand.1), channel_id=1, source_target_pairs={{0,3},{1,0},{2,1},{3,2},{4,7},{5,4},{6,5},{7,6},{8,11},{9,8},{10,9... | collective-permute-start | bytes 589832 | tf_op jit(solution)/shard_map/ppermute | solution.py:264
  29.2 2.0 %collective-permute-start.10 = (bf16[2,32,1536]{2,1,0:T(8,128)(2,1)S(1)}, bf16[2,32,1536]{2,1,0:T(8,128)(2,1)S(1)}, u32[]{:S(2)}, u32[]{:S(2)}) collective-permute-start(bf16[2,32,1536]{2,1,0:T(8,128)(2,1)S(1)} %broadcast_select_fusion.here_ref), channel_id=1, source_target_pairs={{0,1},{1,0},{2,3},{3,2},{4,5},{5,4},{6,7},{7,6},{8,9},{9,8},{10,11... | collective-permute-start | bytes 589832 | tf_op jit(solution)/shard_map/ppermute | solution.py:257
